TPU v7x, 512 devices: a whole 4x8x8 slice. The times are simulated.
512 devices in a mesh: gx: 64 (over x, y, core), gy: 4 (over z_hi), gz: 2 (over z_lo).
Axes of the slice: x: 4, y: 8, z: 8 (z_hi: 4, z_lo: 2; z = z_hi * 2 + z_lo), core: 2. Of those that a mesh axis runs over, the one named last changes fastest.
Arguments:
- right_side: float32 [2560, 160, 256], P('gx', 'gy', 'gz'), may hold values from -6 to 6
- guess_field: float32 [2560, 160, 256], P('gx', 'gy', 'gz'), may hold values from -0.6 to 0.6
- conduct_field: float32 [2560, 160, 256], P('gx', 'gy', 'gz'), may hold values from 1 to 10
Outputs:
- solution_field: float32 [2560, 160, 256], P('gx', 'gy', 'gz')
- residual: float32 [2560, 160, 256], P('gx', 'gy', 'gz')
All inputs are finite; a program needn't handle non-finite values.
Results may differ from a plain program's by a relative error of at most 0.0055.
Values sent between devices are 32-bit elements; how exact they have to be, the bound alone decides.
No kernel may reach another device: no remote copies, remote signals or barrier semaphores. Data moves between devices by JAX's collectives and lax.ppermute only.
A program may use at most 64 MiB of HBM per device.

v0:
```python
import functools

import jax
import jax.numpy as jnp
import ml_dtypes
import numpy as np
from jax import lax
from jax.experimental import pallas as pl
from jax.experimental.pallas import tpu as pltpu
from jax.sharding import Mesh
from jax.sharding import PartitionSpec as P

OVER = 8
C = 40
CZ = 128
EXT = C + 2 * OVER
EXTZ = CZ + 2 * OVER
TILES = EXT // 8
GROUPS = EXT * TILES
stiff_scale = 3.0
mass_term = 0.001

F32 = jnp.float32
BF16 = jnp.bfloat16
VMEM = pl.BlockSpec(memory_space=pltpu.VMEM)
SMEM = pl.BlockSpec(memory_space=pltpu.SMEM)

YROWS = 440
XROWS = 568
PER_Z = 12
ZROWS = 8 * -(-GROUPS // PER_Z)
PER = 14
XROWS2 = 9 * EXT + 40
YROWS2 = 416
ZGROUPS2 = 42 * 5 + 12
ZROWS2 = 8 * -(-ZGROUPS2 // PER)


def sine_table(count):
    k = np.arange(1, count + 1)
    basis = np.sqrt(2.0 / (count + 1)) * np.sin(np.pi * k[:, None] * k[None, :] / (count + 1))
    eigen = 2.0 - 2.0 * np.cos(np.pi * k / (count + 1))
    return basis, eigen


def two_parts(table):
    high = table.astype(ml_dtypes.bfloat16)
    low = (table - high.astype(np.float64)).astype(ml_dtypes.bfloat16)
    return high, low


@functools.cache
def tables():
    basis, eigen = sine_table(EXT)
    basis_z, eigen_z = sine_table(EXTZ)
    high, low = two_parts(basis)
    plane = np.zeros((EXT, 192), ml_dtypes.bfloat16)
    plane[:, 0:EXT] = high
    plane[:, 64 : 64 + EXT] = low
    plane[:, 128 : 128 + EXT] = high
    forward = np.zeros((2, 256, 256))
    inverse = np.zeros((2, 256, 256))
    for gz in range(2):
        own = basis_z[8 : 8 + CZ]
        strip = basis_z[136:144] if gz == 0 else basis_z[0:8]
        face_own, face_far = (135, 136) if gz == 0 else (8, 7)
        forward[gz, :CZ, :EXTZ] = own
        forward[gz, CZ, :EXTZ] = basis_z[face_own] - basis_z[face_far]
        forward[gz, CZ + 2 : CZ + 10, :EXTZ] = strip
        inverse[gz, :EXTZ, :CZ] = own.T
        inverse[gz, :EXTZ, CZ : CZ + 9] = (basis_z[135:144] if gz == 0 else basis_z[0:9]).T
    forward = np.stack(two_parts(forward), 1)
    inverse = np.stack(two_parts(inverse), 1)
    denom = np.full((EXT, 256), 1.0)
    denom[:, :EXTZ] = stiff_scale * (eigen[:, None] + eigen_z[None, :]) + mass_term
    return (
        plane,
        forward,
        inverse,
        denom.astype(np.float32),
        (stiff_scale * eigen).astype(np.float32),
    )


def roll(value, shift, axis):
    if isinstance(shift, int):
        shift = shift % value.shape[axis]
        return value if shift == 0 else pltpu.roll(value, shift, axis)
    return pltpu.roll(value, lax.rem(shift + 2 * value.shape[axis], value.shape[axis]), axis)


def lanes(rows):
    return lax.broadcasted_iota(jnp.int32, (rows, CZ), 1)


def rows_at(start, size):
    return pl.ds(pl.multiple_of(start, 8), size)


def tile_at(index):
    return rows_at(index * 8, 8)


def call(body, out_rows, *args, scratch=(), limit=16, name=None, smem=(), flops=0):
    return pl.pallas_call(
        body,
        out_shape=[jax.ShapeDtypeStruct((rows, CZ), F32) for rows in out_rows],
        in_specs=[SMEM if i in smem else VMEM for i in range(len(args))],
        out_specs=[VMEM] * len(out_rows),
        scratch_shapes=list(scratch),
        compiler_params=pltpu.CompilerParams(vmem_limit_bytes=limit * 2**20),
        name=name,
    )(*args)


def strip_base():
    return jnp.where(lax.axis_index("gz") == 0, 118, 126)


def face_lane():
    return jnp.where(lax.axis_index("gz") == 0, 127, 0)


def residual_kernel(v, h, b, part, vh, up, down, edge):
    gz = lax.axis_index("gz")
    base, face = strip_base(), face_lane()
    lane = lanes(C)
    row = lax.broadcasted_iota(jnp.int32, (C, CZ), 0)
    y_half = jnp.where(row > 0, 0.5, 0.0)
    z_half = jnp.where(lane < CZ - 1, 0.5, 0.0)
    outer = jnp.where(lane == jnp.where(gz == 0, 0, 127), 0.5, 0.0)
    v_lane, h_lane = lane == base, lane == base + 1

    def visit(x, carry):
        flux_x, pack_up, pack_down = carry
        own = rows_at(x * C, C)
        following = rows_at(jnp.minimum(x + 1, C - 1) * C, C)
        vi, hi = v[own, :], h[own, :]
        next_x = 0.5 * (hi + h[following, :]) * (v[following, :] - vi)
        flux_y = y_half * (hi + roll(hi, 1, 0)) * (vi - roll(vi, 1, 0))
        flux_z = z_half * (hi + roll(hi, -1, 1)) * (roll(vi, -1, 1) - vi)
        applied = (
            mass_term * vi
            - (next_x - flux_x)
            - (roll(flux_y, -1, 0) - flux_y)
            - (flux_z - roll(flux_z, 1, 1))
            + outer * hi * vi
        )
        resid = b[own, :] - applied
        part[own, :] = resid
        down[tile_at(x), :] = resid[0:8]
        up[tile_at(x), :] = resid[32:40]
        pair = jnp.where(v_lane, roll(vi, base - face, 1), 0.0) + jnp.where(
            h_lane, roll(hi, base + 1 - face, 1), 0.0
        )
        vh[own, :] = pair
        shift = 2 * x - base
        return (
            next_x,
            pack_up + roll(pair[32:40], shift, 1),
            pack_down + roll(pair[0:8], shift, 1),
        )

    zero = jnp.zeros((C, CZ), F32)
    zero8 = jnp.zeros((8, CZ), F32)
    _, pack_up, pack_down = lax.fori_loop(0, C, visit, (zero, zero8, zero8), unroll=4)
    up[432:440, :] = pack_up
    down[432:440, :] = pack_down
    last = (C - 1) * C
    for message, first in ((up, 32), (down, 0)):
        face_row = C - 1 if first else 0
        message[320:360, :] = v[pl.ds(face_row, C, stride=C), :]
        message[360:400, :] = h[pl.ds(face_row, C, stride=C), :]
        message[400:408, :] = v[first : first + 8, :]
        message[408:416, :] = h[first : first + 8, :]
        message[416:424, :] = v[last + first : last + first + 8, :]
        message[424:432, :] = h[last + first : last + first + 8, :]
    edge[0:40, :] = v[0:40, :]
    edge[40:80, :] = h[0:40, :]
    edge[80:120, :] = v[last : last + 40, :]
    edge[120:160, :] = h[last : last + 40, :]


def pack_pairs(vh, first):
    base = strip_base()

    def visit(i, acc):
        for t in range(TILES):
            j = i * TILES + t
            acc = acc + roll(vh[tile_at(first + j), :], 2 * j - base, 1)
        return acc

    return lax.fori_loop(0, OVER, visit, jnp.zeros((8, CZ), F32), unroll=2)


def extend_y_kernel(flags, part, vh, up, down, edge, low, high, out, vh_out, right, left):
    base = strip_base()
    lane = lanes(8)
    pair_lanes = (lane == base) | (lane == base + 1)

    def visit(x, _):
        out[rows_at(x * EXT, 8), :] = low[tile_at(x), :]
        out[rows_at(x * EXT + 8, C), :] = part[rows_at(x * C, C), :]
        out[rows_at(x * EXT + 48, 8), :] = high[tile_at(x), :]
        vh_out[rows_at(x * EXT, 8), :] = jnp.where(
            pair_lanes, roll(low[432:440, :], base - 2 * x, 1), 0.0
        )
        vh_out[rows_at(x * EXT + 8, C), :] = vh[rows_at(x * C, C), :]
        vh_out[rows_at(x * EXT + 48, 8), :] = jnp.where(
            pair_lanes, roll(high[432:440, :], base - 2 * x, 1), 0.0
        )
        return 0

    lax.fori_loop(0, C, visit, 0, unroll=4)
    flux = 0.5 * (low[360:400, :] + down[360:400, :]) * (down[320:360, :] - low[320:360, :])
    out[pl.ds(8, C, stride=EXT), :] = out[pl.ds(8, C, stride=EXT), :] - flux
    out[pl.ds(7, C, stride=EXT), :] = out[pl.ds(7, C, stride=EXT), :] + flux * flags[2]
    flux = 0.5 * (up[360:400, :] + high[360:400, :]) * (high[320:360, :] - up[320:360, :])
    out[pl.ds(47, C, stride=EXT), :] = out[pl.ds(47, C, stride=EXT), :] + flux
    out[pl.ds(48, C, stride=EXT), :] = out[pl.ds(48, C, stride=EXT), :] - flux * flags[3]
    for message, first, strip, own in ((left, 0, 400, 0), (right, 32, 416, 80)):
        message[0:448, :] = out[first * EXT : first * EXT + 448, :]
        for k in range(2):
            at = 448 + k * EXT
            message[at : at + 8, :] = low[strip + 8 * k : strip + 8 * k + 8, :]
            message[at + 8 : at + 48, :] = edge[own + 40 * k : own + 40 * k + 40, :]
            message[at + 48 : at + 56, :] = high[strip + 8 * k : strip + 8 * k + 8, :]
        message[560:568, :] = pack_pairs(vh_out, first * TILES)


def extend_x_kernel(flags, part, vh, right, left, before, after, out, message, vh_all):
    base = strip_base()
    gz = lax.axis_index("gz")
    lane = lanes(8)
    pair_lanes = (lane == base) | (lane == base + 1)
    strip_lanes = jnp.where(gz == 0, lane - 120, 7 - lane) >= 0
    side = OVER * EXT
    out[0:side, :] = before[0:side, :]
    out[side : side + C * EXT, :] = part[...]
    out[side + C * EXT : EXT * EXT, :] = after[0:side, :]
    vh_all[side : side + C * EXT, :] = vh[...]

    def visit(j, _):
        vh_all[tile_at(j), :] = jnp.where(
            pair_lanes, roll(before[560:568, :], base - 2 * j, 1), 0.0
        )
        vh_all[tile_at(j + (OVER + C) * TILES), :] = jnp.where(
            pair_lanes, roll(after[560:568, :], base - 2 * j, 1), 0.0
        )
        return 0

    lax.fori_loop(0, OVER * TILES, visit, 0, unroll=8)
    flux = 0.5 * (before[504:560, :] + left[504:560, :]) * (left[448:504, :] - before[448:504, :])
    at = OVER * EXT
    out[at : at + EXT, :] = out[at : at + EXT, :] - flux
    out[at - EXT : at, :] = out[at - EXT : at, :] + flux * flags[0]
    flux = 0.5 * (right[504:560, :] + after[504:560, :]) * (after[448:504, :] - right[448:504, :])
    at = (OVER + C) * EXT
    out[at - EXT : at, :] = out[at - EXT : at, :] + flux
    out[at : at + EXT, :] = out[at : at + EXT, :] - flux * flags[1]

    def pack(q, count):
        acc = jnp.zeros((8, CZ), F32)
        for j in range(count):
            at = tile_at(q * PER_Z + j)
            both = jnp.where(strip_lanes, out[at, :], vh_all[at, :])
            acc = acc + roll(both, 10 * j - base, 1)
        message[tile_at(q), :] = acc

    def visit_pack(q, _):
        pack(q, PER_Z)
        return 0

    whole = GROUPS // PER_Z
    lax.fori_loop(0, whole, visit_pack, 0, unroll=2)
    pack(whole, GROUPS - whole * PER_Z)


def halves(value):
    high = value.astype(BF16)
    return high, (value - high.astype(F32)).astype(BF16)


def dot(a, b):
    return jnp.dot(a, b, preferred_element_type=F32)


def along_lanes(value, table_high, table_low):
    high, low = halves(value)
    return dot(high, table_high) + (dot(low, table_high) + dot(high, table_low))


def along_rows(table, value):
    padded = jnp.concatenate([value, jnp.zeros((8, value.shape[1]), F32)], axis=0)
    high, low = halves(padded)
    return dot(table, jnp.concatenate([high, high, low], axis=0))


PLANES = 8


def solve_kernel(
    eigen,
    ext,
    own_z,
    far_z,
    plane,
    forward,
    inverse,
    denom,
    resid,
    coef,
    sol,
    strip,
    right,
    left,
    halo_pack,
    coef_pack,
    halo,
    first_a,
    first_b,
    second_a,
    second_b,
):
    gz = lax.axis_index("gz")
    face = face_lane()
    lane = lanes(ZROWS)
    at_face = lax.rem(lane, 10) == 0
    both = own_z[...] + far_z[...]
    half = 0.5 * roll(both, -1, 1)
    halo_pack[...] = jnp.where(at_face, half * (far_z[...] - own_z[...]), far_z[...])
    coef_pack[...] = half
    lane8 = lanes(8)
    face_only = lane8 == face

    def unpack(q, count):
        packed = halo_pack[tile_at(q), :]
        for j in range(count):
            halo[tile_at(q * PER_Z + j), :] = roll(packed, -10 * j, 1)

    def visit_unpack(q, _):
        unpack(q, PER_Z)
        return 0

    whole = GROUPS // PER_Z
    lax.fori_loop(0, whole, visit_unpack, 0, unroll=2)
    unpack(whole, GROUPS - whole * PER_Z)

    def visit_own(x, _):
        for t in range(5):
            g = (x + OVER) * TILES + 1 + t
            q = g // PER_Z
            to = rows_at(x * C + 8 * t, 8)
            flux = roll(halo[tile_at(g), :], face, 1)
            resid[to, :] = ext[tile_at(g), :] + jnp.where(face_only, flux, 0.0)
            shift = face - 10 * (g - q * PER_Z)
            coef[to, :] = jnp.where(face_only, roll(coef_pack[tile_at(q), :], shift, 1), 0.0)
        return 0

    lax.fori_loop(0, C, visit_own, 0, unroll=2)

    table = plane[...]
    forward_high, forward_low = forward[gz, 0], forward[gz, 1]
    inverse_high, inverse_low = inverse[gz, 0], inverse[gz, 1]

    def visit_forward(c, _):
        at = rows_at(c * PLANES * EXT, PLANES * EXT)
        value = jnp.concatenate([ext[at, :], halo[at, :]], axis=1)
        value = along_lanes(value, forward_high, forward_low)
        for i in range(PLANES):
            part = along_rows(table, value[i * EXT : (i + 1) * EXT])
            to = rows_at((c * PLANES + i) * EXT, EXT)
            first_a[to, :] = part[:, :CZ]
            first_b[to, :] = part[:, CZ:]
        return 0

    lax.fori_loop(0, EXT // PLANES, visit_forward, 0)

    def visit_middle(c, _):
        for i in range(4):
            y = c * 4 + i
            at = pl.ds(y, EXT, stride=EXT)
            value = jnp.concatenate([first_a[at, :], first_b[at, :]], axis=1)
            value = along_rows(table, value) / (denom[...] + eigen[y])
            value = along_rows(table, value)
            second_a[at, :] = value[:, :CZ]
            second_b[at, :] = value[:, CZ:]
        return 0

    lax.fori_loop(0, EXT // 4, visit_middle, 0)

    def visit_inverse(c, _):
        parts = []
        for i in range(PLANES):
            at = rows_at((c * PLANES + i) * EXT, EXT)
            value = jnp.concatenate([second_a[at, :], second_b[at, :]], axis=1)
            parts.append(along_rows(table, value))
        value = along_lanes(jnp.concatenate(parts, axis=0), inverse_high, inverse_low)
        to = rows_at(c * PLANES * EXT, PLANES * EXT)
        sol[to, :] = value[:, :CZ]
        strip[to, :] = value[:, CZ:]
        return 0

    lax.fori_loop(0, EXT // PLANES, visit_inverse, 0)

    for message, start in ((left, 0), (right, 47)):
        message[0 : 9 * EXT, :] = sol[start * EXT : (start + 9) * EXT, :]
        pack_tiles(message, 9 * EXT, [strip[pl.ds((start * TILES + j) * 8, 8), :] for j in range(63)])


def pack_tiles(message, at, values):
    for q in range(-(-len(values) // PER)):
        acc = values[q * PER]
        for j, value in enumerate(values[q * PER + 1 : (q + 1) * PER], 1):
            acc = acc + roll(value, 9 * j, 1)
        message[at + 8 * q : at + 8 * q + 8, :] = acc


def unpack_tile(message, at, index):
    q = index // PER
    return roll(message[rows_at(at + 8 * q, 8), :], -9 * (index - q * PER), 1)


def fold_x_kernel(flags, sol, strip, before, after, out, out_strip, up, down, line):
    first = 7 * EXT
    size = 42 * EXT
    narrow = lanes(8) < 9
    out[...] = sol[first : first + size, :]
    out_strip[...] = strip[first : first + size, :]
    out[0 : 9 * EXT, :] = out[0 : 9 * EXT, :] + before[0 : 9 * EXT, :]
    tail = 33 * EXT
    out[tail:size, :] = out[tail:size, :] + after[0 : 9 * EXT, :]

    for j in range(63):
        for message, at in ((before, 8 * j), (after, tail + 8 * j)):
            value = jnp.where(narrow, unpack_tile(message, 9 * EXT, j), 0.0)
            out_strip[at : at + 8, :] = out_strip[at : at + 8, :] + value

    for array in (out, out_strip):
        array[0:EXT, :] = array[0:EXT, :] * flags[0]
        array[41 * EXT : size, :] = array[41 * EXT : size, :] * flags[1]

    for message, tile, single in ((up, 6, 47), (down, 0, 8)):
        for p in range(42):
            message[8 * p : 8 * p + 8, :] = out[p * EXT + 8 * tile : p * EXT + 8 * tile + 8, :]
        message[376:384, :] = jnp.zeros((8, CZ), F32)
        message[336:378, :] = out[pl.ds(single, 42, stride=EXT), :]
        line[40:48, :] = jnp.zeros((8, CZ), F32)
        line[0:42, :] = out_strip[pl.ds(single, 42, stride=EXT), :]
        values = [out_strip[p * EXT + 8 * tile : p * EXT + 8 * tile + 8, :] for p in range(42)]
        values += [line[8 * j : 8 * j + 8, :] for j in range(6)]
        pack_tiles(message, 384, values)


def fold_y_kernel(flags, sol, strip, low, high, out, message, work, line):
    narrow = lanes(8) < 9
    out[...] = sol[...]
    work[...] = strip[...]
    for source, tile, single, flag in ((low, 1, 7, 2), (high, 5, 48, 3)):
        for p in range(42):
            at = p * EXT + 8 * tile
            out[at : at + 8, :] = out[at : at + 8, :] + source[8 * p : 8 * p + 8, :]
            value = jnp.where(narrow, unpack_tile(source, 384, p), 0.0)
            work[at : at + 8, :] = work[at : at + 8, :] + value
        at = pl.ds(single, 42, stride=EXT)
        out[at, :] = (out[at, :] + source[336:378, :]) * flags[flag]
        for j in range(6):
            line[8 * j : 8 * j + 8, :] = jnp.where(narrow, unpack_tile(source, 384, 42 + j), 0.0)
        work[at, :] = (work[at, :] + line[0:42, :]) * flags[flag]
    values = []
    for p in range(42):
        for t in range(1, 6):
            at = p * EXT + 8 * t
            values.append(work[at : at + 8, :])
    for k, single in enumerate((7, 48)):
        line[48 * k + 40 : 48 * k + 48, :] = jnp.zeros((8, CZ), F32)
        line[48 * k : 48 * k + 42, :] = work[pl.ds(single, 42, stride=EXT), :]
        values += [line[48 * k + 8 * j : 48 * k + 8 * j + 8, :] for j in range(6)]
    pack_tiles(message, 0, values)


def conduct_kernel(h, low, high, before, after, out):
    out[0:EXT, :] = before[504:560, :]
    out[41 * EXT : 42 * EXT, :] = after[504:560, :]

    def visit(x, _):
        out[rows_at((x + 1) * EXT + 8, C), :] = h[rows_at(x * C, C), :]
        return 0

    lax.fori_loop(0, C, visit, 0, unroll=4)
    out[pl.ds(EXT + 7, C, stride=EXT), :] = low[360:400, :]
    out[pl.ds(EXT + 48, C, stride=EXT), :] = high[360:400, :]


def apply_kernel(sol, own_z, far_z, resid, cond, coef, out, applied, sums, field, pack, line):
    gz = lax.axis_index("gz")
    lane = lanes(ZROWS2)
    at_face = lax.rem(lane, 9) == jnp.where(gz == 0, 8, 0)
    shift = jnp.where(gz == 0, 7, 121)
    pack[...] = far_z[...] + jnp.where(at_face, roll(own_z[...], shift, 1), 0.0)
    lane8 = lanes(8)
    folded = jnp.where(gz == 0, lane8 - 120, 7 - lane8) >= 0
    base = jnp.where(gz == 0, 120, 127)
    toward = jnp.where(gz == 0, 119, 128)

    def tile(index, to):
        q = index // PER
        return roll(pack[rows_at(8 * q, 8), :], to - 9 * (index - q * PER), 1)

    def visit_fold(p, _):
        for t in range(5):
            at = rows_at(p * EXT + 8 * t + 8, 8)
            field[at, :] = sol[at, :] + jnp.where(folded, tile(p * 5 + t, base), 0.0)
        return 0

    lax.fori_loop(0, 42, visit_fold, 0, unroll=2)
    for k, single in enumerate((7, 48)):
        for j in range(6):
            line[8 * j : 8 * j + 8, :] = jnp.where(folded, tile(210 + 6 * k + j, base), 0.0)
        at = pl.ds(single, 42, stride=EXT)
        field[at, :] = sol[at, :] + line[0:42, :]

    lane40 = lanes(C)
    z_half = jnp.where(lane40 < CZ - 1, 0.5, 0.0)
    outer = jnp.where(lane40 == jnp.where(gz == 0, 0, 127), 0.5, 0.0)

    def visit(x, carry):
        flux_x, sum_a, sum_b = carry
        at = (x + 1) * EXT
        own = rows_at(at + 8, C)
        z, h = field[own, :], cond[own, :]
        ahead = rows_at(at + EXT + 8, C)
        next_x = 0.5 * (h + cond[ahead, :]) * (field[ahead, :] - z)
        z_plane, h_plane = field[rows_at(at, EXT), :], cond[rows_at(at, EXT), :]
        z_up, h_up = roll(z_plane, -1, 0)[8:48], roll(h_plane, -1, 0)[8:48]
        z_down, h_down = roll(z_plane, 1, 0)[8:48], roll(h_plane, 1, 0)[8:48]
        net = (next_x - flux_x) + 0.5 * ((h + h_up) * (z_up - z) - (h + h_down) * (z - z_down))
        flux_z = z_half * (h + roll(h, -1, 1)) * (roll(z, -1, 1) - z)
        far = jnp.concatenate([tile((x + 1) * 5 + t, toward) for t in range(5)], axis=0)
        to = rows_at(x * C, C)
        net = net + (flux_z - roll(flux_z, 1, 1)) + coef[to, :] * (far - z) - outer * h * z
        image = mass_term * z - net
        out[to, :] = z
        applied[to, :] = image
        a, b = resid[to, :] * z, z * image
        for t in range(5):
            sum_a = sum_a + a[8 * t : 8 * t + 8]
            sum_b = sum_b + b[8 * t : 8 * t + 8]
        return next_x, sum_a, sum_b

    own = pl.ds(EXT + 8, C)
    behind = pl.ds(8, C)
    flux = 0.5 * (cond[own, :] + cond[behind, :]) * (field[own, :] - field[behind, :])
    zero8 = jnp.zeros((8, CZ), F32)
    _, sum_a, sum_b = lax.fori_loop(0, C, visit, (flux, zero8, zero8), unroll=2)
    total_a = jnp.sum(sum_a, axis=0, keepdims=True)
    total_b = jnp.sum(sum_b, axis=0, keepdims=True)
    row = lax.broadcasted_iota(jnp.int32, (8, CZ), 0)
    sums[...] = jnp.where(row == 0, total_a, jnp.where(row == 1, total_b, 0.0))


def update_kernel(sums, guess, resid, field, applied, solution_out, resid_out):
    total = jnp.sum(sums[...], axis=1, keepdims=True)
    step = total[0:1, :] / total[1:2, :]
    solution_out[...] = guess[...] + step * field[...]
    resid_out[...] = resid[...] - step * applied[...]


def on_device(gx, splits, right_side, guess_field, conduct_field):
    shape = right_side.shape
    b, v, h = (a.reshape(C * C, CZ) for a in (right_side, guess_field, conduct_field))
    n_gx, n_gy = lax.axis_size(gx), lax.axis_size("gy")
    at_x, at_y = lax.axis_index(gx), lax.axis_index("gy")
    flags = jnp.stack([at_x > 0, at_x < n_gx - 1, at_y > 0, at_y < n_gy - 1]).astype(F32)

    def exchange(axis, up, down):
        n = lax.axis_size(axis)
        forward = [(i, i + 1) for i in range(n - 1)]
        backward = [(i + 1, i) for i in range(n - 1)]
        return lax.ppermute(up, axis, forward), lax.ppermute(down, axis, backward)

    def swap(value):
        return lax.ppermute(value, "gz", [(0, 1), (1, 0)])

    plane, forward, inverse, denom, eigen = tables()

    part, vh, up, down, edge = call(
        residual_kernel, (1600, 1600, YROWS, YROWS, 160), v, h, b, name="residual"
    )
    low, high = exchange("gy", up, down)
    part, vh, right, left = call(
        extend_y_kernel,
        (C * EXT, C * EXT, XROWS, XROWS),
        flags, part, vh, up, down, edge, low, high,
        smem=(0,),
        name="extend_y",
    )
    before, after = exchange(gx, right, left)
    ext, own_z = call(
        extend_x_kernel,
        (EXT * EXT, ZROWS),
        flags, part, vh, right, left, before, after,
        scratch=[pltpu.VMEM((EXT * EXT, CZ), F32)],
        smem=(0,),
        name="extend_x",
    )
    far_z = swap(own_z)
    (cond,) = call(conduct_kernel, (42 * EXT,), h, low, high, before, after, name="conduct")
    big = pltpu.VMEM((EXT * EXT, CZ), F32)
    small = pltpu.VMEM((ZROWS, CZ), F32)
    resid, coef, sol, strip, right, left = call(
        solve_kernel,
        (1600, 1600, EXT * EXT, EXT * EXT, XROWS2, XROWS2),
        eigen, ext, own_z, far_z, plane, forward, inverse, denom,
        scratch=[small, small, big, big, big, big, big],
        smem=(0,),
        limit=32,
        name="solve",
    )
    before, after = exchange(gx, right, left)
    sol, strip, up, down = call(
        fold_x_kernel,
        (42 * EXT, 42 * EXT, YROWS2, YROWS2),
        flags, sol, strip, before, after,
        scratch=[pltpu.VMEM((48, CZ), F32)],
        smem=(0,),
        name="fold_x",
    )
    low, high = exchange("gy", up, down)
    sol, own_z = call(
        fold_y_kernel,
        (42 * EXT, ZROWS2),
        flags, sol, strip, low, high,
        scratch=[pltpu.VMEM((42 * EXT, CZ), F32), pltpu.VMEM((96, CZ), F32)],
        smem=(0,),
        name="fold_y",
    )
    far_z = swap(own_z)
    field, applied, sums = call(
        apply_kernel,
        (1600, 1600, 8),
        sol, own_z, far_z, resid, cond, coef,
        scratch=[
            pltpu.VMEM((42 * EXT, CZ), F32),
            pltpu.VMEM((ZROWS2, CZ), F32),
            pltpu.VMEM((48, CZ), F32),
        ],
        name="apply",
    )
    for axes in splits:
        sums = lax.psum(sums, axes)
    out, resid = call(
        update_kernel, (1600, 1600), sums, v, resid, field, applied, name="update"
    )
    return out.reshape(shape), resid.reshape(shape)


def solution(mesh):
    n_gx, n_gy, n_gz = mesh.devices.shape
    if n_gx == 64:
        mesh = Mesh(mesh.devices.reshape(4, 8, 2, n_gy, n_gz), ("gx_x", "gx_y", "gx_c", "gy", "gz"))
        gx = ("gx_x", "gx_y", "gx_c")
        splits = (("gx_c",), ("gx_x",), ("gx_y",), ("gy", "gz"))
    else:
        gx = "gx"
        splits = (("gx", "gy", "gz"),)
    placed = P(gx, "gy", "gz")
    return jax.shard_map(
        functools.partial(on_device, gx, splits),
        mesh=mesh,
        in_specs=(placed,) * 3,
        out_specs=(placed,) * 2,
        check_vma=False,
    )
```

profile of v0, /device:TPU:64, one launch (start us, length us, event | category | flops | bytes accessed | tf_op | source)
XLA Modules:
  0.0 161.9 jit_solution(10429949211004534805)
XLA Ops:
  0.6 1.1 copy-done
  1.8 1.1 copy-done.2
  2.9 1.1 copy-done.4
  4.1 2.2 %residual.1 = (f32[1600,128]{1,0:T(8,128)S(1)}, f32[1600,128]{1,0:T(8,128)S(1)}, f32[440,128]{1,0:T(8,128)S(1)}, f32[440,128]{1,0:T(8,128)S(1)}, f32[160,128]{1,0:T(8,128)S(1)}) custom-call(f32[1600,128]{1,0:T(8,128)S(1)} %bitcast.11, f32[1600,128]{1,0:T(8,128)S(1)} %bitcast.9, f32[1600,128]{1,0:T(8,128)S(1)} %bitcast.13), custom_call_target="tpu_custom_call" | custom-call | tf_op jit(solution)/shard_map/residual/pallas_call | solution.py:105
  6.3 6.1 %collective-permute-start = (f32[440,128]{1,0:T(8,128)S(1)}, f32[440,128]{1,0:T(8,128)S(1)}, u32[]{:S(2)}, u32[]{:S(2)}) collective-permute-start(f32[440,128]{1,0:T(8,128)S(1)} %get-tuple-element.32.up), channel_id=1, source_target_pairs={{0,2},{2,4},{4,6},{1,3},{3,5},{5,7},{8,10},{10,12},{12,14},{9,11},... | collective-permute-start | bytes 675848 | tf_op jit(solution)/shard_map/ppermute | solution.py:580
  12.4 1.3 collective-permute-start.1
  13.8 7.3 %collective-permute-done.low = f32[440,128]{1,0:T(8,128)S(1)} collective-permute-done((f32[440,128]{1,0:T(8,128)S(1)}, f32[440,128]{1,0:T(8,128)S(1)}, u32[]{:S(2)}, u32[]{:S(2)}) %collective-permute-start) | collective-permute-done | bytes 225312 | tf_op jit(solution)/shard_map/ppermute | solution.py:580
  21.1 4.8 %collective-permute-done.1.high = f32[440,128]{1,0:T(8,128)S(1)} collective-permute-done((f32[440,128]{1,0:T(8,128)S(1)}, f32[440,128]{1,0:T(8,128)S(1)}, u32[]{:S(2)}, u32[]{:S(2)}) %collective-permute-start.1) | collective-permute-done | bytes 225312 | tf_op jit(solution)/shard_map/ppermute | solution.py:580
  25.9 2.2 %extend_y.1 = (f32[2240,128]{1,0:T(8,128)S(1)}, f32[2240,128]{1,0:T(8,128)S(1)}, f32[568,128]{1,0:T(8,128)S(1)}, f32[568,128]{1,0:T(8,128)S(1)}) custom-call(f32[4]{0:T(128)S(1)} %add_convert_fusion.flags, f32[1600,128]{1,0:T(8,128)S(1)} %get-tuple-element.30.part, f32[1600,128]{1,0:T(8,128)S(1)} %get-tuple-element.31.vh, ...), custom_call_target="tpu_custom_call" | custom-call | tf_op jit(solution)/shard_map/extend_y/pallas_call | solution.py:105
  28.1 1.3 collective-permute-start.2
  29.4 1.3 collective-permute-start.3
  30.7 4.0 %collective-permute-done.3.after = f32[568,128]{1,0:T(8,128)S(1)} collective-permute-done((f32[568,128]{1,0:T(8,128)S(1)}, f32[568,128]{1,0:T(8,128)S(1)}, u32[]{:S(2)}, u32[]{:S(2)}) %collective-permute-start.3) | collective-permute-done | bytes 290848 | tf_op jit(solution)/shard_map/ppermute | solution.py:580
  34.7 2.9 %extend_x.1 = (f32[3136,128]{1,0:T(8,128)S(1)}, f32[264,128]{1,0:T(8,128)S(1)}) custom-call(f32[4]{0:T(128)S(1)} %add_convert_fusion.flags, f32[2240,128]{1,0:T(8,128)S(1)} %get-tuple-element.35.part, f32[2240,128]{1,0:T(8,128)S(1)} %get-tuple-element.36.vh, f32[568,128]{1,0:T(8,128)S(1)} %get-tuple-element.37.right, f32[568,128]{1,0:T(8,128)S(1)} %get-tuple-element.38.left, ...), custom_call_target="tpu_custom_call" | custom-call | tf_op jit(solution)/shard_map/extend_x/pallas_call | solution.py:105
  37.6 5.4 %collective-permute-start.4 = (f32[264,128]{1,0:T(8,128)S(1)}, f32[264,128]{1,0:T(8,128)S(1)}, u32[]{:S(2)}, u32[]{:S(2)}) collective-permute-start(f32[264,128]{1,0:T(8,128)S(1)} %get-tuple-element.40.own_z), channel_id=1, source_target_pairs={{0,1},{1,0},{2,3},{3,2},{4,5},{5,4},{6,7},{7,6},{8,9},{9,8},{10,11... | collective-permute-start | bytes 405512 | tf_op jit(solution)/shard_map/ppermute | solution.py:583
  43.0 3.0 %collective-permute-done.4.far_z = f32[264,128]{1,0:T(8,128)S(1)} collective-permute-done((f32[264,128]{1,0:T(8,128)S(1)}, f32[264,128]{1,0:T(8,128)S(1)}, u32[]{:S(2)}, u32[]{:S(2)}) %collective-permute-start.4) | collective-permute-done | bytes 135200 | tf_op jit(solution)/shard_map/ppermute | solution.py:583
  46.1 19.2 %solve.1 = (f32[1600,128]{1,0:T(8,128)S(1)}, f32[1600,128]{1,0:T(8,128)S(1)}, f32[3136,128]{1,0:T(8,128)S(1)}, f32[3136,128]{1,0:T(8,128)S(1)}, f32[544,128]{1,0:T(8,128)S(1)}, /*index=5*/f32[544,128]{1,0:T(8,128)S(1)}) custom-call(f32[56]{0:T(128)S(1)} %copy-done.9, f32[3136,128]{1,0:T(8,128)S(1)} %get-tuple-element.39.ext, ...), custom_call_target="tpu_custom_call" | custom-call | tf_op jit(solution)/shard_map/solve/pallas_call | solution.py:105
  65.3 6.1 %collective-permute-start.5 = (f32[544,128]{1,0:T(8,128)S(1)}, f32[544,128]{1,0:T(8,128)S(1)}, u32[]{:S(2)}, u32[]{:S(2)}) collective-permute-start(f32[544,128]{1,0:T(8,128)S(1)} %get-tuple-element.43), channel_id=1, source_target_pairs={{0,8},{8,16},{16,24},{24,32},{32,40},{40,48},{48,56},{56,64},{64,7... | collective-permute-start | bytes 835592 | tf_op jit(solution)/shard_map/ppermute | solution.py:580
  71.3 1.3 collective-permute-start.6
  72.6 2.6 %collective-permute-done.6.after = f32[544,128]{1,0:T(8,128)S(1)} collective-permute-done((f32[544,128]{1,0:T(8,128)S(1)}, f32[544,128]{1,0:T(8,128)S(1)}, u32[]{:S(2)}, u32[]{:S(2)}) %collective-permute-start.6) | collective-permute-done | bytes 278560 | tf_op jit(solution)/shard_map/ppermute | solution.py:580
  76.2 5.7 %collective-permute-start.7 = (f32[416,128]{1,0:T(8,128)S(1)}, f32[416,128]{1,0:T(8,128)S(1)}, u32[]{:S(2)}, u32[]{:S(2)}) collective-permute-start(f32[416,128]{1,0:T(8,128)S(1)} %get-tuple-element.47), channel_id=1, source_target_pairs={{0,2},{2,4},{4,6},{1,3},{3,5},{5,7},{8,10},{10,12},{12,14},{9,11},... | collective-permute-start | bytes 638984 | tf_op jit(solution)/shard_map/ppermute | solution.py:580
  82.0 1.3 collective-permute-start.8
  83.3 4.5 %collective-permute-done.7.low = f32[416,128]{1,0:T(8,128)S(1)} collective-permute-done((f32[416,128]{1,0:T(8,128)S(1)}, f32[416,128]{1,0:T(8,128)S(1)}, u32[]{:S(2)}, u32[]{:S(2)}) %collective-permute-start.7) | collective-permute-done | bytes 213024 | tf_op jit(solution)/shard_map/ppermute | solution.py:580
  87.8 2.9 %collective-permute-done.8.high = f32[416,128]{1,0:T(8,128)S(1)} collective-permute-done((f32[416,128]{1,0:T(8,128)S(1)}, f32[416,128]{1,0:T(8,128)S(1)}, u32[]{:S(2)}, u32[]{:S(2)}) %collective-permute-start.8) | collective-permute-done | bytes 213024 | tf_op jit(solution)/shard_map/ppermute | solution.py:580
  90.7 1.0 fold_y.1
  91.7 7.9 %collective-permute-start.9 = (f32[128,128]{1,0:T(8,128)S(1)}, f32[128,128]{1,0:T(8,128)S(1)}, u32[]{:S(2)}, u32[]{:S(2)}) collective-permute-start(f32[128,128]{1,0:T(8,128)S(1)} %get-tuple-element.50.own_z), channel_id=1, source_target_pairs={{0,1},{1,0},{2,3},{3,2},{4,5},{5,4},{6,7},{7,6},{8,9},{9,8},{10,11... | collective-permute-start | bytes 196616 | tf_op jit(solution)/shard_map/ppermute | solution.py:583
  99.7 2.1 %collective-permute-done.9.far_z = f32[128,128]{1,0:T(8,128)S(1)} collective-permute-done((f32[128,128]{1,0:T(8,128)S(1)}, f32[128,128]{1,0:T(8,128)S(1)}, u32[]{:S(2)}, u32[]{:S(2)}) %collective-permute-start.9) | collective-permute-done | bytes 65568 | tf_op jit(solution)/shard_map/ppermute | solution.py:583
  101.9 6.6 %apply.1 = (f32[1600,128]{1,0:T(8,128)S(1)}, f32[1600,128]{1,0:T(8,128)S(1)}, f32[8,128]{1,0:T(8,128)S(1)}) custom-call(f32[2352,128]{1,0:T(8,128)S(1)} %get-tuple-element.49.sol, f32[128,128]{1,0:T(8,128)S(1)} %get-tuple-element.50.own_z, f32[128,128]{1,0:T(8,128)S(1)} %collective-permute-done.9.far_z, f32[1600,128]{1,0:T(8,128)S(1)} %get-tuple-element.51.resid, ...), custom_call_target="tpu_custom_call" | custom-call | tf_op jit(solution)/shard_map/apply/pallas_call | solution.py:105
  108.4 3.3 %psum.28 = f32[8,128]{1,0:T(8,128)S(1)} all-reduce(f32[8,128]{1,0:T(8,128)S(1)} %get-tuple-element.53), channel_id=1, replica_groups=mesh['gx_x'=4,'gx_y'=8,'gx_c'=2,'gy'=4,'gz'=2] {'gx_c'}, use_global_device_ids=true, to_apply=%region_0.0 | all-reduce | flops 1024 | bytes 8192 | tf_op jit(solution)/shard_map/psum | solution.py:651
  111.7 17.0 %psum.29 = f32[8,128]{1,0:T(8,128)S(1)} all-reduce(f32[8,128]{1,0:T(8,128)S(1)} %psum.28), channel_id=1, replica_groups=mesh['gx_x'=4,'gx_y'=8,'gx_c'=2,'gy'=4,'gz'=2] {'gx_x'}, use_global_device_ids=true, to_apply=%region_1.0 | all-reduce | flops 1024 | bytes 8192 | tf_op jit(solution)/shard_map/psum | solution.py:651
  128.7 15.7 %psum.30 = f32[8,128]{1,0:T(8,128)S(1)} all-reduce(f32[8,128]{1,0:T(8,128)S(1)} %psum.29), channel_id=1, replica_groups=mesh['gx_x'=4,'gx_y'=8,'gx_c'=2,'gy'=4,'gz'=2] {'gx_y'}, use_global_device_ids=true, to_apply=%region_2.0 | all-reduce | flops 1024 | bytes 8192 | tf_op jit(solution)/shard_map/psum | solution.py:651
  144.4 16.1 %psum.31.sums = f32[8,128]{1,0:T(8,128)S(1)} all-reduce(f32[8,128]{1,0:T(8,128)S(1)} %psum.30), channel_id=1, replica_groups=mesh['gx_x'=4,'gx_y'=8,'gx_c'=2,'gy'=4,'gz'=2] {'gy','gz'}, use_global_device_ids=true, to_apply=%region_3.0 | all-reduce | flops 1024 | bytes 8192 | tf_op jit(solution)/shard_map/psum | solution.py:651
  160.5 1.4 update.1
  (22 shorter events, 1.2 us)
Async XLA Ops:
  0.6 1.1 copy-start
  1.8 1.1 copy-start.2
  2.9 1.1 copy-start.4
  6.3 14.8 %collective-permute-start = (f32[440,128]{1,0:T(8,128)S(1)}, f32[440,128]{1,0:T(8,128)S(1)}, u32[]{:S(2)}, u32[]{:S(2)}) collective-permute-start(f32[440,128]{1,0:T(8,128)S(1)} %get-tuple-element.32.up), channel_id=1, source_target_pairs={{0,2},{2,4},{4,6},{1,3},{3,5},{5,7},{8,10},{10,12},{12,14},{9,11},... | collective-permute-start | bytes 675848 | tf_op jit(solution)/shard_map/ppermute | solution.py:580
  12.4 13.5 %collective-permute-start.1 = (f32[440,128]{1,0:T(8,128)S(1)}, f32[440,128]{1,0:T(8,128)S(1)}, u32[]{:S(2)}, u32[]{:S(2)}) collective-permute-start(f32[440,128]{1,0:T(8,128)S(1)} %get-tuple-element.33.down), channel_id=1, source_target_pairs={{2,0},{4,2},{6,4},{3,1},{5,3},{7,5},{10,8},{12,10},{14,12},{11,9},... | collective-permute-start | bytes 675848 | tf_op jit(solution)/shard_map/ppermute | solution.py:580
  28.1 2.6 %collective-permute-start.2 = (f32[568,128]{1,0:T(8,128)S(1)}, f32[568,128]{1,0:T(8,128)S(1)}, u32[]{:S(2)}, u32[]{:S(2)}) collective-permute-start(f32[568,128]{1,0:T(8,128)S(1)} %get-tuple-element.37.right), channel_id=1, source_target_pairs={{0,8},{8,16},{16,24},{24,32},{32,40},{40,48},{48,56},{56,64},{64,7... | collective-permute-start | bytes 872456 | tf_op jit(solution)/shard_map/ppermute | solution.py:580
  29.4 5.3 %collective-permute-start.3 = (f32[568,128]{1,0:T(8,128)S(1)}, f32[568,128]{1,0:T(8,128)S(1)}, u32[]{:S(2)}, u32[]{:S(2)}) collective-permute-start(f32[568,128]{1,0:T(8,128)S(1)} %get-tuple-element.38.left), channel_id=1, source_target_pairs={{8,0},{16,8},{24,16},{32,24},{40,32},{48,40},{56,48},{64,56},{72,6... | collective-permute-start | bytes 872456 | tf_op jit(solution)/shard_map/ppermute | solution.py:580
  34.7 11.3 %copy-start.5 = (bf16[2,2,256,256]{3,2,1,0:T(8,128)(2,1)S(1)}, bf16[2,2,256,256]{3,2,1,0:T(8,128)(2,1)}, u32[]{:S(2)}) copy-start(bf16[2,2,256,256]{3,2,1,0:T(8,128)(2,1)} %constant.39.clone.forward) | copy-start | bytes 1572868
  34.7 11.3 %copy-start.6 = (bf16[2,2,256,256]{3,2,1,0:T(8,128)(2,1)S(1)}, bf16[2,2,256,256]{3,2,1,0:T(8,128)(2,1)}, u32[]{:S(2)}) copy-start(bf16[2,2,256,256]{3,2,1,0:T(8,128)(2,1)} %constant.40.clone.inverse) | copy-start | bytes 1572868
  34.7 11.3 %copy-start.7 = (f32[56,256]{1,0:T(8,128)S(1)}, f32[56,256]{1,0:T(8,128)}, u32[]{:S(2)}) copy-start(f32[56,256]{1,0:T(8,128)} %constant.41.clone.denom) | copy-start | bytes 172036
  34.7 11.3 %copy-start.8 = (bf16[56,192]{1,0:T(8,128)(2,1)S(1)}, bf16[56,192]{1,0:T(8,128)(2,1)}, u32[]{:S(2)}) copy-start(bf16[56,192]{1,0:T(8,128)(2,1)} %constant.38.clone.plane) | copy-start | bytes 64516
  34.7 11.3 %copy-start.9 = (f32[56]{0:T(128)S(1)}, f32[56]{0:T(128)}, u32[]{:S(2)}) copy-start(f32[56]{0:T(128)} %constant.37.clone.eigen) | copy-start | bytes 676
  37.6 8.4 %collective-permute-start.4 = (f32[264,128]{1,0:T(8,128)S(1)}, f32[264,128]{1,0:T(8,128)S(1)}, u32[]{:S(2)}, u32[]{:S(2)}) collective-permute-start(f32[264,128]{1,0:T(8,128)S(1)} %get-tuple-element.40.own_z), channel_id=1, source_target_pairs={{0,1},{1,0},{2,3},{3,2},{4,5},{5,4},{6,7},{7,6},{8,9},{9,8},{10,11... | collective-permute-start | bytes 405512 | tf_op jit(solution)/shard_map/ppermute | solution.py:583
  65.3 7.4 %collective-permute-start.5 = (f32[544,128]{1,0:T(8,128)S(1)}, f32[544,128]{1,0:T(8,128)S(1)}, u32[]{:S(2)}, u32[]{:S(2)}) collective-permute-start(f32[544,128]{1,0:T(8,128)S(1)} %get-tuple-element.43), channel_id=1, source_target_pairs={{0,8},{8,16},{16,24},{24,32},{32,40},{40,48},{48,56},{56,64},{64,7... | collective-permute-start | bytes 835592 | tf_op jit(solution)/shard_map/ppermute | solution.py:580
  71.3 3.9 %collective-permute-start.6 = (f32[544,128]{1,0:T(8,128)S(1)}, f32[544,128]{1,0:T(8,128)S(1)}, u32[]{:S(2)}, u32[]{:S(2)}) collective-permute-start(f32[544,128]{1,0:T(8,128)S(1)} %get-tuple-element.44), channel_id=1, source_target_pairs={{8,0},{16,8},{24,16},{32,24},{40,32},{48,40},{56,48},{64,56},{72,6... | collective-permute-start | bytes 835592 | tf_op jit(solution)/shard_map/ppermute | solution.py:580
  76.2 11.6 %collective-permute-start.7 = (f32[416,128]{1,0:T(8,128)S(1)}, f32[416,128]{1,0:T(8,128)S(1)}, u32[]{:S(2)}, u32[]{:S(2)}) collective-permute-start(f32[416,128]{1,0:T(8,128)S(1)} %get-tuple-element.47), channel_id=1, source_target_pairs={{0,2},{2,4},{4,6},{1,3},{3,5},{5,7},{8,10},{10,12},{12,14},{9,11},... | collective-permute-start | bytes 638984 | tf_op jit(solution)/shard_map/ppermute | solution.py:580
  82.0 8.7 %collective-permute-start.8 = (f32[416,128]{1,0:T(8,128)S(1)}, f32[416,128]{1,0:T(8,128)S(1)}, u32[]{:S(2)}, u32[]{:S(2)}) collective-permute-start(f32[416,128]{1,0:T(8,128)S(1)} %get-tuple-element.48), channel_id=1, source_target_pairs={{2,0},{4,2},{6,4},{3,1},{5,3},{7,5},{10,8},{12,10},{14,12},{11,9},... | collective-permute-start | bytes 638984 | tf_op jit(solution)/shard_map/ppermute | solution.py:580
  90.7 8.9 %copy-start.1 = (f32[40,40,128]{2,1,0:T(8,128)S(1)}, f32[40,40,128]{2,1,0:T(8,128)}, u32[]{:S(2)}) copy-start(f32[40,40,128]{2,1,0:T(8,128)} %param.10) | copy-start | bytes 2457604
  91.7 10.2 %collective-permute-start.9 = (f32[128,128]{1,0:T(8,128)S(1)}, f32[128,128]{1,0:T(8,128)S(1)}, u32[]{:S(2)}, u32[]{:S(2)}) collective-permute-start(f32[128,128]{1,0:T(8,128)S(1)} %get-tuple-element.50.own_z), channel_id=1, source_target_pairs={{0,1},{1,0},{2,3},{3,2},{4,5},{5,4},{6,7},{7,6},{8,9},{9,8},{10,11... | collective-permute-start | bytes 196616 | tf_op jit(solution)/shard_map/ppermute | solution.py:583
  101.9 58.6 %copy-start.3 = (f32[40,40,128]{2,1,0:T(8,128)S(1)}, f32[40,40,128]{2,1,0:T(8,128)}, u32[]{:S(2)}) copy-start(f32[40,40,128]{2,1,0:T(8,128)} %param.9) | copy-start | bytes 2457604
where the time goes:
time: 162 us
  blocking collectives  52 us (32%)
  starting transfers between devices  37.8 us (23%)
  Pallas kernels  36.6 us (23%)
  waiting for transfers between devices  31.2 us (19%)
  local copies, waits for them, and re-layouts  3.46 us (2%)
    psum x4, blocking collectives, on_device(): sums = lax.psum(sums, axes)  52 us
    pallas_call x9, Pallas kernels, call(): pl.pallas_call(body, out_shape=[jax.ShapeDtypeStruct((rows, CZ), F32) for...  36.6 us
    ppermute x8, waiting for transfers between devices, exchange(): return (lax.ppermute(up, axis, forward), lax.ppermute(down, axis, backward))  26.1 us
    ppermute x8, starting transfers between devices, exchange(): return (lax.ppermute(up, axis, forward), lax.ppermute(down, axis, backward))  24.4 us
    ppermute x2, starting transfers between devices, swap(): return lax.ppermute(value, 'gz', [(0, 1), (1, 0)])  13.4 us
    ppermute x2, waiting for transfers between devices, swap(): return lax.ppermute(value, 'gz', [(0, 1), (1, 0)])  5.1 us
    unnamed x20, local copies, waits for them, and re-layouts  3.46 us
  transfers between devices with their start and end apart: 10, of which 8 were waited for; matrix products, arithmetic and copies ran while one was open for 0% of the time, Pallas kernels for 0%

commit v1 on v0

v1 whole, which is shorter than its diff:
```python
import functools

import jax
import jax.numpy as jnp
import ml_dtypes
import numpy as np
from jax import lax
from jax.experimental import pallas as pl
from jax.experimental.pallas import tpu as pltpu
from jax.sharding import Mesh
from jax.sharding import PartitionSpec as P

OVER = 8
C = 40
CZ = 128
EXT = C + 2 * OVER
EXTZ = CZ + 2 * OVER
TILES = EXT // 8
stiff_scale = 3.0
mass_term = 0.001

F32 = jnp.float32
BF16 = jnp.bfloat16
VMEM = pl.BlockSpec(memory_space=pltpu.VMEM)
SMEM = pl.BlockSpec(memory_space=pltpu.SMEM)
HBM = pl.BlockSpec(memory_space=pltpu.HBM)

YROWS = 440
XROWS = 568
PER_Z = 12
BLOCKS_Z = -(-EXT // PER_Z)
ZROWS = BLOCKS_Z * EXT
PER = 14
XROWS2 = 9 * EXT + 40
YROWS2 = 416
ZGROUPS2 = 42 * 5 + 12
ZROWS2 = 8 * -(-ZGROUPS2 // PER)


def sine_table(count):
    k = np.arange(1, count + 1)
    basis = np.sqrt(2.0 / (count + 1)) * np.sin(np.pi * k[:, None] * k[None, :] / (count + 1))
    eigen = 2.0 - 2.0 * np.cos(np.pi * k / (count + 1))
    return basis, eigen


def two_parts(table):
    high = table.astype(ml_dtypes.bfloat16)
    low = (table - high.astype(np.float64)).astype(ml_dtypes.bfloat16)
    return high, low


@functools.cache
def tables():
    basis, eigen = sine_table(EXT)
    basis_z, eigen_z = sine_table(EXTZ)
    high, low = two_parts(basis)
    plane = np.zeros((EXT, 192), ml_dtypes.bfloat16)
    plane[:, 0:EXT] = high
    plane[:, 64 : 64 + EXT] = low
    plane[:, 128 : 128 + EXT] = high
    forward = np.zeros((2, 256, 256))
    inverse = np.zeros((2, 256, 256))
    for gz in range(2):
        own = basis_z[8 : 8 + CZ]
        strip = basis_z[136:144] if gz == 0 else basis_z[0:8]
        face_own, face_far = (135, 136) if gz == 0 else (8, 7)
        forward[gz, :CZ, :EXTZ] = own
        forward[gz, CZ, :EXTZ] = basis_z[face_own] - basis_z[face_far]
        forward[gz, CZ + 2 : CZ + 10, :EXTZ] = strip
        inverse[gz, :EXTZ, :CZ] = own.T
        inverse[gz, :EXTZ, CZ : CZ + 9] = (basis_z[135:144] if gz == 0 else basis_z[0:9]).T

    def stacked(table):
        high, low = two_parts(table)
        return np.concatenate([high, high, low], axis=1)

    denom = np.full((EXT, 256), 1.0)
    denom[:, :EXTZ] = stiff_scale * (eigen[:, None] + eigen_z[None, :]) + mass_term
    return (
        plane,
        stacked(forward),
        stacked(inverse),
        denom.astype(np.float32),
        (stiff_scale * eigen).astype(np.float32),
    )


def roll(value, shift, axis):
    if isinstance(shift, int):
        shift = shift % value.shape[axis]
        return value if shift == 0 else pltpu.roll(value, shift, axis)
    return pltpu.roll(value, lax.rem(shift + 2 * value.shape[axis], value.shape[axis]), axis)


def lanes(rows):
    return lax.broadcasted_iota(jnp.int32, (rows, CZ), 1)


def rows_at(start, size):
    return pl.ds(pl.multiple_of(start, 8), size)


def tile_at(index):
    return rows_at(index * 8, 8)


def call(body, out_rows, *args, scratch=(), limit=16, name=None, smem=(), hbm=(), work=0):
    place = {**{i: SMEM for i in smem}, **{i: HBM for i in hbm}}
    return pl.pallas_call(
        body,
        out_shape=[jax.ShapeDtypeStruct((rows, CZ), F32) for rows in out_rows],
        in_specs=[place.get(i, VMEM) for i in range(len(args))],
        out_specs=[VMEM] * len(out_rows),
        scratch_shapes=list(scratch),
        compiler_params=pltpu.CompilerParams(vmem_limit_bytes=limit * 2**20),
        cost_estimate=pl.CostEstimate(
            flops=int(work * 1e9), bytes_accessed=int(work * 2e6), transcendentals=0
        )
        if work
        else None,
        name=name,
    )(*args)


def strip_base():
    return jnp.where(lax.axis_index("gz") == 0, 118, 126)


def face_lane():
    return jnp.where(lax.axis_index("gz") == 0, 127, 0)


def outer_lane():
    return jnp.where(lax.axis_index("gz") == 0, 0, 127)


CHUNKS = 5


def pair_of(v, h, lane, base, face):
    return jnp.where(lane == base, roll(v, base - face, 1), 0.0) + jnp.where(
        lane == base + 1, roll(h, base + 1 - face, 1), 0.0
    )


def residual_kernel(v_in, h_in, b_in, part, up, down, edge, v, h, b, sems):
    base, face = strip_base(), face_lane()
    size = C * C // CHUNKS
    copies = []
    for c in range(CHUNKS):
        at = pl.ds(c * size, size)
        for k, (source, target) in enumerate(((v_in, v), (h_in, h), (b_in, b))):
            copies.append(pltpu.make_async_copy(source.at[at, :], target.at[at, :], sems.at[k, c]))
            copies[-1].start()
    lane, lane8 = lanes(C), lanes(8)
    row = lax.broadcasted_iota(jnp.int32, (C, CZ), 0)
    y_half = jnp.where(row > 0, 0.5, 0.0)
    z_half = jnp.where(lane < CZ - 1, 0.5, 0.0)
    outer = jnp.where(lane == outer_lane(), 0.5, 0.0)
    flux_x = jnp.zeros((C, CZ), F32)
    pack_up = jnp.zeros((8, CZ), F32)
    pack_down = jnp.zeros((8, CZ), F32)
    waited = 0
    for x in range(C):
        need = min((x + 1) // 8 + 1, CHUNKS)
        while waited < need:
            for k in range(3):
                copies[3 * waited + k].wait()
            waited += 1
        vi, hi = v[x * C : x * C + C, :], h[x * C : x * C + C, :]
        flux_y = y_half * (hi + roll(hi, 1, 0)) * (vi - roll(vi, 1, 0))
        flux_z = z_half * (hi + roll(hi, -1, 1)) * (roll(vi, -1, 1) - vi)
        applied = (
            mass_term * vi
            - (roll(flux_y, -1, 0) - flux_y)
            - (flux_z - roll(flux_z, 1, 1))
            + outer * hi * vi
        )
        if x < C - 1:
            to = pl.ds((x + 1) * C, C)
            next_x = 0.5 * (hi + h[to, :]) * (v[to, :] - vi)
            applied = applied - (next_x - flux_x)
            flux_x = next_x
        else:
            applied = applied + flux_x
        resid = b[x * C : x * C + C, :] - applied
        part[x * C : x * C + C, :] = resid
        down[8 * x : 8 * x + 8, :] = resid[0:8]
        up[8 * x : 8 * x + 8, :] = resid[32:40]
        pack_up = pack_up + roll(pair_of(vi[32:40], hi[32:40], lane8, base, face), 2 * x, 1)
        pack_down = pack_down + roll(pair_of(vi[0:8], hi[0:8], lane8, base, face), 2 * x, 1)
    up[432:440, :] = roll(pack_up, -base, 1)
    down[432:440, :] = roll(pack_down, -base, 1)
    last = (C - 1) * C
    for message, first in ((up, 32), (down, 0)):
        face_row = C - 1 if first else 0
        message[320:360, :] = v[pl.ds(face_row, C, stride=C), :]
        message[360:400, :] = h[pl.ds(face_row, C, stride=C), :]
        message[400:408, :] = v[first : first + 8, :]
        message[408:416, :] = h[first : first + 8, :]
        message[416:424, :] = v[last + first : last + first + 8, :]
        message[424:432, :] = h[last + first : last + first + 8, :]
    edge[0:40, :] = v[0:40, :]
    edge[40:80, :] = h[0:40, :]
    edge[80:120, :] = v[last : last + 40, :]
    edge[120:160, :] = h[last : last + 40, :]


def pairs_kernel(v, h, out):
    base, face = strip_base(), face_lane()
    lane = lanes(C)

    def visit(x, _):
        at = rows_at(x * C, C)
        out[at, :] = pair_of(v[at, :], h[at, :], lane, base, face)
        return 0

    lax.fori_loop(0, C, visit, 0, unroll=8)


def scale_kernel(eigen, denom, out_a, out_b):
    def visit(y, _):
        value = 1.0 / (denom[...] + eigen[y])
        at = rows_at(y * EXT, EXT)
        out_a[at, :] = value[:, :CZ]
        out_b[at, :] = value[:, CZ:]
        return 0

    lax.fori_loop(0, EXT, visit, 0, unroll=4)


def pick(pack, index, to):
    pair = lax.div(lanes(8), 2) == index
    return roll(jnp.where(pair, pack, 0.0), to - 2 * index, 1)


def extend_y_kernel(flags, part, vh, up, down, edge, low, high, out, right, left):
    base = strip_base()
    for x in range(C):
        out[x * EXT : x * EXT + 8, :] = low[8 * x : 8 * x + 8, :]
        out[x * EXT + 8 : x * EXT + 48, :] = part[x * C : x * C + C, :]
        out[x * EXT + 48 : x * EXT + 56, :] = high[8 * x : 8 * x + 8, :]
    flux = 0.5 * (low[360:400, :] + down[360:400, :]) * (down[320:360, :] - low[320:360, :])
    out[pl.ds(8, C, stride=EXT), :] = out[pl.ds(8, C, stride=EXT), :] - flux
    out[pl.ds(7, C, stride=EXT), :] = out[pl.ds(7, C, stride=EXT), :] + flux * flags[2]
    flux = 0.5 * (up[360:400, :] + high[360:400, :]) * (high[320:360, :] - up[320:360, :])
    out[pl.ds(47, C, stride=EXT), :] = out[pl.ds(47, C, stride=EXT), :] + flux
    out[pl.ds(48, C, stride=EXT), :] = out[pl.ds(48, C, stride=EXT), :] - flux * flags[3]
    for message, first, strip, own in ((left, 0, 400, 0), (right, 32, 416, 80)):
        message[0:448, :] = out[first * EXT : first * EXT + 448, :]
        for k in range(2):
            at = 448 + k * EXT
            message[at : at + 8, :] = low[strip + 8 * k : strip + 8 * k + 8, :]
            message[at + 8 : at + 48, :] = edge[own + 40 * k : own + 40 * k + 40, :]
            message[at + 48 : at + 56, :] = high[strip + 8 * k : strip + 8 * k + 8, :]
        near = jnp.zeros((8, CZ), F32)
        taken = jnp.zeros((8, CZ), F32)
        for i in range(OVER):
            x = first + i
            for t in range(5):
                at = x * C + 8 * t
                near = near + roll(vh[at : at + 8, :], 2 * (i * TILES + 1 + t), 1)
            taken = taken + pick(low[432:440, :], x, 2 * i * TILES)
            taken = taken + pick(high[432:440, :], x, 2 * (i * TILES + 6))
        message[560:568, :] = roll(near, -base, 1) + taken


def extend_x_kernel(flags, part, vh, low, high, right, left, before, after, out, message):
    base = strip_base()
    gz = lax.axis_index("gz")
    lane = lanes(8)
    strip_lanes = jnp.where(gz == 0, lane - 120, 7 - lane) >= 0
    side = OVER * EXT
    out[0:side, :] = before[0:side, :]
    out[side : side + C * EXT, :] = part[...]
    out[side + C * EXT : EXT * EXT, :] = after[0:side, :]
    flux = 0.5 * (before[504:560, :] + left[504:560, :]) * (left[448:504, :] - before[448:504, :])
    at = OVER * EXT
    out[at : at + EXT, :] = out[at : at + EXT, :] - flux
    out[at - EXT : at, :] = out[at - EXT : at, :] + flux * flags[0]
    flux = 0.5 * (right[504:560, :] + after[504:560, :]) * (after[448:504, :] - right[448:504, :])
    at = (OVER + C) * EXT
    out[at - EXT : at, :] = out[at - EXT : at, :] + flux
    out[at : at + EXT, :] = out[at : at + EXT, :] - flux * flags[1]
    for q in range(BLOCKS_Z):
        for t in range(TILES):
            near = jnp.zeros((8, CZ), F32)
            taken = jnp.zeros((8, CZ), F32)
            for j in range(min(PER_Z, EXT - q * PER_Z)):
                x = q * PER_Z + j
                own = x - OVER
                at = x * EXT + 8 * t
                value = jnp.where(strip_lanes, out[at : at + 8, :], 0.0)
                if own < 0:
                    taken = taken + pick(before[560:568, :], x * TILES + t, 10 * j)
                elif own >= C:
                    taken = taken + pick(after[560:568, :], (own - C) * TILES + t, 10 * j)
                elif t == 0:
                    taken = taken + pick(low[432:440, :], own, 10 * j)
                elif t == 6:
                    taken = taken + pick(high[432:440, :], own, 10 * j)
                else:
                    start = own * C + 8 * (t - 1)
                    value = value + vh[start : start + 8, :]
                near = near + roll(value, 10 * j, 1)
            at = q * EXT + 8 * t
            message[at : at + 8, :] = roll(near, -base, 1) + taken


def halves(value):
    high = value.astype(BF16)
    return high, (value - high.astype(F32)).astype(BF16)


def dot(a, b):
    return jnp.dot(a, b, preferred_element_type=F32)


def along_lanes(value, table):
    high, low = halves(value)
    return dot(jnp.concatenate([high, low, high], axis=1), table)


def along_rows(table, value):
    padded = jnp.concatenate([value, jnp.zeros((8, value.shape[1]), F32)], axis=0)
    high, low = halves(padded)
    return dot(table, jnp.concatenate([high, high, low], axis=0))


def beside(a, b):
    return jnp.concatenate([a, b], axis=1)


def forward_kernel(plane, ext, out, first):
    table = plane[...]

    def visit_y(c, _):
        for i in range(14):
            x = 2 * (c * 14 + i)
            at, then = rows_at(x * EXT, EXT), rows_at((x + 1) * EXT, EXT)
            value = along_rows(table, beside(ext[at, :], ext[then, :]))
            first[at, :] = value[:, :CZ]
            first[then, :] = value[:, CZ:]
        return 0

    lax.fori_loop(0, 2, visit_y, 0)

    def visit_x(c, _):
        for i in range(14):
            y = 2 * (c * 14 + i)
            value = beside(first[pl.ds(y, EXT, stride=EXT), :], first[pl.ds(y + 1, EXT, stride=EXT), :])
            value = along_rows(table, value)
            out[rows_at(y * EXT, EXT), :] = value[:, :CZ]
            out[rows_at((y + 1) * EXT, EXT), :] = value[:, CZ:]
        return 0

    lax.fori_loop(0, 2, visit_x, 0)


def face_terms(own_z, far_z):
    both = own_z[...] + far_z[...]
    half = 0.5 * roll(both, -1, 1)
    return half, half * (far_z[...] - own_z[...])


STEP = 8


def solve_kernel(
    own_z, far_z, main, plane, forward, inverse, scale_a, scale_b,
    second_a, second_b, sol, strip, right, left, halo,
):
    gz = lax.axis_index("gz")
    table = plane[...]
    _, flux = face_terms(own_z, far_z)
    pack = jnp.where(lax.rem(lanes(ZROWS), 10) == 0, flux, far_z[...])
    blocks = [pack[q * EXT : (q + 1) * EXT] for q in range(BLOCKS_Z)]
    done = []
    for q in range(0, BLOCKS_Z - 1, 2):
        value = along_rows(table, beside(blocks[q], blocks[q + 1]))
        done += [value[:, :CZ], value[:, CZ:]]
    done.append(along_rows(table, blocks[-1]))
    for x in range(EXT):
        q, j = x // PER_Z, x % PER_Z
        halo[x * EXT : (x + 1) * EXT, :] = roll(done[q], -10 * j, 1)

    forward_table = forward[gz]
    inverse_table = inverse[gz]

    def visit(c, _):
        parts = []
        for i in range(0, STEP, 2):
            y = c * STEP + i
            value = beside(halo[pl.ds(y, EXT, stride=EXT), :], halo[pl.ds(y + 1, EXT, stride=EXT), :])
            value = along_rows(table, value)
            parts.append(beside(main[rows_at(y * EXT, EXT), :], value[:, :CZ]))
            parts.append(beside(main[rows_at((y + 1) * EXT, EXT), :], value[:, CZ:]))
        value = along_lanes(jnp.concatenate(parts, axis=0), forward_table)
        at = rows_at(c * STEP * EXT, STEP * EXT)
        value = value * beside(scale_a[at, :], scale_b[at, :])
        for i in range(STEP):
            part = along_rows(table, value[i * EXT : (i + 1) * EXT])
            to = pl.ds(c * STEP + i, EXT, stride=EXT)
            second_a[to, :] = part[:, :CZ]
            second_b[to, :] = part[:, CZ:]
        return 0

    lax.fori_loop(0, EXT // STEP, visit, 0)

    for k, (message, start) in enumerate(((left, 0), (right, 47))):
        inverse_planes(table, inverse_table, second_a, second_b, sol, strip, range(start, start + 9), 9 * k)
        message[0 : 9 * EXT, :] = sol[9 * k * EXT : 9 * (k + 1) * EXT, :]
        tiles = [strip[pl.ds((9 * k * TILES + j) * 8, 8), :] for j in range(63)]
        pack_tiles(message, 9 * EXT, tiles)


def inverse_planes(table, inverse_table, second_a, second_b, sol, strip, planes, to):
    parts = []
    for x in planes:
        at = pl.ds(x * EXT, EXT)
        parts.append(along_rows(table, beside(second_a[at, :], second_b[at, :])))
    value = along_lanes(jnp.concatenate(parts, axis=0), inverse_table)
    at = pl.ds(to * EXT, len(planes) * EXT)
    sol[at, :] = value[:, :CZ]
    strip[at, :] = value[:, CZ:]


def rest_kernel(plane, inverse, second_a, second_b, sol, strip):
    table, inverse_table = plane[...], inverse[lax.axis_index("gz")]
    for first, last in ((9, 19), (19, 29), (29, 38), (38, 47)):
        inverse_planes(
            table, inverse_table, second_a, second_b, sol, strip, range(first, last), first - 9
        )


def own_kernel(h, low, high, before, after, ext, own_z, far_z, resid, c_x, c_down, c_up, c_z, c_face, cond):
    face, outer = face_lane(), outer_lane()
    half, flux = face_terms(own_z, far_z)
    half, flux = roll(half, face, 1), roll(flux, face, 1)
    lane8 = lanes(8)
    for x in range(C):
        q, j = (x + OVER) // PER_Z, (x + OVER) % PER_Z
        for t in range(5):
            at = q * EXT + 8 * (t + 1)
            to = x * C + 8 * t
            source = (x + OVER) * EXT + 8 * (t + 1)
            moved = jnp.where(lane8 == face, roll(flux[at : at + 8], -10 * j, 1), 0.0)
            resid[to : to + 8, :] = ext[source : source + 8, :] + moved
            c_face[to : to + 8, :] = jnp.where(
                lane8 == face, roll(half[at : at + 8], -10 * j, 1), 0.0
            )
    cond[0:C, :] = before[512:552, :]
    cond[C : C + C * C, :] = h[...]
    cond[C + C * C :, :] = after[512:552, :]
    z_half = jnp.where(lanes(C) < CZ - 1, 0.5, 0.0)
    row = lax.broadcasted_iota(jnp.int32, (C, CZ), 0)
    for x in range(C):
        at = x * C
        hi = h[at : at + C, :]
        c_x[at : at + C, :] = 0.5 * (cond[at : at + C, :] + hi)
        below = jnp.where(row == 0, low[360 + x : 361 + x, :], roll(hi, 1, 0))
        above = jnp.where(row == C - 1, high[360 + x : 361 + x, :], roll(hi, -1, 0))
        c_down[at : at + C, :] = 0.5 * (hi + below)
        c_up[at : at + C, :] = 0.5 * (hi + above)
        c_z[at : at + C, :] = z_half * (hi + roll(hi, -1, 1))
    c_x[C * C :, :] = 0.5 * (cond[C * C : C * C + C, :] + cond[C * C + C :, :])


def pack_tiles(message, at, values):
    for q in range(-(-len(values) // PER)):
        acc = values[q * PER]
        for j, value in enumerate(values[q * PER + 1 : (q + 1) * PER], 1):
            acc = acc + roll(value, 9 * j, 1)
        message[at + 8 * q : at + 8 * q + 8, :] = acc


def unpack_tile(message, at, index):
    q = index // PER
    return roll(message[rows_at(at + 8 * q, 8), :], -9 * (index - q * PER), 1)


def fold_x_kernel(flags, sides, side_strip, sol, strip, before, after, out, out_strip, up, down, line):
    size = 42 * EXT
    narrow = lanes(8) < 9
    for target, outside, inside in ((out, sides, sol), (out_strip, side_strip, strip)):
        target[0 : 2 * EXT, :] = outside[7 * EXT : 9 * EXT, :]
        target[2 * EXT : 40 * EXT, :] = inside[...]
        target[40 * EXT : size, :] = outside[9 * EXT : 11 * EXT, :]
    out[0 : 9 * EXT, :] = out[0 : 9 * EXT, :] + before[0 : 9 * EXT, :]
    tail = 33 * EXT
    out[tail:size, :] = out[tail:size, :] + after[0 : 9 * EXT, :]

    for j in range(63):
        for message, at in ((before, 8 * j), (after, tail + 8 * j)):
            value = jnp.where(narrow, unpack_tile(message, 9 * EXT, j), 0.0)
            out_strip[at : at + 8, :] = out_strip[at : at + 8, :] + value

    for array in (out, out_strip):
        array[0:EXT, :] = array[0:EXT, :] * flags[0]
        array[41 * EXT : size, :] = array[41 * EXT : size, :] * flags[1]

    for message, tile, single in ((up, 6, 47), (down, 0, 8)):
        for p in range(42):
            message[8 * p : 8 * p + 8, :] = out[p * EXT + 8 * tile : p * EXT + 8 * tile + 8, :]
        message[376:384, :] = jnp.zeros((8, CZ), F32)
        message[336:378, :] = out[pl.ds(single, 42, stride=EXT), :]
        line[40:48, :] = jnp.zeros((8, CZ), F32)
        line[0:42, :] = out_strip[pl.ds(single, 42, stride=EXT), :]
        values = [out_strip[p * EXT + 8 * tile : p * EXT + 8 * tile + 8, :] for p in range(42)]
        values += [line[8 * j : 8 * j + 8, :] for j in range(6)]
        pack_tiles(message, 384, values)


def fold_y_kernel(flags, sol, strip, low, high, out, message, work, line):
    narrow = lanes(8) < 9
    out[...] = sol[...]
    work[...] = strip[...]
    for source, tile, single, flag in ((low, 1, 7, 2), (high, 5, 48, 3)):
        for p in range(42):
            at = p * EXT + 8 * tile
            out[at : at + 8, :] = out[at : at + 8, :] + source[8 * p : 8 * p + 8, :]
            value = jnp.where(narrow, unpack_tile(source, 384, p), 0.0)
            work[at : at + 8, :] = work[at : at + 8, :] + value
        at = pl.ds(single, 42, stride=EXT)
        out[at, :] = (out[at, :] + source[336:378, :]) * flags[flag]
        for j in range(6):
            line[8 * j : 8 * j + 8, :] = jnp.where(narrow, unpack_tile(source, 384, 42 + j), 0.0)
        work[at, :] = (work[at, :] + line[0:42, :]) * flags[flag]
    values = []
    for p in range(42):
        for t in range(1, 6):
            at = p * EXT + 8 * t
            values.append(work[at : at + 8, :])
    for k, single in enumerate((7, 48)):
        line[48 * k + 40 : 48 * k + 48, :] = jnp.zeros((8, CZ), F32)
        line[48 * k : 48 * k + 42, :] = work[pl.ds(single, 42, stride=EXT), :]
        values += [line[48 * k + 8 * j : 48 * k + 8 * j + 8, :] for j in range(6)]
    pack_tiles(message, 0, values)


def apply_kernel(
    sol, own_z, far_z, resid, c_x, c_down, c_up, c_z, c_face, h,
    out, applied, sums, field, pack, line,
):
    gz = lax.axis_index("gz")
    lane = lanes(ZROWS2)
    at_face = lax.rem(lane, 9) == jnp.where(gz == 0, 8, 0)
    shift = jnp.where(gz == 0, 7, 121)
    packed = far_z[...] + jnp.where(at_face, roll(own_z[...], shift, 1), 0.0)
    pack[...] = roll(packed, jnp.where(gz == 0, 120, 127), 1)
    toward = jnp.where(gz == 0, 127, 1)
    lane8 = lanes(8)
    folded = jnp.where(gz == 0, lane8 - 120, 7 - lane8) >= 0

    def tile(index):
        q, j = divmod(index, PER)
        return roll(pack[8 * q : 8 * q + 8, :], -9 * j, 1)

    for p in range(42):
        for t in range(5):
            at = p * EXT + 8 * t + 8
            field[at : at + 8, :] = sol[at : at + 8, :] + jnp.where(folded, tile(p * 5 + t), 0.0)
    for k, single in enumerate((7, 48)):
        for j in range(6):
            line[8 * j : 8 * j + 8, :] = jnp.where(folded, tile(210 + 6 * k + j), 0.0)
        at = pl.ds(single, 42, stride=EXT)
        field[at, :] = sol[at, :] + line[0:42, :]
    pack[...] = roll(pack[...], toward, 1)

    outer = jnp.where(lanes(C) == outer_lane(), 0.5, 0.0)
    flux_x = c_x[0:C, :] * (field[EXT + 8 : EXT + 48, :] - field[8:48, :])
    sum_a = jnp.zeros((8, CZ), F32)
    sum_b = jnp.zeros((8, CZ), F32)
    for x in range(C):
        at = (x + 1) * EXT
        to = pl.ds(x * C, C)
        z = field[at + 8 : at + 48, :]
        next_x = c_x[x * C + C : x * C + 2 * C, :] * (field[at + EXT + 8 : at + EXT + 48, :] - z)
        net = next_x - flux_x
        flux_x = next_x
        net = net + c_up[to, :] * (field[at + 9 : at + 49, :] - z)
        net = net - c_down[to, :] * (z - field[at + 7 : at + 47, :])
        flux_z = c_z[to, :] * (roll(z, -1, 1) - z)
        far = jnp.concatenate([tile((x + 1) * 5 + t) for t in range(5)], axis=0)
        net = net + (flux_z - roll(flux_z, 1, 1)) + c_face[to, :] * (far - z)
        image = mass_term * z - net + outer * h[to, :] * z
        out[to, :] = z
        applied[to, :] = image
        a, b = resid[to, :] * z, z * image
        for t in range(5):
            sum_a = sum_a + a[8 * t : 8 * t + 8]
            sum_b = sum_b + b[8 * t : 8 * t + 8]
    total_a = jnp.sum(sum_a, axis=0, keepdims=True)
    total_b = jnp.sum(sum_b, axis=0, keepdims=True)
    total_a = total_a + roll(total_a, CZ // 2, 1)
    total_b = total_b + roll(total_b, CZ // 2, 1)
    total = jnp.where(lanes(1) < CZ // 2, total_a, total_b)
    sums[...] = jnp.broadcast_to(total, sums.shape)


def gather_kernel(sums, out):
    out[...] = jnp.broadcast_to(jnp.sum(sums[...], axis=0, keepdims=True), out.shape)


def update_kernel(sums, guess, resid, field, applied, solution_out, resid_out):
    total = jnp.sum(sums[...], axis=0, keepdims=True)
    first = lanes(1) < CZ // 2
    above = jnp.sum(jnp.where(first, total, 0.0), axis=1, keepdims=True)
    below = jnp.sum(jnp.where(first, 0.0, total), axis=1, keepdims=True)
    step = above / below
    solution_out[...] = guess[...] + step * field[...]
    resid_out[...] = resid[...] - step * applied[...]


def on_device(gx, splits, right_side, guess_field, conduct_field):
    shape = right_side.shape
    b, v, h = (a.reshape(C * C, CZ) for a in (right_side, guess_field, conduct_field))
    n_gx, n_gy = lax.axis_size(gx), lax.axis_size("gy")
    at_x, at_y = lax.axis_index(gx), lax.axis_index("gy")
    flags = jnp.stack([at_x > 0, at_x < n_gx - 1, at_y > 0, at_y < n_gy - 1]).astype(F32)

    def exchange(axis, up, down):
        n = lax.axis_size(axis)
        forward = [(i, i + 1) for i in range(n - 1)]
        backward = [(i + 1, i) for i in range(n - 1)]
        return lax.ppermute(up, axis, forward), lax.ppermute(down, axis, backward)

    def swap(value):
        return lax.ppermute(value, "gz", [(0, 1), (1, 0)])

    plane, forward, inverse, denom, eigen = tables()
    own = C * C
    box = EXT * EXT

    def buffer(rows):
        return pltpu.VMEM((rows, CZ), F32)

    part, up, down, edge = call(
        residual_kernel, (own, YROWS, YROWS, 160), v, h, b,
        scratch=[buffer(own)] * 3 + [pltpu.SemaphoreType.DMA((3, CHUNKS))],
        hbm=(0, 1, 2), name="residual", work=2,
    )
    low, high = exchange("gy", up, down)
    (pairs,) = call(pairs_kernel, (own,), v, h, name="pairs", work=1)
    scale_a, scale_b = call(
        scale_kernel, (box, box), eigen, denom, smem=(0,), name="scale", work=2
    )
    part, right, left = call(
        extend_y_kernel, (C * EXT, XROWS, XROWS),
        flags, part, pairs, up, down, edge, low, high,
        smem=(0,), name="extend_y", work=1,
    )
    before, after = exchange(gx, right, left)
    ext, own_z = call(
        extend_x_kernel, (box, ZROWS),
        flags, part, pairs, low, high, right, left, before, after,
        smem=(0,), name="extend_x", work=1,
    )
    far_z = swap(own_z)
    (main,) = call(forward_kernel, (box,), plane, ext, scratch=[buffer(box)], name="forward", work=2)
    second_a, second_b, sides, side_strip, right, left = call(
        solve_kernel, (box, box, 18 * EXT, 18 * EXT, XROWS2, XROWS2),
        own_z, far_z, main, plane, forward, inverse, scale_a, scale_b,
        scratch=[buffer(box)], name="solve", work=6,
    )
    resid, c_x, c_down, c_up, c_z, c_face = call(
        own_kernel, (own, own + C, own, own, own, own),
        h, low, high, before, after, ext, own_z, far_z,
        scratch=[buffer(own + 2 * C)], name="own", work=2,
    )
    before, after = exchange(gx, right, left)
    sol, strip = call(
        rest_kernel, (38 * EXT, 38 * EXT), plane, inverse, second_a, second_b, name="rest", work=2
    )
    sol, strip, up, down = call(
        fold_x_kernel, (42 * EXT, 42 * EXT, YROWS2, YROWS2),
        flags, sides, side_strip, sol, strip, before, after,
        scratch=[buffer(48)], smem=(0,), name="fold_x", work=1,
    )
    low, high = exchange("gy", up, down)
    sol, own_z = call(
        fold_y_kernel, (42 * EXT, ZROWS2),
        flags, sol, strip, low, high,
        scratch=[buffer(42 * EXT), buffer(96)], smem=(0,), name="fold_y", work=1,
    )
    far_z = swap(own_z)
    first, last = splits
    field, applied, sums = call(
        apply_kernel, (own, own, lax.axis_size(first)),
        sol, own_z, far_z, resid, c_x, c_down, c_up, c_z, c_face, h,
        scratch=[buffer(42 * EXT), buffer(ZROWS2), buffer(48)], name="apply", work=3,
    )
    sums = lax.all_to_all(sums, first, 0, 0, tiled=True)
    (sums,) = call(gather_kernel, (lax.axis_size(last),), sums, name="gather")
    sums = lax.all_to_all(sums, last, 0, 0, tiled=True)
    out, resid = call(update_kernel, (own, own), sums, v, resid, field, applied, name="update", work=2)
    return out.reshape(shape), resid.reshape(shape)


def solution(mesh):
    n_gx, n_gy, n_gz = mesh.devices.shape
    if n_gx == 64:
        mesh = Mesh(mesh.devices.reshape(4, 8, 2, n_gy, n_gz), ("gx_x", "gx_y", "gx_c", "gy", "gz"))
        gx = ("gx_x", "gx_y", "gx_c")
        splits = (("gx_x", "gx_y"), ("gx_c", "gy", "gz"))
    else:
        gx = "gx"
        splits = (("gx",), ("gy", "gz"))
    placed = P(gx, "gy", "gz")
    return jax.shard_map(
        functools.partial(on_device, gx, splits),
        mesh=mesh,
        in_specs=(placed,) * 3,
        out_specs=(placed,) * 2,
        check_vma=False,
    )
```

time: 162 us -> 137 us (0.85)
  the two profiles are of different devices: /device:TPU:64 before, /device:TPU:1 now
where the time goes in v1:
time: 137 us
  waiting for transfers between devices  36.9 us (27%)
  blocking collectives  35.5 us (26%)
  starting transfers between devices  30.4 us (22%)
  Pallas kernels  29.3 us (21%)
  local copies, waits for them, and re-layouts  3.46 us (3%)
    ppermute x8, waiting for transfers between devices, exchange(): return (lax.ppermute(up, axis, forward), lax.ppermute(down, axis, backward))  32.4 us
    pallas_call x14, Pallas kernels, call(): pl.pallas_call(body, out_shape=[jax.ShapeDtypeStruct((rows, CZ), F32) for...  29.3 us
    ppermute x8, starting transfers between devices, exchange(): return (lax.ppermute(up, axis, forward), lax.ppermute(down, axis, backward))  26.6 us
    all_to_all x1, blocking collectives, on_device(): sums = lax.all_to_all(sums, first, 0, 0, tiled=True)  21.9 us
    all_to_all x1, blocking collectives, on_device(): sums = lax.all_to_all(sums, last, 0, 0, tiled=True)  13.6 us
    ppermute x2, waiting for transfers between devices, swap(): return lax.ppermute(value, 'gz', [(0, 1), (1, 0)])  4.57 us
    ppermute x2, starting transfers between devices, swap(): return lax.ppermute(value, 'gz', [(0, 1), (1, 0)])  3.84 us
    unnamed x20, local copies, waits for them, and re-layouts  3.46 us
  transfers between devices with their start and end apart: 10, of which 9 were waited for; matrix products, arithmetic and copies ran while one was open for 0% of the time, Pallas kernels for 4%

profile of v1, /device:TPU:1, one launch (start us, length us, event | category | flops | bytes accessed | tf_op | source)
XLA Modules:
  0.0 136.6 jit_solution(11019022242087736775)
XLA Ops:
  0.6 1.1 copy-done
  1.8 1.1 copy-done.1
  2.9 1.1 copy-done.3
  4.1 6.1 %residual.1 = (f32[1600,128]{1,0:T(8,128)S(1)}, f32[440,128]{1,0:T(8,128)S(1)}, f32[440,128]{1,0:T(8,128)S(1)}, f32[160,128]{1,0:T(8,128)S(1)}) custom-call(f32[1600,128]{1,0:T(8,128)S(1)} %bitcast.26, f32[1600,128]{1,0:T(8,128)S(1)} %bitcast.22, f32[1600,128]{1,0:T(8,128)S(1)} %bitcast.21), custom_call_target="tpu_custom_call" | custom-call | flops 2000000000 | bytes 4000000 | tf_op jit(solution)/shard_map/residual/pallas_call | solution.py:110
  10.2 6.6 %collective-permute-start = (f32[440,128]{1,0:T(8,128)S(1)}, f32[440,128]{1,0:T(8,128)S(1)}, u32[]{:S(2)}, u32[]{:S(2)}) collective-permute-start(f32[440,128]{1,0:T(8,128)S(1)} %get-tuple-element.39.up), channel_id=1, source_target_pairs={{0,2},{2,4},{4,6},{1,3},{3,5},{5,7},{8,10},{10,12},{12,14},{9,11},... | collective-permute-start | bytes 675848 | tf_op jit(solution)/shard_map/ppermute | solution.py:627
  16.8 1.3 collective-permute-start.1
  19.0 1.4 collective-permute-done.low
  20.4 13.3 %collective-permute-done.1.high = f32[440,128]{1,0:T(8,128)S(1)} collective-permute-done((f32[440,128]{1,0:T(8,128)S(1)}, f32[440,128]{1,0:T(8,128)S(1)}, u32[]{:S(2)}, u32[]{:S(2)}) %collective-permute-start.1) | collective-permute-done | bytes 225312 | tf_op jit(solution)/shard_map/ppermute | solution.py:627
  34.5 4.5 %collective-permute-start.2 = (f32[568,128]{1,0:T(8,128)S(1)}, f32[568,128]{1,0:T(8,128)S(1)}, u32[]{:S(2)}, u32[]{:S(2)}) collective-permute-start(f32[568,128]{1,0:T(8,128)S(1)} %get-tuple-element.43.right), channel_id=1, source_target_pairs={{0,8},{8,16},{16,24},{24,32},{32,40},{40,48},{48,56},{56,64},{64,7... | collective-permute-start | bytes 872456 | tf_op jit(solution)/shard_map/ppermute | solution.py:627
  39.0 1.9 %collective-permute-start.3 = (f32[568,128]{1,0:T(8,128)S(1)}, f32[568,128]{1,0:T(8,128)S(1)}, u32[]{:S(2)}, u32[]{:S(2)}) collective-permute-start(f32[568,128]{1,0:T(8,128)S(1)} %get-tuple-element.44.left), channel_id=1, source_target_pairs={{8,0},{16,8},{24,16},{32,24},{40,32},{48,40},{56,48},{64,56},{72,6... | collective-permute-start | bytes 872456 | tf_op jit(solution)/shard_map/ppermute | solution.py:627
  41.0 1.1 scale.1
  42.6 4.4 %collective-permute-done.3.after = f32[568,128]{1,0:T(8,128)S(1)} collective-permute-done((f32[568,128]{1,0:T(8,128)S(1)}, f32[568,128]{1,0:T(8,128)S(1)}, u32[]{:S(2)}, u32[]{:S(2)}) %collective-permute-start.3) | collective-permute-done | bytes 290848 | tf_op jit(solution)/shard_map/ppermute | solution.py:627
  47.0 2.9 %extend_x.1 = (f32[3136,128]{1,0:T(8,128)S(1)}, f32[280,128]{1,0:T(8,128)S(1)}) custom-call(f32[4]{0:T(128)S(1)} %add_convert_fusion.flags, f32[2240,128]{1,0:T(8,128)S(1)} %get-tuple-element.42.part, f32[1600,128]{1,0:T(8,128)S(1)} %pairs.1.vh, f32[440,128]{1,0:T(8,128)S(1)} %collective-permute-done.low, f32[440,128]{1,0:T(8,128)S(1)} %collective-permute-done.1.high, ...), custom_call_target="tpu_custom_call" | custom-call | flops 1000000000 | bytes 2000000 | tf_op jit(solution)/shard_map/extend_x/pallas_call | solution.py:110
  50.0 1.9 %collective-permute-start.4 = (f32[280,128]{1,0:T(8,128)S(1)}, f32[280,128]{1,0:T(8,128)S(1)}, u32[]{:S(2)}, u32[]{:S(2)}) collective-permute-start(f32[280,128]{1,0:T(8,128)S(1)} %get-tuple-element.45.own_z), channel_id=1, source_target_pairs={{0,1},{1,0},{2,3},{3,2},{4,5},{5,4},{6,7},{7,6},{8,9},{9,8},{10,11... | collective-permute-start | bytes 430088 | tf_op jit(solution)/shard_map/ppermute | solution.py:630
  51.9 1.5 %forward.2.main = f32[3136,128]{1,0:T(8,128)S(1)} custom-call(bf16[56,192]{1,0:T(8,128)(2,1)S(1)} %copy-done.8, f32[3136,128]{1,0:T(8,128)S(1)} %get-tuple-element.46.ext), custom_call_target="tpu_custom_call" | custom-call | flops 2000000000 | bytes 4000000 | tf_op jit(solution)/shard_map/forward/pallas_call | solution.py:110
  53.4 2.4 %collective-permute-done.4.far_z = f32[280,128]{1,0:T(8,128)S(1)} collective-permute-done((f32[280,128]{1,0:T(8,128)S(1)}, f32[280,128]{1,0:T(8,128)S(1)}, u32[]{:S(2)}, u32[]{:S(2)}) %collective-permute-start.4) | collective-permute-done | bytes 143392 | tf_op jit(solution)/shard_map/ppermute | solution.py:630
  55.8 7.2 %solve.1 = (f32[3136,128]{1,0:T(8,128)S(1)}, f32[3136,128]{1,0:T(8,128)S(1)}, f32[1008,128]{1,0:T(8,128)S(1)}, f32[1008,128]{1,0:T(8,128)S(1)}, f32[544,128]{1,0:T(8,128)S(1)}, /*index=5*/f32[544,128]{1,0:T(8,128)S(1)}) custom-call(f32[280,128]{1,0:T(8,128)S(1)} %get-tuple-element.45.own_z, f32[280,128]{1,0:T(8,128)S(1)} %collective-permute-done.4.far_z, ...), custom_call_target="tpu_custom_call" | custom-call | flops 6000000000 | bytes 12000000 | tf_op jit(solution)/shard_map/solve/pallas_call | solution.py:110
  63.0 3.6 %collective-permute-start.5 = (f32[544,128]{1,0:T(8,128)S(1)}, f32[544,128]{1,0:T(8,128)S(1)}, u32[]{:S(2)}, u32[]{:S(2)}) collective-permute-start(f32[544,128]{1,0:T(8,128)S(1)} %get-tuple-element.55), channel_id=1, source_target_pairs={{0,8},{8,16},{16,24},{24,32},{32,40},{40,48},{48,56},{56,64},{64,7... | collective-permute-start | bytes 835592 | tf_op jit(solution)/shard_map/ppermute | solution.py:627
  66.6 1.9 %collective-permute-start.6 = (f32[544,128]{1,0:T(8,128)S(1)}, f32[544,128]{1,0:T(8,128)S(1)}, u32[]{:S(2)}, u32[]{:S(2)}) collective-permute-start(f32[544,128]{1,0:T(8,128)S(1)} %get-tuple-element.56), channel_id=1, source_target_pairs={{8,0},{16,8},{24,16},{32,24},{40,32},{48,40},{56,48},{64,56},{72,6... | collective-permute-start | bytes 835592 | tf_op jit(solution)/shard_map/ppermute | solution.py:627
  68.5 1.7 %rest.1 = (f32[2128,128]{1,0:T(8,128)S(1)}, f32[2128,128]{1,0:T(8,128)S(1)}) custom-call(bf16[56,192]{1,0:T(8,128)(2,1)S(1)} %copy-done.8, bf16[2,768,256]{2,1,0:T(8,128)(2,1)S(1)} %copy-done.5, f32[3136,128]{1,0:T(8,128)S(1)} %get-tuple-element.51.second_a, f32[3136,128]{1,0:T(8,128)S(1)} %get-tuple-element.52.second_b), custom_call_target="tpu_custom_call" | custom-call | flops 2000000000 | bytes 4000000 | tf_op jit(solution)/shard_map/rest/pallas_call | solution.py:110
  70.3 4.2 %collective-permute-done.6.after = f32[544,128]{1,0:T(8,128)S(1)} collective-permute-done((f32[544,128]{1,0:T(8,128)S(1)}, f32[544,128]{1,0:T(8,128)S(1)}, u32[]{:S(2)}, u32[]{:S(2)}) %collective-permute-start.6) | collective-permute-done | bytes 278560 | tf_op jit(solution)/shard_map/ppermute | solution.py:627
  75.4 5.4 %collective-permute-start.7 = (f32[416,128]{1,0:T(8,128)S(1)}, f32[416,128]{1,0:T(8,128)S(1)}, u32[]{:S(2)}, u32[]{:S(2)}) collective-permute-start(f32[416,128]{1,0:T(8,128)S(1)} %get-tuple-element.59), channel_id=1, source_target_pairs={{0,2},{2,4},{4,6},{1,3},{3,5},{5,7},{8,10},{10,12},{12,14},{9,11},... | collective-permute-start | bytes 638984 | tf_op jit(solution)/shard_map/ppermute | solution.py:627
  80.9 1.3 collective-permute-start.8
  82.2 1.5 %collective-permute-done.7.low = f32[416,128]{1,0:T(8,128)S(1)} collective-permute-done((f32[416,128]{1,0:T(8,128)S(1)}, f32[416,128]{1,0:T(8,128)S(1)}, u32[]{:S(2)}, u32[]{:S(2)}) %collective-permute-start.7) | collective-permute-done | bytes 213024 | tf_op jit(solution)/shard_map/ppermute | solution.py:627
  83.7 7.0 %collective-permute-done.8.high = f32[416,128]{1,0:T(8,128)S(1)} collective-permute-done((f32[416,128]{1,0:T(8,128)S(1)}, f32[416,128]{1,0:T(8,128)S(1)}, u32[]{:S(2)}, u32[]{:S(2)}) %collective-permute-start.8) | collective-permute-done | bytes 213024 | tf_op jit(solution)/shard_map/ppermute | solution.py:627
  90.7 1.0 fold_y.1
  91.7 1.9 %collective-permute-start.9 = (f32[128,128]{1,0:T(8,128)S(1)}, f32[128,128]{1,0:T(8,128)S(1)}, u32[]{:S(2)}, u32[]{:S(2)}) collective-permute-start(f32[128,128]{1,0:T(8,128)S(1)} %get-tuple-element.62.own_z), channel_id=1, source_target_pairs={{0,1},{1,0},{2,3},{3,2},{4,5},{5,4},{6,7},{7,6},{8,9},{9,8},{10,11... | collective-permute-start | bytes 196616 | tf_op jit(solution)/shard_map/ppermute | solution.py:630
  94.5 2.2 %collective-permute-done.9.far_z = f32[128,128]{1,0:T(8,128)S(1)} collective-permute-done((f32[128,128]{1,0:T(8,128)S(1)}, f32[128,128]{1,0:T(8,128)S(1)}, u32[]{:S(2)}, u32[]{:S(2)}) %collective-permute-start.9) | collective-permute-done | bytes 65568 | tf_op jit(solution)/shard_map/ppermute | solution.py:630
  96.7 3.0 %apply.1 = (f32[1600,128]{1,0:T(8,128)S(1)}, f32[1600,128]{1,0:T(8,128)S(1)}, f32[32,128]{1,0:T(8,128)S(1)}) custom-call(f32[2352,128]{1,0:T(8,128)S(1)} %get-tuple-element.61.sol, f32[128,128]{1,0:T(8,128)S(1)} %get-tuple-element.62.own_z, f32[128,128]{1,0:T(8,128)S(1)} %collective-permute-done.9.far_z, f32[1600,128]{1,0:T(8,128)S(1)} %get-tuple-element.63.resid, ...), custom_call_target="tpu_custom_call" | custom-call | flops 3000000000 | bytes 6000000 | tf_op jit(solution)/shard_map/apply/pallas_call | solution.py:110
  99.7 21.9 %all_to_all.22 = f32[32,1,128]{2,1,0:T(1,128)S(1)} all-to-all(f32[32,1,128]{2,1,0:T(1,128)S(1)} %bitcast.19), channel_id=1, replica_groups=mesh['gx_x'=4,'gx_y'=8,'gx_c'=2,'gy'=4,'gz'=2] {'gx_x','gx_y'}, dimensions={0} | all-to-all | bytes 32768 | tf_op jit(solution)/shard_map/all_to_all | solution.py:694
  121.6 13.6 %all_to_all.23 = f32[16,1,128]{2,1,0:T(1,128)S(1)} all-to-all(f32[16,1,128]{2,1,0:T(1,128)S(1)} %bitcast.18), channel_id=1, replica_groups=mesh['gx_x'=4,'gx_y'=8,'gx_c'=2,'gy'=4,'gz'=2] {'gx_c','gy','gz'}, dimensions={0} | all-to-all | bytes 16384 | tf_op jit(solution)/shard_map/all_to_all | solution.py:696
  135.2 1.4 %update.1 = (f32[1600,128]{1,0:T(8,128)}, f32[1600,128]{1,0:T(8,128)}) custom-call(f32[16,128]{1,0:T(8,128)S(1)} %bitcast.20, f32[1600,128]{1,0:T(8,128)S(1)} %bitcast.28, f32[1600,128]{1,0:T(8,128)S(1)} %get-tuple-element.63.resid, f32[1600,128]{1,0:T(8,128)S(1)} %get-tuple-element.70.field, f32[1600,128]{1,0:T(8,128)S(1)} %get-tuple-element.71.applied), custom_call_target="tpu_custom_call" | custom-call | flops 2000000000 | bytes 4000000 | tf_op jit(solution)/shard_map/update/pallas_call | solution.py:110
  (25 shorter events, 4.0 us)
Async XLA Ops:
  0.6 1.1 copy-start
  1.8 1.1 copy-start.1
  2.9 1.1 copy-start.3
  4.1 14.1 %copy-start.2 = (f32[40,40,128]{2,1,0:T(8,128)S(1)}, f32[40,40,128]{2,1,0:T(8,128)}, u32[]{:S(2)}) copy-start(f32[40,40,128]{2,1,0:T(8,128)} %param.10) | copy-start | bytes 2457604
  4.1 14.1 %copy-start.4 = (f32[40,40,128]{2,1,0:T(8,128)S(1)}, f32[40,40,128]{2,1,0:T(8,128)}, u32[]{:S(2)}) copy-start(f32[40,40,128]{2,1,0:T(8,128)} %param.9) | copy-start | bytes 2457604
  10.2 10.2 %collective-permute-start = (f32[440,128]{1,0:T(8,128)S(1)}, f32[440,128]{1,0:T(8,128)S(1)}, u32[]{:S(2)}, u32[]{:S(2)}) collective-permute-start(f32[440,128]{1,0:T(8,128)S(1)} %get-tuple-element.39.up), channel_id=1, source_target_pairs={{0,2},{2,4},{4,6},{1,3},{3,5},{5,7},{8,10},{10,12},{12,14},{9,11},... | collective-permute-start | bytes 675848 | tf_op jit(solution)/shard_map/ppermute | solution.py:627
  16.8 16.9 %collective-permute-start.1 = (f32[440,128]{1,0:T(8,128)S(1)}, f32[440,128]{1,0:T(8,128)S(1)}, u32[]{:S(2)}, u32[]{:S(2)}) collective-permute-start(f32[440,128]{1,0:T(8,128)S(1)} %get-tuple-element.40.down), channel_id=1, source_target_pairs={{2,0},{4,2},{6,4},{3,1},{5,3},{7,5},{10,8},{12,10},{14,12},{11,9},... | collective-permute-start | bytes 675848 | tf_op jit(solution)/shard_map/ppermute | solution.py:627
  33.7 7.3 %copy-start.7 = (f32[56,256]{1,0:T(8,128)S(1)}, f32[56,256]{1,0:T(8,128)}, u32[]{:S(2)}) copy-start(f32[56,256]{1,0:T(8,128)} %constant.38.clone.denom) | copy-start | bytes 172036
  33.7 7.3 %copy-start.9 = (f32[56]{0:T(128)S(1)}, f32[56]{0:T(128)}, u32[]{:S(2)}) copy-start(f32[56]{0:T(128)} %constant.37.clone.eigen) | copy-start | bytes 676
  34.5 8.1 %collective-permute-start.2 = (f32[568,128]{1,0:T(8,128)S(1)}, f32[568,128]{1,0:T(8,128)S(1)}, u32[]{:S(2)}, u32[]{:S(2)}) collective-permute-start(f32[568,128]{1,0:T(8,128)S(1)} %get-tuple-element.43.right), channel_id=1, source_target_pairs={{0,8},{8,16},{16,24},{24,32},{32,40},{40,48},{48,56},{56,64},{64,7... | collective-permute-start | bytes 872456 | tf_op jit(solution)/shard_map/ppermute | solution.py:627
  39.0 8.0 %collective-permute-start.3 = (f32[568,128]{1,0:T(8,128)S(1)}, f32[568,128]{1,0:T(8,128)S(1)}, u32[]{:S(2)}, u32[]{:S(2)}) collective-permute-start(f32[568,128]{1,0:T(8,128)S(1)} %get-tuple-element.44.left), channel_id=1, source_target_pairs={{8,0},{16,8},{24,16},{32,24},{40,32},{48,40},{56,48},{64,56},{72,6... | collective-permute-start | bytes 872456 | tf_op jit(solution)/shard_map/ppermute | solution.py:627
  47.0 4.9 %copy-start.8 = (bf16[56,192]{1,0:T(8,128)(2,1)S(1)}, bf16[56,192]{1,0:T(8,128)(2,1)}, u32[]{:S(2)}) copy-start(bf16[56,192]{1,0:T(8,128)(2,1)} %constant.39.clone.plane) | copy-start | bytes 64516
  50.0 5.8 %collective-permute-start.4 = (f32[280,128]{1,0:T(8,128)S(1)}, f32[280,128]{1,0:T(8,128)S(1)}, u32[]{:S(2)}, u32[]{:S(2)}) collective-permute-start(f32[280,128]{1,0:T(8,128)S(1)} %get-tuple-element.45.own_z), channel_id=1, source_target_pairs={{0,1},{1,0},{2,3},{3,2},{4,5},{5,4},{6,7},{7,6},{8,9},{9,8},{10,11... | collective-permute-start | bytes 430088 | tf_op jit(solution)/shard_map/ppermute | solution.py:630
  51.9 3.9 %copy-start.5 = (bf16[2,768,256]{2,1,0:T(8,128)(2,1)S(1)}, bf16[2,768,256]{2,1,0:T(8,128)(2,1)}, u32[]{:S(2)}) copy-start(bf16[2,768,256]{2,1,0:T(8,128)(2,1)} %constant.41.clone.inverse) | copy-start | bytes 2359300
  51.9 3.9 %copy-start.6 = (bf16[2,768,256]{2,1,0:T(8,128)(2,1)S(1)}, bf16[2,768,256]{2,1,0:T(8,128)(2,1)}, u32[]{:S(2)}) copy-start(bf16[2,768,256]{2,1,0:T(8,128)(2,1)} %constant.40.clone.forward) | copy-start | bytes 2359300
  63.0 7.2 %collective-permute-start.5 = (f32[544,128]{1,0:T(8,128)S(1)}, f32[544,128]{1,0:T(8,128)S(1)}, u32[]{:S(2)}, u32[]{:S(2)}) collective-permute-start(f32[544,128]{1,0:T(8,128)S(1)} %get-tuple-element.55), channel_id=1, source_target_pairs={{0,8},{8,16},{16,24},{24,32},{32,40},{40,48},{48,56},{56,64},{64,7... | collective-permute-start | bytes 835592 | tf_op jit(solution)/shard_map/ppermute | solution.py:627
  66.6 7.9 %collective-permute-start.6 = (f32[544,128]{1,0:T(8,128)S(1)}, f32[544,128]{1,0:T(8,128)S(1)}, u32[]{:S(2)}, u32[]{:S(2)}) collective-permute-start(f32[544,128]{1,0:T(8,128)S(1)} %get-tuple-element.56), channel_id=1, source_target_pairs={{8,0},{16,8},{24,16},{32,24},{40,32},{48,40},{56,48},{64,56},{72,6... | collective-permute-start | bytes 835592 | tf_op jit(solution)/shard_map/ppermute | solution.py:627
  75.4 8.2 %collective-permute-start.7 = (f32[416,128]{1,0:T(8,128)S(1)}, f32[416,128]{1,0:T(8,128)S(1)}, u32[]{:S(2)}, u32[]{:S(2)}) collective-permute-start(f32[416,128]{1,0:T(8,128)S(1)} %get-tuple-element.59), channel_id=1, source_target_pairs={{0,2},{2,4},{4,6},{1,3},{3,5},{5,7},{8,10},{10,12},{12,14},{9,11},... | collective-permute-start | bytes 638984 | tf_op jit(solution)/shard_map/ppermute | solution.py:627
  80.9 9.9 %collective-permute-start.8 = (f32[416,128]{1,0:T(8,128)S(1)}, f32[416,128]{1,0:T(8,128)S(1)}, u32[]{:S(2)}, u32[]{:S(2)}) collective-permute-start(f32[416,128]{1,0:T(8,128)S(1)} %get-tuple-element.60), channel_id=1, source_target_pairs={{2,0},{4,2},{6,4},{3,1},{5,3},{7,5},{10,8},{12,10},{14,12},{11,9},... | collective-permute-start | bytes 638984 | tf_op jit(solution)/shard_map/ppermute | solution.py:627
  91.7 5.0 %collective-permute-start.9 = (f32[128,128]{1,0:T(8,128)S(1)}, f32[128,128]{1,0:T(8,128)S(1)}, u32[]{:S(2)}, u32[]{:S(2)}) collective-permute-start(f32[128,128]{1,0:T(8,128)S(1)} %get-tuple-element.62.own_z), channel_id=1, source_target_pairs={{0,1},{1,0},{2,3},{3,2},{4,5},{5,4},{6,7},{7,6},{8,9},{9,8},{10,11... | collective-permute-start | bytes 196616 | tf_op jit(solution)/shard_map/ppermute | solution.py:630

commit v2 on v1

--- a/solution.py
+++ b/solution.py
@@ -26,7 +26,7 @@
 HBM = pl.BlockSpec(memory_space=pltpu.HBM)
 
 YROWS = 440
-XROWS = 568
+XROWS = 616
 PER_Z = 12
 BLOCKS_Z = -(-EXT // PER_Z)
 ZROWS = BLOCKS_Z * EXT
@@ -105,13 +105,14 @@
     return rows_at(index * 8, 8)
 
 
-def call(body, out_rows, *args, scratch=(), limit=16, name=None, smem=(), hbm=(), work=0):
+def call(body, out_rows, *args, scratch=(), limit=16, name=None, smem=(), hbm=(), hbm_out=(), alias=(), work=0):
     place = {**{i: SMEM for i in smem}, **{i: HBM for i in hbm}}
     return pl.pallas_call(
         body,
         out_shape=[jax.ShapeDtypeStruct((rows, CZ), F32) for rows in out_rows],
         in_specs=[place.get(i, VMEM) for i in range(len(args))],
-        out_specs=[VMEM] * len(out_rows),
+        out_specs=[HBM if i in hbm_out else VMEM for i in range(len(out_rows))],
+        input_output_aliases=dict(alias),
         scratch_shapes=list(scratch),
         compiler_params=pltpu.CompilerParams(vmem_limit_bytes=limit * 2**20),
         cost_estimate=pl.CostEstimate(
@@ -144,9 +145,10 @@
     )
 
 
-def residual_kernel(v_in, h_in, b_in, part, up, down, edge, v, h, b, sems):
+def residual_kernel(v_in, h_in, b_in, part_out, up, down, edge, part, v, h, b, sems):
     base, face = strip_base(), face_lane()
-    size = C * C // CHUNKS
+    planes = C // CHUNKS
+    size = planes * C
     copies = []
     for c in range(CHUNKS):
         at = pl.ds(c * size, size)
@@ -158,40 +160,45 @@
     y_half = jnp.where(row > 0, 0.5, 0.0)
     z_half = jnp.where(lane < CZ - 1, 0.5, 0.0)
     outer = jnp.where(lane == outer_lane(), 0.5, 0.0)
-    flux_x = jnp.zeros((C, CZ), F32)
-    pack_up = jnp.zeros((8, CZ), F32)
-    pack_down = jnp.zeros((8, CZ), F32)
-    waited = 0
-    for x in range(C):
-        need = min((x + 1) // 8 + 1, CHUNKS)
-        while waited < need:
-            for k in range(3):
-                copies[3 * waited + k].wait()
-            waited += 1
-        vi, hi = v[x * C : x * C + C, :], h[x * C : x * C + C, :]
+
+    def visit(x, carry):
+        flux_x, pack_up, pack_down = carry
+        own = rows_at(x * C, C)
+        following = rows_at(jnp.minimum(x + 1, C - 1) * C, C)
+        vi, hi = v[own, :], h[own, :]
+        next_x = 0.5 * (hi + h[following, :]) * (v[following, :] - vi)
         flux_y = y_half * (hi + roll(hi, 1, 0)) * (vi - roll(vi, 1, 0))
         flux_z = z_half * (hi + roll(hi, -1, 1)) * (roll(vi, -1, 1) - vi)
         applied = (
             mass_term * vi
+            - (next_x - flux_x)
             - (roll(flux_y, -1, 0) - flux_y)
             - (flux_z - roll(flux_z, 1, 1))
             + outer * hi * vi
         )
-        if x < C - 1:
-            to = pl.ds((x + 1) * C, C)
-            next_x = 0.5 * (hi + h[to, :]) * (v[to, :] - vi)
-            applied = applied - (next_x - flux_x)
-            flux_x = next_x
-        else:
-            applied = applied + flux_x
-        resid = b[x * C : x * C + C, :] - applied
-        part[x * C : x * C + C, :] = resid
-        down[8 * x : 8 * x + 8, :] = resid[0:8]
-        up[8 * x : 8 * x + 8, :] = resid[32:40]
-        pack_up = pack_up + roll(pair_of(vi[32:40], hi[32:40], lane8, base, face), 2 * x, 1)
-        pack_down = pack_down + roll(pair_of(vi[0:8], hi[0:8], lane8, base, face), 2 * x, 1)
-    up[432:440, :] = roll(pack_up, -base, 1)
-    down[432:440, :] = roll(pack_down, -base, 1)
+        resid = b[own, :] - applied
+        part[own, :] = resid
+        down[tile_at(x), :] = resid[0:8]
+        up[tile_at(x), :] = resid[32:40]
+        pair = pair_of(vi[32:40], hi[32:40], lane8, base, face)
+        pack_up = pack_up + roll(pair, 2 * x - base, 1)
+        pair = pair_of(vi[0:8], hi[0:8], lane8, base, face)
+        pack_down = pack_down + roll(pair, 2 * x - base, 1)
+        return next_x, pack_up, pack_down
+
+    carry = (jnp.zeros((C, CZ), F32), jnp.zeros((8, CZ), F32), jnp.zeros((8, CZ), F32))
+    for k in range(3):
+        copies[k].wait()
+    for c in range(CHUNKS):
+        if c < CHUNKS - 1:
+            for k in range(3):
+                copies[3 * (c + 1) + k].wait()
+        carry = lax.fori_loop(c * planes, (c + 1) * planes, visit, carry, unroll=4)
+        at = pl.ds(c * size, size)
+        copies.append(pltpu.make_async_copy(part.at[at, :], part_out.at[at, :], sems.at[3, c]))
+        copies[-1].start()
+    up[432:440, :] = carry[1]
+    down[432:440, :] = carry[2]
     last = (C - 1) * C
     for message, first in ((up, 32), (down, 0)):
         face_row = C - 1 if first else 0
@@ -205,21 +212,21 @@
     edge[40:80, :] = h[0:40, :]
     edge[80:120, :] = v[last : last + 40, :]
     edge[120:160, :] = h[last : last + 40, :]
-
-
-def pairs_kernel(v, h, out):
+    for copy in copies[-CHUNKS:]:
+        copy.wait()
+
+
+def prepare_kernel(eigen, v, h, denom, out, out_a, out_b):
     base, face = strip_base(), face_lane()
     lane = lanes(C)
 
-    def visit(x, _):
+    def visit_pair(x, _):
         at = rows_at(x * C, C)
         out[at, :] = pair_of(v[at, :], h[at, :], lane, base, face)
         return 0
 
-    lax.fori_loop(0, C, visit, 0, unroll=8)
-
-
-def scale_kernel(eigen, denom, out_a, out_b):
+    lax.fori_loop(0, C, visit_pair, 0, unroll=8)
+
     def visit(y, _):
         value = 1.0 / (denom[...] + eigen[y])
         at = rows_at(y * EXT, EXT)
@@ -230,82 +237,119 @@
     lax.fori_loop(0, EXT, visit, 0, unroll=4)
 
 
+def choose(flag, a, b):
+    return jnp.where(flag > 0.5, a, b)
+
+
+def by_parity(flags, first, second):
+    def before(start, stop):
+        return choose(flags[4], second[start:stop, :], first[start:stop, :])
+
+    def after(start, stop):
+        return choose(flags[4], first[start:stop, :], second[start:stop, :])
+
+    return before, after
+
+
 def pick(pack, index, to):
     pair = lax.div(lanes(8), 2) == index
     return roll(jnp.where(pair, pack, 0.0), to - 2 * index, 1)
 
 
-def extend_y_kernel(flags, part, vh, up, down, edge, low, high, out, right, left):
-    base = strip_base()
-    for x in range(C):
-        out[x * EXT : x * EXT + 8, :] = low[8 * x : 8 * x + 8, :]
-        out[x * EXT + 8 : x * EXT + 48, :] = part[x * C : x * C + C, :]
-        out[x * EXT + 48 : x * EXT + 56, :] = high[8 * x : 8 * x + 8, :]
+def strip_mask():
+    lane = lanes(8)
+    return jnp.where(lax.axis_index("gz") == 0, lane - 120, 7 - lane) >= 0
+
+
+def extend_y_kernel(flags, part, vh, up, down, edge, low, high, out, first, second, faces, right, left):
+    base, strip_lanes = strip_base(), strip_mask()
+
+    def visit(x, _):
+        out[rows_at(x * EXT, 8), :] = low[tile_at(x), :]
+        out[rows_at(x * EXT + 8, C), :] = part[rows_at(x * C, C), :]
+        out[rows_at(x * EXT + 48, 8), :] = high[tile_at(x), :]
+        return 0
+
+    lax.fori_loop(0, C, visit, 0, unroll=8)
     flux = 0.5 * (low[360:400, :] + down[360:400, :]) * (down[320:360, :] - low[320:360, :])
     out[pl.ds(8, C, stride=EXT), :] = out[pl.ds(8, C, stride=EXT), :] - flux
     out[pl.ds(7, C, stride=EXT), :] = out[pl.ds(7, C, stride=EXT), :] + flux * flags[2]
     flux = 0.5 * (up[360:400, :] + high[360:400, :]) * (high[320:360, :] - up[320:360, :])
     out[pl.ds(47, C, stride=EXT), :] = out[pl.ds(47, C, stride=EXT), :] + flux
     out[pl.ds(48, C, stride=EXT), :] = out[pl.ds(48, C, stride=EXT), :] - flux * flags[3]
-    for message, first, strip, own in ((left, 0, 400, 0), (right, 32, 416, 80)):
-        message[0:448, :] = out[first * EXT : first * EXT + 448, :]
+    for message, start, strip, own in ((left, 0, 400, 0), (right, 32, 416, 80)):
+        message[0:448, :] = out[start * EXT : start * EXT + 448, :]
         for k in range(2):
             at = 448 + k * EXT
             message[at : at + 8, :] = low[strip + 8 * k : strip + 8 * k + 8, :]
             message[at + 8 : at + 48, :] = edge[own + 40 * k : own + 40 * k + 40, :]
             message[at + 48 : at + 56, :] = high[strip + 8 * k : strip + 8 * k + 8, :]
-        near = jnp.zeros((8, CZ), F32)
-        taken = jnp.zeros((8, CZ), F32)
-        for i in range(OVER):
-            x = first + i
-            for t in range(5):
-                at = x * C + 8 * t
-                near = near + roll(vh[at : at + 8, :], 2 * (i * TILES + 1 + t), 1)
-            taken = taken + pick(low[432:440, :], x, 2 * i * TILES)
-            taken = taken + pick(high[432:440, :], x, 2 * (i * TILES + 6))
-        message[560:568, :] = roll(near, -base, 1) + taken
-
-
-def extend_x_kernel(flags, part, vh, low, high, right, left, before, after, out, message):
-    base = strip_base()
-    gz = lax.axis_index("gz")
-    lane = lanes(8)
-    strip_lanes = jnp.where(gz == 0, lane - 120, 7 - lane) >= 0
-    side = OVER * EXT
-    out[0:side, :] = before[0:side, :]
-    out[side : side + C * EXT, :] = part[...]
-    out[side + C * EXT : EXT * EXT, :] = after[0:side, :]
-    flux = 0.5 * (before[504:560, :] + left[504:560, :]) * (left[448:504, :] - before[448:504, :])
-    at = OVER * EXT
-    out[at : at + EXT, :] = out[at : at + EXT, :] - flux
-    out[at - EXT : at, :] = out[at - EXT : at, :] + flux * flags[0]
-    flux = 0.5 * (right[504:560, :] + after[504:560, :]) * (after[448:504, :] - right[448:504, :])
-    at = (OVER + C) * EXT
-    out[at - EXT : at, :] = out[at - EXT : at, :] + flux
-    out[at : at + EXT, :] = out[at : at + EXT, :] - flux * flags[1]
+        for t in range(TILES):
+            near = jnp.zeros((8, CZ), F32)
+            taken = jnp.zeros((8, CZ), F32)
+            for i in range(OVER):
+                x = start + i
+                value = jnp.where(strip_lanes, out[x * EXT + 8 * t : x * EXT + 8 * t + 8, :], 0.0)
+                if t == 0:
+                    taken = taken + pick(low[432:440, :], x, 10 * i)
+                elif t == 6:
+                    taken = taken + pick(high[432:440, :], x, 10 * i)
+                else:
+                    value = value + vh[x * C + 8 * t - 8 : x * C + 8 * t, :]
+                near = near + roll(value, 10 * i, 1)
+            message[560 + 8 * t : 568 + 8 * t, :] = roll(near, -base, 1) + taken
+    faces[0:112, :] = left[448:560, :]
+    faces[112:224, :] = right[448:560, :]
+    first[...] = choose(flags[4], right[...], left[...])
+    second[...] = choose(flags[4], left[...], right[...])
+
+
+def pack_z_kernel(part, vh, low, high, message):
+    base, strip_lanes = strip_base(), strip_mask()
     for q in range(BLOCKS_Z):
         for t in range(TILES):
             near = jnp.zeros((8, CZ), F32)
             taken = jnp.zeros((8, CZ), F32)
-            for j in range(min(PER_Z, EXT - q * PER_Z)):
-                x = q * PER_Z + j
-                own = x - OVER
-                at = x * EXT + 8 * t
-                value = jnp.where(strip_lanes, out[at : at + 8, :], 0.0)
-                if own < 0:
-                    taken = taken + pick(before[560:568, :], x * TILES + t, 10 * j)
-                elif own >= C:
-                    taken = taken + pick(after[560:568, :], (own - C) * TILES + t, 10 * j)
-                elif t == 0:
-                    taken = taken + pick(low[432:440, :], own, 10 * j)
+            for j in range(PER_Z):
+                x = q * PER_Z + j - OVER
+                if not 0 <= x < C:
+                    continue
+                value = jnp.where(strip_lanes, part[x * EXT + 8 * t : x * EXT + 8 * t + 8, :], 0.0)
+                if t == 0:
+                    taken = taken + pick(low[432:440, :], x, 10 * j)
                 elif t == 6:
-                    taken = taken + pick(high[432:440, :], own, 10 * j)
+                    taken = taken + pick(high[432:440, :], x, 10 * j)
                 else:
-                    start = own * C + 8 * (t - 1)
-                    value = value + vh[start : start + 8, :]
+                    value = value + vh[x * C + 8 * t - 8 : x * C + 8 * t, :]
                 near = near + roll(value, 10 * j, 1)
             at = q * EXT + 8 * t
             message[at : at + 8, :] = roll(near, -base, 1) + taken
+
+
+def extend_x_kernel(flags, packed, faces, first, second, inner, message, fluxes):
+    base, strip_lanes = strip_base(), strip_mask()
+    before, after = by_parity(flags, first, second)
+    flux_a = 0.5 * (before(504, 560) + faces[56:112, :]) * (faces[0:56, :] - before(448, 504))
+    flux_b = 0.5 * (faces[168:224, :] + after(504, 560)) * (after(448, 504) - faces[112:168, :])
+    fluxes[0:EXT, :] = flux_a
+    fluxes[EXT : 2 * EXT, :] = flux_b
+    message[...] = packed[...]
+    end = (BLOCKS_Z - 1) * EXT
+    message[0:EXT, :] = message[0:EXT, :] + before(560, 616)
+    message[end : end + EXT, :] = message[end : end + EXT, :] + after(560, 616)
+
+    def add(x, t, value):
+        q, j = divmod(x, PER_Z)
+        at = q * EXT + 8 * t
+        message[at : at + 8, :] = message[at : at + 8, :] + roll(value, 10 * j, 1)
+
+    for t in range(TILES):
+        a = roll(jnp.where(strip_lanes, flux_a[8 * t : 8 * t + 8], 0.0), -base, 1)
+        b = roll(jnp.where(strip_lanes, flux_b[8 * t : 8 * t + 8], 0.0), -base, 1)
+        add(OVER - 1, t, a * flags[0])
+        add(OVER, t, -a)
+        add(OVER + C - 1, t, b)
+        add(OVER + C, t, -b * flags[1])
 
 
 def halves(value):
@@ -332,19 +376,31 @@
     return jnp.concatenate([a, b], axis=1)
 
 
-def forward_kernel(plane, ext, out, first):
+def inner_kernel(plane, part, out):
     table = plane[...]
-
-    def visit_y(c, _):
-        for i in range(14):
-            x = 2 * (c * 14 + i)
-            at, then = rows_at(x * EXT, EXT), rows_at((x + 1) * EXT, EXT)
-            value = along_rows(table, beside(ext[at, :], ext[then, :]))
-            first[at, :] = value[:, :CZ]
-            first[then, :] = value[:, CZ:]
-        return 0
-
-    lax.fori_loop(0, 2, visit_y, 0)
+    for x in range(1, C - 1, 2):
+        at, then = pl.ds(x * EXT, EXT), pl.ds((x + 1) * EXT, EXT)
+        value = along_rows(table, beside(part[at, :], part[then, :]))
+        out[(x - 1) * EXT : x * EXT, :] = value[:, :CZ]
+        out[x * EXT : (x + 1) * EXT, :] = value[:, CZ:]
+
+
+def forward_kernel(flags, plane, part, inner, fluxes, one, two, out, first):
+    before, after = by_parity(flags, one, two)
+    table = plane[...]
+    flux_a, flux_b = fluxes[0:EXT, :], fluxes[EXT : 2 * EXT, :]
+    planes = {x: before(x * EXT, (x + 1) * EXT) for x in range(OVER)}
+    planes[7] = planes[7] + flux_a * flags[0]
+    planes[8] = part[0:EXT, :] - flux_a
+    planes[47] = part[(C - 1) * EXT : C * EXT, :] + flux_b
+    planes.update({48 + x: after(x * EXT, (x + 1) * EXT) for x in range(OVER)})
+    planes[48] = planes[48] - flux_b * flags[1]
+    first[9 * EXT : 47 * EXT, :] = inner[...]
+    order = sorted(planes)
+    for x, then in zip(order[0::2], order[1::2]):
+        value = along_rows(table, beside(planes[x], planes[then]))
+        first[x * EXT : (x + 1) * EXT, :] = value[:, :CZ]
+        first[then * EXT : (then + 1) * EXT, :] = value[:, CZ:]
 
     def visit_x(c, _):
         for i in range(14):
@@ -364,12 +420,12 @@
     return half, half * (far_z[...] - own_z[...])
 
 
-STEP = 8
+STEP = 28
 
 
 def solve_kernel(
-    own_z, far_z, main, plane, forward, inverse, scale_a, scale_b,
-    second_a, second_b, sol, strip, right, left, halo,
+    flags, own_z, far_z, main, plane, forward, inverse, scale_a, scale_b,
+    second_a, second_b, sol, strip, first, second, halo, right, left,
 ):
     gz = lax.axis_index("gz")
     table = plane[...]
@@ -413,6 +469,8 @@
         message[0 : 9 * EXT, :] = sol[9 * k * EXT : 9 * (k + 1) * EXT, :]
         tiles = [strip[pl.ds((9 * k * TILES + j) * 8, 8), :] for j in range(63)]
         pack_tiles(message, 9 * EXT, tiles)
+    first[...] = choose(flags[4], right[...], left[...])
+    second[...] = choose(flags[4], left[...], right[...])
 
 
 def inverse_planes(table, inverse_table, second_a, second_b, sol, strip, planes, to):
@@ -426,15 +484,18 @@
     strip[at, :] = value[:, CZ:]
 
 
-def rest_kernel(plane, inverse, second_a, second_b, sol, strip):
+def rest_kernel(plane, inverse, second_a, second_b, sides, side_strip, sol, strip):
     table, inverse_table = plane[...], inverse[lax.axis_index("gz")]
     for first, last in ((9, 19), (19, 29), (29, 38), (38, 47)):
         inverse_planes(
-            table, inverse_table, second_a, second_b, sol, strip, range(first, last), first - 9
+            table, inverse_table, second_a, second_b, sol, strip, range(first, last), first - 7
         )
-
-
-def own_kernel(h, low, high, before, after, ext, own_z, far_z, resid, c_x, c_down, c_up, c_z, c_face, cond):
+    for target, source in ((sol, sides), (strip, side_strip)):
+        target[0 : 2 * EXT, :] = source[7 * EXT : 9 * EXT, :]
+        target[40 * EXT : 42 * EXT, :] = source[9 * EXT : 11 * EXT, :]
+
+
+def own_kernel(flags, h, low, high, one, two, part, fluxes, own_z, far_z, resid, c_x, c_down, c_up, c_z, c_face, cond):
     face, outer = face_lane(), outer_lane()
     half, flux = face_terms(own_z, far_z)
     half, flux = roll(half, face, 1), roll(flux, face, 1)
@@ -444,15 +505,20 @@
         for t in range(5):
             at = q * EXT + 8 * (t + 1)
             to = x * C + 8 * t
-            source = (x + OVER) * EXT + 8 * (t + 1)
+            source = x * EXT + 8 * (t + 1)
             moved = jnp.where(lane8 == face, roll(flux[at : at + 8], -10 * j, 1), 0.0)
-            resid[to : to + 8, :] = ext[source : source + 8, :] + moved
+            if x == 0:
+                moved = moved - fluxes[source : source + 8, :]
+            elif x == C - 1:
+                moved = moved + fluxes[source + EXT - x * EXT : source + EXT - x * EXT + 8, :]
+            resid[to : to + 8, :] = part[source : source + 8, :] + moved
             c_face[to : to + 8, :] = jnp.where(
                 lane8 == face, roll(half[at : at + 8], -10 * j, 1), 0.0
             )
-    cond[0:C, :] = before[512:552, :]
+    before, after = by_parity(flags, one, two)
+    cond[0:C, :] = before(512, 552)
     cond[C : C + C * C, :] = h[...]
-    cond[C + C * C :, :] = after[512:552, :]
+    cond[C + C * C :, :] = after(512, 552)
     z_half = jnp.where(lanes(C) < CZ - 1, 0.5, 0.0)
     row = lax.broadcasted_iota(jnp.int32, (C, CZ), 0)
     for x in range(C):
@@ -480,20 +546,19 @@
     return roll(message[rows_at(at + 8 * q, 8), :], -9 * (index - q * PER), 1)
 
 
-def fold_x_kernel(flags, sides, side_strip, sol, strip, before, after, out, out_strip, up, down, line):
+def fold_x_kernel(flags, sol, strip, one, two, out, out_strip, up, down, line):
     size = 42 * EXT
     narrow = lanes(8) < 9
-    for target, outside, inside in ((out, sides, sol), (out_strip, side_strip, strip)):
-        target[0 : 2 * EXT, :] = outside[7 * EXT : 9 * EXT, :]
-        target[2 * EXT : 40 * EXT, :] = inside[...]
-        target[40 * EXT : size, :] = outside[9 * EXT : 11 * EXT, :]
-    out[0 : 9 * EXT, :] = out[0 : 9 * EXT, :] + before[0 : 9 * EXT, :]
+    before, after = by_parity(flags, one, two)
+    out[0 : 9 * EXT, :] = out[0 : 9 * EXT, :] + before(0, 9 * EXT)
     tail = 33 * EXT
-    out[tail:size, :] = out[tail:size, :] + after[0 : 9 * EXT, :]
+    out[tail:size, :] = out[tail:size, :] + after(0, 9 * EXT)
+    packs = [side(9 * EXT, XROWS2) for side in (before, after)]
 
     for j in range(63):
-        for message, at in ((before, 8 * j), (after, tail + 8 * j)):
-            value = jnp.where(narrow, unpack_tile(message, 9 * EXT, j), 0.0)
+        q, i = divmod(j, PER)
+        for pack, at in ((packs[0], 8 * j), (packs[1], tail + 8 * j)):
+            value = jnp.where(narrow, roll(pack[8 * q : 8 * q + 8], -9 * i, 1), 0.0)
             out_strip[at : at + 8, :] = out_strip[at : at + 8, :] + value
 
     for array in (out, out_strip):
@@ -512,10 +577,8 @@
         pack_tiles(message, 384, values)
 
 
-def fold_y_kernel(flags, sol, strip, low, high, out, message, work, line):
+def fold_y_kernel(flags, sol, strip, low, high, resid, out, work, message, line):
     narrow = lanes(8) < 9
-    out[...] = sol[...]
-    work[...] = strip[...]
     for source, tile, single, flag in ((low, 1, 7, 2), (high, 5, 48, 3)):
         for p in range(42):
             at = p * EXT + 8 * tile
@@ -572,18 +635,17 @@
     flux_x = c_x[0:C, :] * (field[EXT + 8 : EXT + 48, :] - field[8:48, :])
     sum_a = jnp.zeros((8, CZ), F32)
     sum_b = jnp.zeros((8, CZ), F32)
-    for x in range(C):
+    def visit(x, carry):
+        flux_x, sum_a, sum_b = carry
         at = (x + 1) * EXT
-        to = pl.ds(x * C, C)
-        z = field[at + 8 : at + 48, :]
-        next_x = c_x[x * C + C : x * C + 2 * C, :] * (field[at + EXT + 8 : at + EXT + 48, :] - z)
+        to = rows_at(x * C, C)
+        z = field[rows_at(at + 8, C), :]
+        next_x = c_x[rows_at(x * C + C, C), :] * (field[rows_at(at + EXT + 8, C), :] - z)
         net = next_x - flux_x
-        flux_x = next_x
-        net = net + c_up[to, :] * (field[at + 9 : at + 49, :] - z)
-        net = net - c_down[to, :] * (z - field[at + 7 : at + 47, :])
+        net = net + c_up[to, :] * (field[pl.ds(at + 9, C), :] - z)
+        net = net - c_down[to, :] * (z - field[pl.ds(at + 7, C), :])
         flux_z = c_z[to, :] * (roll(z, -1, 1) - z)
-        far = jnp.concatenate([tile((x + 1) * 5 + t) for t in range(5)], axis=0)
-        net = net + (flux_z - roll(flux_z, 1, 1)) + c_face[to, :] * (far - z)
+        net = net + (flux_z - roll(flux_z, 1, 1)) + c_face[to, :] * (out[to, :] - z)
         image = mass_term * z - net + outer * h[to, :] * z
         out[to, :] = z
         applied[to, :] = image
@@ -591,6 +653,12 @@
         for t in range(5):
             sum_a = sum_a + a[8 * t : 8 * t + 8]
             sum_b = sum_b + b[8 * t : 8 * t + 8]
+        return next_x, sum_a, sum_b
+
+    for x in range(C):
+        for t in range(5):
+            out[x * C + 8 * t : x * C + 8 * t + 8, :] = tile((x + 1) * 5 + t)
+    _, sum_a, sum_b = lax.fori_loop(0, C, visit, (flux_x, sum_a, sum_b), unroll=8)
     total_a = jnp.sum(sum_a, axis=0, keepdims=True)
     total_b = jnp.sum(sum_b, axis=0, keepdims=True)
     total_a = total_a + roll(total_a, CZ // 2, 1)
@@ -618,7 +686,7 @@
     b, v, h = (a.reshape(C * C, CZ) for a in (right_side, guess_field, conduct_field))
     n_gx, n_gy = lax.axis_size(gx), lax.axis_size("gy")
     at_x, at_y = lax.axis_index(gx), lax.axis_index("gy")
-    flags = jnp.stack([at_x > 0, at_x < n_gx - 1, at_y > 0, at_y < n_gy - 1]).astype(F32)
+    flags = jnp.stack([at_x > 0, at_x < n_gx - 1, at_y > 0, at_y < n_gy - 1, at_x % 2 == 1]).astype(F32)
 
     def exchange(axis, up, down):
         n = lax.axis_size(axis)
@@ -626,6 +694,10 @@
         backward = [(i + 1, i) for i in range(n - 1)]
         return lax.ppermute(up, axis, forward), lax.ppermute(down, axis, backward)
 
+    def exchange_x(first, second):
+        pairs = [[(i + k, i + 1 - k) for i in range(start, n_gx - 1, 2) for k in (0, 1)] for start in (1, 0)]
+        return lax.ppermute(first, gx, pairs[0]), lax.ppermute(second, gx, pairs[1])
+
     def swap(value):
         return lax.ppermute(value, "gz", [(0, 1), (1, 0)])
 
@@ -638,51 +710,55 @@
 
     part, up, down, edge = call(
         residual_kernel, (own, YROWS, YROWS, 160), v, h, b,
-        scratch=[buffer(own)] * 3 + [pltpu.SemaphoreType.DMA((3, CHUNKS))],
-        hbm=(0, 1, 2), name="residual", work=2,
+        scratch=[buffer(own)] * 4 + [pltpu.SemaphoreType.DMA((4, CHUNKS))],
+        hbm=(0, 1, 2), hbm_out=(0,), limit=56, name="residual", work=2,
     )
     low, high = exchange("gy", up, down)
-    (pairs,) = call(pairs_kernel, (own,), v, h, name="pairs", work=1)
-    scale_a, scale_b = call(
-        scale_kernel, (box, box), eigen, denom, smem=(0,), name="scale", work=2
-    )
-    part, right, left = call(
-        extend_y_kernel, (C * EXT, XROWS, XROWS),
+    pairs, scale_a, scale_b = call(
+        prepare_kernel, (own, box, box), eigen, v, h, denom, smem=(0,), name="prepare", work=2
+    )
+    part, right, left, faces = call(
+        extend_y_kernel, (C * EXT, XROWS, XROWS, 4 * EXT),
         flags, part, pairs, up, down, edge, low, high,
-        smem=(0,), name="extend_y", work=1,
-    )
-    before, after = exchange(gx, right, left)
-    ext, own_z = call(
-        extend_x_kernel, (box, ZROWS),
-        flags, part, pairs, low, high, right, left, before, after,
+        scratch=[buffer(XROWS)] * 2, smem=(0,), name="extend_y", work=1,
+    )
+    one, two = exchange_x(right, left)
+    (packed,) = call(pack_z_kernel, (ZROWS,), part, pairs, low, high, name="pack_z", work=2)
+    (inner,) = call(inner_kernel, (38 * EXT,), plane, part, name="inner", work=1)
+    own_z, fluxes = call(
+        extend_x_kernel, (ZROWS, 2 * EXT), flags, packed, faces, one, two, inner,
         smem=(0,), name="extend_x", work=1,
     )
     far_z = swap(own_z)
-    (main,) = call(forward_kernel, (box,), plane, ext, scratch=[buffer(box)], name="forward", work=2)
+    (main,) = call(
+        forward_kernel, (box,), flags, plane, part, inner, fluxes, one, two,
+        scratch=[buffer(box)], smem=(0,), name="forward", work=2,
+    )
     second_a, second_b, sides, side_strip, right, left = call(
         solve_kernel, (box, box, 18 * EXT, 18 * EXT, XROWS2, XROWS2),
-        own_z, far_z, main, plane, forward, inverse, scale_a, scale_b,
-        scratch=[buffer(box)], name="solve", work=6,
+        flags, own_z, far_z, main, plane, forward, inverse, scale_a, scale_b,
+        scratch=[buffer(box), buffer(XROWS2), buffer(XROWS2)], smem=(0,), name="solve", work=6,
     )
     resid, c_x, c_down, c_up, c_z, c_face = call(
         own_kernel, (own, own + C, own, own, own, own),
-        h, low, high, before, after, ext, own_z, far_z,
-        scratch=[buffer(own + 2 * C)], name="own", work=2,
-    )
-    before, after = exchange(gx, right, left)
+        flags, h, low, high, one, two, part, fluxes, own_z, far_z,
+        scratch=[buffer(own + 2 * C)], smem=(0,), name="own", work=2,
+    )
+    one, two = exchange_x(right, left)
     sol, strip = call(
-        rest_kernel, (38 * EXT, 38 * EXT), plane, inverse, second_a, second_b, name="rest", work=2
+        rest_kernel, (42 * EXT, 42 * EXT),
+        plane, inverse, second_a, second_b, sides, side_strip, name="rest", work=2,
     )
     sol, strip, up, down = call(
         fold_x_kernel, (42 * EXT, 42 * EXT, YROWS2, YROWS2),
-        flags, sides, side_strip, sol, strip, before, after,
-        scratch=[buffer(48)], smem=(0,), name="fold_x", work=1,
+        flags, sol, strip, one, two,
+        scratch=[buffer(48)], smem=(0,), alias={1: 0, 2: 1}, name="fold_x", work=1,
     )
     low, high = exchange("gy", up, down)
-    sol, own_z = call(
-        fold_y_kernel, (42 * EXT, ZROWS2),
-        flags, sol, strip, low, high,
-        scratch=[buffer(42 * EXT), buffer(96)], smem=(0,), name="fold_y", work=1,
+    sol, _, own_z = call(
+        fold_y_kernel, (42 * EXT, 42 * EXT, ZROWS2),
+        flags, sol, strip, low, high, resid,
+        scratch=[buffer(96)], smem=(0,), alias={1: 0, 2: 1}, name="fold_y", work=1,
     )
     far_z = swap(own_z)
     first, last = splits

time: 137 us -> 124 us (0.905)
  blocking collectives: 35.5 us -> 31.6 us
  waiting for transfers between devices: 36.9 us -> 33.5 us
  local copies, waits for them, and re-layouts: 3.46 us -> 0.17 us
  Pallas kernels: 29.3 us -> 26.8 us
    ppermute x0 -> x4, starting transfers between devices: none -> 12.2 us  [the longest x2 8.33 us: exchange_x(): lax.ppermute(first, gx, pairs[0])]
    ppermute x8 -> x4, starting transfers between devices: 26.6 us -> 14.7 us  [exchange(): return (lax.ppermute(up, axis, forward), lax.ppermute(down, axis, backward))]
    ppermute x8 -> x4, waiting for transfers between devices: 32.4 us -> 25.3 us  [exchange(): return (lax.ppermute(up, axis, forward), lax.ppermute(down, axis, backward))]
    all_to_all x1, blocking collectives: 21.9 us -> 18.1 us  [on_device(): sums = lax.all_to_all(sums, first, 0, 0, tiled=True)]
    unnamed x20 -> x22, local copies, waits for them, and re-layouts: 3.46 us -> 0.06 us
    pallas_call x14 -> x15, Pallas kernels: 29.3 us -> 26.8 us  [call(): pl.pallas_call(body, out_shape=[jax.ShapeDtypeStruct((rows, CZ), F32) for...]
    ppermute x2, waiting for transfers between devices: 4.57 us -> 6.93 us  [swap(): return lax.ppermute(value, 'gz', [(0, 1), (1, 0)])]
  transfers between devices with their start and end apart: 10 -> 10, of which waited for: 9 -> 8; matrix products, arithmetic and copies ran while one was open for 0% -> 0% of each run, Pallas kernels for 4% -> 7%
where the time goes in v2:
time: 124 us
  waiting for transfers between devices  33.5 us (27%)
  blocking collectives  31.6 us (25%)
  starting transfers between devices  30.7 us (25%)
  Pallas kernels  26.8 us (22%)
    pallas_call x15, Pallas kernels, call(): pl.pallas_call(body, out_shape=[jax.ShapeDtypeStruct((rows, CZ), F32) for...  26.8 us
    ppermute x4, waiting for transfers between devices, exchange(): return (lax.ppermute(up, axis, forward), lax.ppermute(down, axis, backward))  25.3 us
    all_to_all x1, blocking collectives, on_device(): sums = lax.all_to_all(sums, first, 0, 0, tiled=True)  18.1 us
    ppermute x4, starting transfers between devices, exchange(): return (lax.ppermute(up, axis, forward), lax.ppermute(down, axis, backward))  14.7 us
    all_to_all x1, blocking collectives, on_device(): sums = lax.all_to_all(sums, last, 0, 0, tiled=True)  13.5 us
    ppermute x2, starting transfers between devices, exchange_x(): lax.ppermute(first, gx, pairs[0])  8.33 us
    ppermute x2, waiting for transfers between devices, swap(): return lax.ppermute(value, 'gz', [(0, 1), (1, 0)])  6.93 us
    ppermute x2, starting transfers between devices, exchange_x(): lax.ppermute(second, gx, pairs[1])  3.84 us
  transfers between devices with their start and end apart: 10, of which 8 were waited for; matrix products, arithmetic and copies ran while one was open for 0% of the time, Pallas kernels for 7%

profile of v2, /device:TPU:1, one launch (start us, length us, event | category | flops | bytes accessed | tf_op | source)
XLA Modules:
  0.0 123.8 jit_solution(10290715088275995499)
XLA Ops:
  0.7 5.0 %residual.1 = (f32[1600,128]{1,0:T(8,128)}, f32[440,128]{1,0:T(8,128)}, f32[440,128]{1,0:T(8,128)}, f32[160,128]{1,0:T(8,128)}) custom-call(f32[1600,128]{1,0:T(8,128)} %bitcast.26, f32[1600,128]{1,0:T(8,128)} %bitcast.22, f32[1600,128]{1,0:T(8,128)} %bitcast.29), custom_call_target="tpu_custom_call" | custom-call | flops 2000000000 | bytes 4000000 | tf_op jit(solution)/shard_map/residual/pallas_call | solution.py:110
  5.7 6.6 %collective-permute-start = (f32[440,128]{1,0:T(8,128)}, f32[440,128]{1,0:T(8,128)S(1)}, u32[]{:S(2)}, u32[]{:S(2)}) collective-permute-start(f32[440,128]{1,0:T(8,128)} %get-tuple-element.42.up), channel_id=1, source_target_pairs={{0,2},{2,4},{4,6},{1,3},{3,5},{5,7},{8,10},{10,12},{12,14},{9,11},... | collective-permute-start | bytes 675848 | tf_op jit(solution)/shard_map/ppermute | solution.py:695
  12.3 1.3 %collective-permute-start.1 = (f32[440,128]{1,0:T(8,128)}, f32[440,128]{1,0:T(8,128)S(1)}, u32[]{:S(2)}, u32[]{:S(2)}) collective-permute-start(f32[440,128]{1,0:T(8,128)} %get-tuple-element.43.down), channel_id=1, source_target_pairs={{2,0},{4,2},{6,4},{3,1},{5,3},{7,5},{10,8},{12,10},{14,12},{11,9},... | collective-permute-start | bytes 675848 | tf_op jit(solution)/shard_map/ppermute | solution.py:695
  13.8 1.9 %prepare.1 = (f32[1600,128]{1,0:T(8,128)S(1)}, f32[3136,128]{1,0:T(8,128)S(1)}, f32[3136,128]{1,0:T(8,128)S(1)}) custom-call(f32[56]{0:T(128)S(1)} %copy-done.8, f32[1600,128]{1,0:T(8,128)S(1)} %bitcast.27, f32[1600,128]{1,0:T(8,128)S(1)} %bitcast.23, f32[56,256]{1,0:T(8,128)S(1)} %copy-done.6), custom_call_target="tpu_custom_call" | custom-call | flops 2000000000 | bytes 4000000 | tf_op jit(solution)/shard_map/prepare/pallas_call | solution.py:110
  16.2 13.2 %collective-permute-done.1.high = f32[440,128]{1,0:T(8,128)S(1)} collective-permute-done((f32[440,128]{1,0:T(8,128)}, f32[440,128]{1,0:T(8,128)S(1)}, u32[]{:S(2)}, u32[]{:S(2)}) %collective-permute-start.1) | collective-permute-done | bytes 225312 | tf_op jit(solution)/shard_map/ppermute | solution.py:695
  29.4 1.0 extend_y.1
  30.4 4.5 %collective-permute-start.2 = (f32[616,128]{1,0:T(8,128)S(1)}, f32[616,128]{1,0:T(8,128)S(1)}, u32[]{:S(2)}, u32[]{:S(2)}) collective-permute-start(f32[616,128]{1,0:T(8,128)S(1)} %get-tuple-element.47), channel_id=1, source_target_pairs={{8,16},{16,8},{24,32},{32,24},{40,48},{48,40},{56,64},{64,56},{72,... | collective-permute-start | bytes 946184 | tf_op jit(solution)/shard_map/ppermute | solution.py:699
  34.9 1.9 %collective-permute-start.3 = (f32[616,128]{1,0:T(8,128)S(1)}, f32[616,128]{1,0:T(8,128)S(1)}, u32[]{:S(2)}, u32[]{:S(2)}) collective-permute-start(f32[616,128]{1,0:T(8,128)S(1)} %get-tuple-element.48), channel_id=1, source_target_pairs={{0,8},{8,0},{16,24},{24,16},{32,40},{40,32},{48,56},{56,48},{64,72... | collective-permute-start | bytes 946184 | tf_op jit(solution)/shard_map/ppermute | solution.py:699
  37.3 1.4 %pack_z.1.packed = f32[280,128]{1,0:T(8,128)S(1)} custom-call(f32[2240,128]{1,0:T(8,128)S(1)} %get-tuple-element.45.part, f32[1600,128]{1,0:T(8,128)S(1)} %get-tuple-element.41.vh, f32[440,128]{1,0:T(8,128)S(1)} %collective-permute-done.low, f32[440,128]{1,0:T(8,128)S(1)} %collective-permute-done.1.high), custom_call_target="tpu_custom_call" | custom-call | flops 2000000000 | bytes 4000000 | tf_op jit(solution)/shard_map/pack_z/pallas_call | solution.py:110
  38.7 0.8 collective-permute-done.2.first.one
  39.5 0.7 extend_x.1
  40.2 1.9 %collective-permute-start.4 = (f32[280,128]{1,0:T(8,128)S(1)}, f32[280,128]{1,0:T(8,128)S(1)}, u32[]{:S(2)}, u32[]{:S(2)}) collective-permute-start(f32[280,128]{1,0:T(8,128)S(1)} %get-tuple-element.49.own_z), channel_id=1, source_target_pairs={{0,1},{1,0},{2,3},{3,2},{4,5},{5,4},{6,7},{7,6},{8,9},{9,8},{10,11... | collective-permute-start | bytes 430088 | tf_op jit(solution)/shard_map/ppermute | solution.py:702
  42.2 1.7 %forward.2.main = f32[3136,128]{1,0:T(8,128)S(1)} custom-call(f32[5]{0:T(128)S(1)} %convert_element_type.3.flags, bf16[56,192]{1,0:T(8,128)(2,1)S(1)} %copy-done.7, f32[2240,128]{1,0:T(8,128)S(1)} %get-tuple-element.45.part, f32[2128,128]{1,0:T(8,128)S(1)} %inner.1, f32[112,128]{1,0:T(8,128)S(1)} %get-tuple-element.50.fluxes, ...), custom_call_target="tpu_custom_call" | custom-call | flops 2000000000 | bytes 4000000 | tf_op jit(solution)/shard_map/forward/pallas_call | solution.py:110
  43.9 3.9 %collective-permute-done.4.far_z = f32[280,128]{1,0:T(8,128)S(1)} collective-permute-done((f32[280,128]{1,0:T(8,128)S(1)}, f32[280,128]{1,0:T(8,128)S(1)}, u32[]{:S(2)}, u32[]{:S(2)}) %collective-permute-start.4) | collective-permute-done | bytes 143392 | tf_op jit(solution)/shard_map/ppermute | solution.py:702
  47.7 6.2 %solve.1 = (f32[3136,128]{1,0:T(8,128)S(1)}, f32[3136,128]{1,0:T(8,128)S(1)}, f32[1008,128]{1,0:T(8,128)S(1)}, f32[1008,128]{1,0:T(8,128)S(1)}, f32[544,128]{1,0:T(8,128)S(1)}, /*index=5*/f32[544,128]{1,0:T(8,128)S(1)}) custom-call(f32[5]{0:T(128)S(1)} %convert_element_type.3.flags, f32[280,128]{1,0:T(8,128)S(1)} %get-tuple-element.49.own_z, ...), custom_call_target="tpu_custom_call" | custom-call | flops 6000000000 | bytes 12000000 | tf_op jit(solution)/shard_map/solve/pallas_call | solution.py:110
  53.9 3.8 %collective-permute-start.5 = (f32[544,128]{1,0:T(8,128)S(1)}, f32[544,128]{1,0:T(8,128)S(1)}, u32[]{:S(2)}, u32[]{:S(2)}) collective-permute-start(f32[544,128]{1,0:T(8,128)S(1)} %get-tuple-element.59), channel_id=1, source_target_pairs={{8,16},{16,8},{24,32},{32,24},{40,48},{48,40},{56,64},{64,56},{72,... | collective-permute-start | bytes 835592 | tf_op jit(solution)/shard_map/ppermute | solution.py:699
  57.8 1.9 %collective-permute-start.6 = (f32[544,128]{1,0:T(8,128)S(1)}, f32[544,128]{1,0:T(8,128)S(1)}, u32[]{:S(2)}, u32[]{:S(2)}) collective-permute-start(f32[544,128]{1,0:T(8,128)S(1)} %get-tuple-element.60), channel_id=1, source_target_pairs={{0,8},{8,0},{16,24},{24,16},{32,40},{40,32},{48,56},{56,48},{64,72... | collective-permute-start | bytes 835592 | tf_op jit(solution)/shard_map/ppermute | solution.py:699
  59.7 1.8 %rest.1 = (f32[2352,128]{1,0:T(8,128)S(1)}, f32[2352,128]{1,0:T(8,128)S(1)}) custom-call(bf16[56,192]{1,0:T(8,128)(2,1)S(1)} %copy-done.7, bf16[2,768,256]{2,1,0:T(8,128)(2,1)S(1)} %copy-done.4, f32[3136,128]{1,0:T(8,128)S(1)} %get-tuple-element.53.second_a, f32[3136,128]{1,0:T(8,128)S(1)} %get-tuple-element.54.second_b, ...), custom_call_target="tpu_custom_call" | custom-call | flops 2000000000 | bytes 4000000 | tf_op jit(solution)/shard_map/rest/pallas_call | solution.py:110
  61.5 0.5 collective-permute-done.5.one
  62.0 1.0 fold_x.1
  62.9 5.5 %collective-permute-start.7 = (f32[416,128]{1,0:T(8,128)S(1)}, f32[416,128]{1,0:T(8,128)S(1)}, u32[]{:S(2)}, u32[]{:S(2)}) collective-permute-start(f32[416,128]{1,0:T(8,128)S(1)} %get-tuple-element.63), channel_id=1, source_target_pairs={{0,2},{2,4},{4,6},{1,3},{3,5},{5,7},{8,10},{10,12},{12,14},{9,11},... | collective-permute-start | bytes 638984 | tf_op jit(solution)/shard_map/ppermute | solution.py:695
  68.4 1.3 %collective-permute-start.8 = (f32[416,128]{1,0:T(8,128)S(1)}, f32[416,128]{1,0:T(8,128)S(1)}, u32[]{:S(2)}, u32[]{:S(2)}) collective-permute-start(f32[416,128]{1,0:T(8,128)S(1)} %get-tuple-element.64), channel_id=1, source_target_pairs={{2,0},{4,2},{6,4},{3,1},{5,3},{7,5},{10,8},{12,10},{14,12},{11,9},... | collective-permute-start | bytes 638984 | tf_op jit(solution)/shard_map/ppermute | solution.py:695
  69.7 1.4 %own.1 = (f32[1600,128]{1,0:T(8,128)S(1)}, f32[1640,128]{1,0:T(8,128)S(1)}, f32[1600,128]{1,0:T(8,128)S(1)}, f32[1600,128]{1,0:T(8,128)S(1)}, f32[1600,128]{1,0:T(8,128)S(1)}, /*index=5*/f32[1600,128]{1,0:T(8,128)S(1)}) custom-call(f32[5]{0:T(128)S(1)} %convert_element_type.3.flags, f32[1600,128]{1,0:T(8,128)S(1)} %bitcast.24, ...), custom_call_target="tpu_custom_call" | custom-call | flops 2000000000 | bytes 4000000 | tf_op jit(solution)/shard_map/own/pallas_call | solution.py:110
  71.1 2.0 %collective-permute-done.7.low = f32[416,128]{1,0:T(8,128)S(1)} collective-permute-done((f32[416,128]{1,0:T(8,128)S(1)}, f32[416,128]{1,0:T(8,128)S(1)}, u32[]{:S(2)}, u32[]{:S(2)}) %collective-permute-start.7) | collective-permute-done | bytes 213024 | tf_op jit(solution)/shard_map/ppermute | solution.py:695
  73.1 9.6 %collective-permute-done.8.high = f32[416,128]{1,0:T(8,128)S(1)} collective-permute-done((f32[416,128]{1,0:T(8,128)S(1)}, f32[416,128]{1,0:T(8,128)S(1)}, u32[]{:S(2)}, u32[]{:S(2)}) %collective-permute-start.8) | collective-permute-done | bytes 213024 | tf_op jit(solution)/shard_map/ppermute | solution.py:695
  82.7 0.9 fold_y.1
  83.7 1.9 %collective-permute-start.9 = (f32[128,128]{1,0:T(8,128)S(1)}, f32[128,128]{1,0:T(8,128)S(1)}, u32[]{:S(2)}, u32[]{:S(2)}) collective-permute-start(f32[128,128]{1,0:T(8,128)S(1)} %get-tuple-element.67.own_z), channel_id=1, source_target_pairs={{0,1},{1,0},{2,3},{3,2},{4,5},{5,4},{6,7},{7,6},{8,9},{9,8},{10,11... | collective-permute-start | bytes 196616 | tf_op jit(solution)/shard_map/ppermute | solution.py:702
  85.6 3.1 %collective-permute-done.9.far_z = f32[128,128]{1,0:T(8,128)S(1)} collective-permute-done((f32[128,128]{1,0:T(8,128)S(1)}, f32[128,128]{1,0:T(8,128)S(1)}, u32[]{:S(2)}, u32[]{:S(2)}) %collective-permute-start.9) | collective-permute-done | bytes 65568 | tf_op jit(solution)/shard_map/ppermute | solution.py:702
  88.7 2.1 %apply.1 = (f32[1600,128]{1,0:T(8,128)S(1)}, f32[1600,128]{1,0:T(8,128)S(1)}, f32[32,128]{1,0:T(8,128)S(1)}) custom-call(f32[2352,128]{1,0:T(8,128)S(1)} %get-tuple-element.66.sol, f32[128,128]{1,0:T(8,128)S(1)} %get-tuple-element.67.own_z, f32[128,128]{1,0:T(8,128)S(1)} %collective-permute-done.9.far_z, f32[1600,128]{1,0:T(8,128)S(1)} %get-tuple-element.65.resid, ...), custom_call_target="tpu_custom_call" | custom-call | flops 3000000000 | bytes 6000000 | tf_op jit(solution)/shard_map/apply/pallas_call | solution.py:110
  90.8 18.1 %all_to_all.22 = f32[32,1,128]{2,1,0:T(1,128)S(1)} all-to-all(f32[32,1,128]{2,1,0:T(1,128)S(1)} %bitcast.20), channel_id=1, replica_groups=mesh['gx_x'=4,'gx_y'=8,'gx_c'=2,'gy'=4,'gz'=2] {'gx_x','gx_y'}, dimensions={0} | all-to-all | bytes 32768 | tf_op jit(solution)/shard_map/all_to_all | solution.py:770
  108.9 13.5 %all_to_all.23 = f32[16,1,128]{2,1,0:T(1,128)S(1)} all-to-all(f32[16,1,128]{2,1,0:T(1,128)S(1)} %bitcast.19), channel_id=1, replica_groups=mesh['gx_x'=4,'gx_y'=8,'gx_c'=2,'gy'=4,'gz'=2] {'gx_c','gy','gz'}, dimensions={0} | all-to-all | bytes 16384 | tf_op jit(solution)/shard_map/all_to_all | solution.py:772
  122.4 1.4 %update.1 = (f32[1600,128]{1,0:T(8,128)}, f32[1600,128]{1,0:T(8,128)}) custom-call(f32[16,128]{1,0:T(8,128)S(1)} %bitcast.21, f32[1600,128]{1,0:T(8,128)S(1)} %bitcast.28, f32[1600,128]{1,0:T(8,128)S(1)} %get-tuple-element.65.resid, f32[1600,128]{1,0:T(8,128)S(1)} %get-tuple-element.74.field, f32[1600,128]{1,0:T(8,128)S(1)} %get-tuple-element.75.applied), custom_call_target="tpu_custom_call" | custom-call | flops 2000000000 | bytes 4000000 | tf_op jit(solution)/shard_map/update/pallas_call | solution.py:110
  (29 shorter events, 1.2 us)
Async XLA Ops:
  0.6 13.1 %copy-start = (f32[40,40,128]{2,1,0:T(8,128)S(1)}, f32[40,40,128]{2,1,0:T(8,128)}, u32[]{:S(2)}) copy-start(f32[40,40,128]{2,1,0:T(8,128)} %param.10) | copy-start | bytes 2457604
  0.6 13.1 %copy-start.1 = (f32[40,40,128]{2,1,0:T(8,128)S(1)}, f32[40,40,128]{2,1,0:T(8,128)}, u32[]{:S(2)}) copy-start(f32[40,40,128]{2,1,0:T(8,128)} %param.9) | copy-start | bytes 2457604
  0.6 13.1 %copy-start.6 = (f32[56,256]{1,0:T(8,128)S(1)}, f32[56,256]{1,0:T(8,128)}, u32[]{:S(2)}) copy-start(f32[56,256]{1,0:T(8,128)} %constant.49.clone.denom) | copy-start | bytes 172036
  0.7 13.1 %copy-start.8 = (f32[56]{0:T(128)S(1)}, f32[56]{0:T(128)}, u32[]{:S(2)}) copy-start(f32[56]{0:T(128)} %constant.48.clone.eigen) | copy-start | bytes 676
  5.7 10.5 %collective-permute-start = (f32[440,128]{1,0:T(8,128)}, f32[440,128]{1,0:T(8,128)S(1)}, u32[]{:S(2)}, u32[]{:S(2)}) collective-permute-start(f32[440,128]{1,0:T(8,128)} %get-tuple-element.42.up), channel_id=1, source_target_pairs={{0,2},{2,4},{4,6},{1,3},{3,5},{5,7},{8,10},{10,12},{12,14},{9,11},... | collective-permute-start | bytes 675848 | tf_op jit(solution)/shard_map/ppermute | solution.py:695
  12.3 17.1 %collective-permute-start.1 = (f32[440,128]{1,0:T(8,128)}, f32[440,128]{1,0:T(8,128)S(1)}, u32[]{:S(2)}, u32[]{:S(2)}) collective-permute-start(f32[440,128]{1,0:T(8,128)} %get-tuple-element.43.down), channel_id=1, source_target_pairs={{2,0},{4,2},{6,4},{3,1},{5,3},{7,5},{10,8},{12,10},{14,12},{11,9},... | collective-permute-start | bytes 675848 | tf_op jit(solution)/shard_map/ppermute | solution.py:695
  13.8 15.6 %copy-start.2 = (f32[440,128]{1,0:T(8,128)S(1)}, f32[440,128]{1,0:T(8,128)}, u32[]{:S(2)}) copy-start(f32[440,128]{1,0:T(8,128)} %get-tuple-element.42.up) | copy-start | bytes 675844
  13.8 15.6 %copy-start.3 = (f32[440,128]{1,0:T(8,128)S(1)}, f32[440,128]{1,0:T(8,128)}, u32[]{:S(2)}) copy-start(f32[440,128]{1,0:T(8,128)} %get-tuple-element.43.down) | copy-start | bytes 675844
  13.8 15.6 %copy-start.9 = (f32[1600,128]{1,0:T(8,128)S(1)}, f32[1600,128]{1,0:T(8,128)}, u32[]{:S(2)}) copy-start(f32[1600,128]{1,0:T(8,128)} %get-tuple-element.40.part) | copy-start | bytes 2457604
  13.8 15.6 %copy-start.10 = (f32[160,128]{1,0:T(8,128)S(1)}, f32[160,128]{1,0:T(8,128)}, u32[]{:S(2)}) copy-start(f32[160,128]{1,0:T(8,128)} %get-tuple-element.44.edge) | copy-start | bytes 245764
  29.4 7.4 %copy-start.7 = (bf16[56,192]{1,0:T(8,128)(2,1)S(1)}, bf16[56,192]{1,0:T(8,128)(2,1)}, u32[]{:S(2)}) copy-start(bf16[56,192]{1,0:T(8,128)(2,1)} %constant.50.clone.plane) | copy-start | bytes 64516
  30.4 9.1 %collective-permute-start.2 = (f32[616,128]{1,0:T(8,128)S(1)}, f32[616,128]{1,0:T(8,128)S(1)}, u32[]{:S(2)}, u32[]{:S(2)}) collective-permute-start(f32[616,128]{1,0:T(8,128)S(1)} %get-tuple-element.47), channel_id=1, source_target_pairs={{8,16},{16,8},{24,32},{32,24},{40,48},{48,40},{56,64},{64,56},{72,... | collective-permute-start | bytes 946184 | tf_op jit(solution)/shard_map/ppermute | solution.py:699
  34.9 4.6 %collective-permute-start.3 = (f32[616,128]{1,0:T(8,128)S(1)}, f32[616,128]{1,0:T(8,128)S(1)}, u32[]{:S(2)}, u32[]{:S(2)}) collective-permute-start(f32[616,128]{1,0:T(8,128)S(1)} %get-tuple-element.48), channel_id=1, source_target_pairs={{0,8},{8,0},{16,24},{24,16},{32,40},{40,32},{48,56},{56,48},{64,72... | collective-permute-start | bytes 946184 | tf_op jit(solution)/shard_map/ppermute | solution.py:699
  40.2 7.5 %collective-permute-start.4 = (f32[280,128]{1,0:T(8,128)S(1)}, f32[280,128]{1,0:T(8,128)S(1)}, u32[]{:S(2)}, u32[]{:S(2)}) collective-permute-start(f32[280,128]{1,0:T(8,128)S(1)} %get-tuple-element.49.own_z), channel_id=1, source_target_pairs={{0,1},{1,0},{2,3},{3,2},{4,5},{5,4},{6,7},{7,6},{8,9},{9,8},{10,11... | collective-permute-start | bytes 430088 | tf_op jit(solution)/shard_map/ppermute | solution.py:702
  42.2 5.6 %copy-start.4 = (bf16[2,768,256]{2,1,0:T(8,128)(2,1)S(1)}, bf16[2,768,256]{2,1,0:T(8,128)(2,1)}, u32[]{:S(2)}) copy-start(bf16[2,768,256]{2,1,0:T(8,128)(2,1)} %constant.52.clone.inverse) | copy-start | bytes 2359300
  42.2 5.6 %copy-start.5 = (bf16[2,768,256]{2,1,0:T(8,128)(2,1)S(1)}, bf16[2,768,256]{2,1,0:T(8,128)(2,1)}, u32[]{:S(2)}) copy-start(bf16[2,768,256]{2,1,0:T(8,128)(2,1)} %constant.51.clone.forward) | copy-start | bytes 2359300
  53.9 8.0 %collective-permute-start.5 = (f32[544,128]{1,0:T(8,128)S(1)}, f32[544,128]{1,0:T(8,128)S(1)}, u32[]{:S(2)}, u32[]{:S(2)}) collective-permute-start(f32[544,128]{1,0:T(8,128)S(1)} %get-tuple-element.59), channel_id=1, source_target_pairs={{8,16},{16,8},{24,32},{32,24},{40,48},{48,40},{56,64},{64,56},{72,... | collective-permute-start | bytes 835592 | tf_op jit(solution)/shard_map/ppermute | solution.py:699
  57.8 4.2 %collective-permute-start.6 = (f32[544,128]{1,0:T(8,128)S(1)}, f32[544,128]{1,0:T(8,128)S(1)}, u32[]{:S(2)}, u32[]{:S(2)}) collective-permute-start(f32[544,128]{1,0:T(8,128)S(1)} %get-tuple-element.60), channel_id=1, source_target_pairs={{0,8},{8,0},{16,24},{24,16},{32,40},{40,32},{48,56},{56,48},{64,72... | collective-permute-start | bytes 835592 | tf_op jit(solution)/shard_map/ppermute | solution.py:699
  62.9 10.2 %collective-permute-start.7 = (f32[416,128]{1,0:T(8,128)S(1)}, f32[416,128]{1,0:T(8,128)S(1)}, u32[]{:S(2)}, u32[]{:S(2)}) collective-permute-start(f32[416,128]{1,0:T(8,128)S(1)} %get-tuple-element.63), channel_id=1, source_target_pairs={{0,2},{2,4},{4,6},{1,3},{3,5},{5,7},{8,10},{10,12},{12,14},{9,11},... | collective-permute-start | bytes 638984 | tf_op jit(solution)/shard_map/ppermute | solution.py:695
  68.4 14.3 %collective-permute-start.8 = (f32[416,128]{1,0:T(8,128)S(1)}, f32[416,128]{1,0:T(8,128)S(1)}, u32[]{:S(2)}, u32[]{:S(2)}) collective-permute-start(f32[416,128]{1,0:T(8,128)S(1)} %get-tuple-element.64), channel_id=1, source_target_pairs={{2,0},{4,2},{6,4},{3,1},{5,3},{7,5},{10,8},{12,10},{14,12},{11,9},... | collective-permute-start | bytes 638984 | tf_op jit(solution)/shard_map/ppermute | solution.py:695
  83.7 5.0 %collective-permute-start.9 = (f32[128,128]{1,0:T(8,128)S(1)}, f32[128,128]{1,0:T(8,128)S(1)}, u32[]{:S(2)}, u32[]{:S(2)}) collective-permute-start(f32[128,128]{1,0:T(8,128)S(1)} %get-tuple-element.67.own_z), channel_id=1, source_target_pairs={{0,1},{1,0},{2,3},{3,2},{4,5},{5,4},{6,7},{7,6},{8,9},{9,8},{10,11... | collective-permute-start | bytes 196616 | tf_op jit(solution)/shard_map/ppermute | solution.py:702

commit v3 on v2

--- a/solution.py
+++ b/solution.py
@@ -136,33 +136,82 @@
     return jnp.where(lax.axis_index("gz") == 0, 0, 127)
 
 
-CHUNKS = 5
-
-
 def pair_of(v, h, lane, base, face):
     return jnp.where(lane == base, roll(v, base - face, 1), 0.0) + jnp.where(
         lane == base + 1, roll(h, base + 1 - face, 1), 0.0
     )
 
 
-def residual_kernel(v_in, h_in, b_in, part_out, up, down, edge, part, v, h, b, sems):
+def strips_kernel(v_in, h_in, b_in, up, down, v, h, b, sems):
+    copies = []
+    for k, (source, target, size) in enumerate(((v_in, v, 16), (h_in, h, 16), (b_in, b, 8))):
+        for side, first in enumerate((0, C - size)):
+            at = pl.ds(first, size)
+            copies.append(
+                pltpu.make_async_copy(source.at[:, at, :], target.at[:, at, :], sems.at[k, side])
+            )
+            copies[-1].start()
     base, face = strip_base(), face_lane()
-    planes = C // CHUNKS
-    size = planes * C
-    copies = []
-    for c in range(CHUNKS):
-        at = pl.ds(c * size, size)
-        for k, (source, target) in enumerate(((v_in, v), (h_in, h), (b_in, b))):
-            copies.append(pltpu.make_async_copy(source.at[at, :], target.at[at, :], sems.at[k, c]))
-            copies[-1].start()
-    lane, lane8 = lanes(C), lanes(8)
+    lane = lanes(8)
+    row = lax.broadcasted_iota(jnp.int32, (8, CZ), 0)
+    z_half = jnp.where(lane < CZ - 1, 0.5, 0.0)
+    outer = jnp.where(lane == outer_lane(), 0.5, 0.0)
+    last = C - 1
+    for copy in copies:
+        copy.wait()
+
+    def tile(x, start, beyond, sign, flux_x):
+        following = jnp.minimum(x + 1, last)
+        at, to = pl.ds(start, 8), pl.ds(beyond, 8)
+        vi, hi = v[x, at, :], h[x, at, :]
+        next_x = 0.5 * (hi + h[following, at, :]) * (v[following, at, :] - vi)
+        flux_y = 0.5 * (hi + h[x, to, :]) * (v[x, to, :] - vi)
+        edge = 0 if sign > 0 else 7
+        net_y = flux_y - jnp.where(row == edge, 0.0, roll(flux_y, sign, 0))
+        flux_z = z_half * (hi + roll(hi, -1, 1)) * (roll(vi, -1, 1) - vi)
+        applied = (
+            mass_term * vi
+            - (next_x - flux_x)
+            - net_y
+            - (flux_z - roll(flux_z, 1, 1))
+            + outer * hi * vi
+        )
+        return b[x, at, :] - applied, next_x, vi, hi
+
+    def visit(x, carry):
+        flux_up, flux_down, pack_up, pack_down = carry
+        resid, flux_down, vi, hi = tile(x, 0, 1, 1, flux_down)
+        down[tile_at(x), :] = resid
+        down[pl.ds(320 + x, 1), :] = vi[0:1]
+        down[pl.ds(360 + x, 1), :] = hi[0:1]
+        pack_down = pack_down + roll(pair_of(vi, hi, lane, base, face), 2 * x - base, 1)
+        resid, flux_up, vi, hi = tile(x, 32, 31, -1, flux_up)
+        up[tile_at(x), :] = resid
+        up[pl.ds(320 + x, 1), :] = vi[7:8]
+        up[pl.ds(360 + x, 1), :] = hi[7:8]
+        pack_up = pack_up + roll(pair_of(vi, hi, lane, base, face), 2 * x - base, 1)
+        return flux_up, flux_down, pack_up, pack_down
+
+    zero = jnp.zeros((8, CZ), F32)
+    _, _, pack_up, pack_down = lax.fori_loop(0, C, visit, (zero,) * 4, unroll=8)
+    up[432:440, :] = pack_up
+    down[432:440, :] = pack_down
+    for message, first in ((up, 32), (down, 0)):
+        at = pl.ds(first, 8)
+        message[400:408, :] = v[0, at, :]
+        message[408:416, :] = h[0, at, :]
+        message[416:424, :] = v[last, at, :]
+        message[424:432, :] = h[last, at, :]
+
+
+def residual_kernel(v, h, b, part, edge):
+    lane = lanes(C)
     row = lax.broadcasted_iota(jnp.int32, (C, CZ), 0)
     y_half = jnp.where(row > 0, 0.5, 0.0)
     z_half = jnp.where(lane < CZ - 1, 0.5, 0.0)
     outer = jnp.where(lane == outer_lane(), 0.5, 0.0)
 
-    def visit(x, carry):
-        flux_x, pack_up, pack_down = carry
+    def visit(x, flux_x):
         own = rows_at(x * C, C)
         following = rows_at(jnp.minimum(x + 1, C - 1) * C, C)
         vi, hi = v[own, :], h[own, :]
@@ -176,44 +225,15 @@
             - (flux_z - roll(flux_z, 1, 1))
             + outer * hi * vi
         )
-        resid = b[own, :] - applied
-        part[own, :] = resid
-        down[tile_at(x), :] = resid[0:8]
-        up[tile_at(x), :] = resid[32:40]
-        pair = pair_of(vi[32:40], hi[32:40], lane8, base, face)
-        pack_up = pack_up + roll(pair, 2 * x - base, 1)
-        pair = pair_of(vi[0:8], hi[0:8], lane8, base, face)
-        pack_down = pack_down + roll(pair, 2 * x - base, 1)
-        return next_x, pack_up, pack_down
-
-    carry = (jnp.zeros((C, CZ), F32), jnp.zeros((8, CZ), F32), jnp.zeros((8, CZ), F32))
-    for k in range(3):
-        copies[k].wait()
-    for c in range(CHUNKS):
-        if c < CHUNKS - 1:
-            for k in range(3):
-                copies[3 * (c + 1) + k].wait()
-        carry = lax.fori_loop(c * planes, (c + 1) * planes, visit, carry, unroll=4)
-        at = pl.ds(c * size, size)
-        copies.append(pltpu.make_async_copy(part.at[at, :], part_out.at[at, :], sems.at[3, c]))
-        copies[-1].start()
-    up[432:440, :] = carry[1]
-    down[432:440, :] = carry[2]
+        part[own, :] = b[own, :] - applied
+        return next_x
+
+    lax.fori_loop(0, C, visit, jnp.zeros((C, CZ), F32), unroll=4)
     last = (C - 1) * C
-    for message, first in ((up, 32), (down, 0)):
-        face_row = C - 1 if first else 0
-        message[320:360, :] = v[pl.ds(face_row, C, stride=C), :]
-        message[360:400, :] = h[pl.ds(face_row, C, stride=C), :]
-        message[400:408, :] = v[first : first + 8, :]
-        message[408:416, :] = h[first : first + 8, :]
-        message[416:424, :] = v[last + first : last + first + 8, :]
-        message[424:432, :] = h[last + first : last + first + 8, :]
     edge[0:40, :] = v[0:40, :]
     edge[40:80, :] = h[0:40, :]
     edge[80:120, :] = v[last : last + 40, :]
     edge[120:160, :] = h[last : last + 40, :]
-    for copy in copies[-CHUNKS:]:
-        copy.wait()
 
 
 def prepare_kernel(eigen, v, h, denom, out, out_a, out_b):
@@ -261,24 +281,29 @@
     return jnp.where(lax.axis_index("gz") == 0, lane - 120, 7 - lane) >= 0
 
 
-def extend_y_kernel(flags, part, vh, up, down, edge, low, high, out, first, second, faces, right, left):
+def y_fluxes(up, down, low, high):
+    flux_a = 0.5 * (low[360:400, :] + down[360:400, :]) * (down[320:360, :] - low[320:360, :])
+    flux_b = 0.5 * (up[360:400, :] + high[360:400, :]) * (high[320:360, :] - up[320:360, :])
+    return flux_a, flux_b
+
+
+def extend_y(flags, fluxes, part, low, high, out, start, stop):
+    for x in range(start, stop):
+        at = (x - start) * EXT
+        out[at : at + 8, :] = low[8 * x : 8 * x + 8, :]
+        out[at + 8 : at + 48, :] = part[x * C : x * C + C, :]
+        out[at + 48 : at + 56, :] = high[8 * x : 8 * x + 8, :]
+    flux_a, flux_b = (flux[start:stop] for flux in fluxes)
+    for row, value in ((8, -flux_a), (7, flux_a * flags[2]), (47, flux_b), (48, -flux_b * flags[3])):
+        at = pl.ds(row, stop - start, stride=EXT)
+        out[at, :] = out[at, :] + value
+
+
+def extend_y_kernel(flags, part, vh, up, down, edge, low, high, first, second, faces, right, left):
     base, strip_lanes = strip_base(), strip_mask()
-
-    def visit(x, _):
-        out[rows_at(x * EXT, 8), :] = low[tile_at(x), :]
-        out[rows_at(x * EXT + 8, C), :] = part[rows_at(x * C, C), :]
-        out[rows_at(x * EXT + 48, 8), :] = high[tile_at(x), :]
-        return 0
-
-    lax.fori_loop(0, C, visit, 0, unroll=8)
-    flux = 0.5 * (low[360:400, :] + down[360:400, :]) * (down[320:360, :] - low[320:360, :])
-    out[pl.ds(8, C, stride=EXT), :] = out[pl.ds(8, C, stride=EXT), :] - flux
-    out[pl.ds(7, C, stride=EXT), :] = out[pl.ds(7, C, stride=EXT), :] + flux * flags[2]
-    flux = 0.5 * (up[360:400, :] + high[360:400, :]) * (high[320:360, :] - up[320:360, :])
-    out[pl.ds(47, C, stride=EXT), :] = out[pl.ds(47, C, stride=EXT), :] + flux
-    out[pl.ds(48, C, stride=EXT), :] = out[pl.ds(48, C, stride=EXT), :] - flux * flags[3]
+    fluxes = y_fluxes(up, down, low, high)
     for message, start, strip, own in ((left, 0, 400, 0), (right, 32, 416, 80)):
-        message[0:448, :] = out[start * EXT : start * EXT + 448, :]
+        extend_y(flags, fluxes, part, low, high, message, start, start + OVER)
         for k in range(2):
             at = 448 + k * EXT
             message[at : at + 8, :] = low[strip + 8 * k : strip + 8 * k + 8, :]
@@ -289,7 +314,8 @@
             taken = jnp.zeros((8, CZ), F32)
             for i in range(OVER):
                 x = start + i
-                value = jnp.where(strip_lanes, out[x * EXT + 8 * t : x * EXT + 8 * t + 8, :], 0.0)
+                at = i * EXT + 8 * t
+                value = jnp.where(strip_lanes, message[at : at + 8, :], 0.0)
                 if t == 0:
                     taken = taken + pick(low[432:440, :], x, 10 * i)
                 elif t == 6:
@@ -376,8 +402,9 @@
     return jnp.concatenate([a, b], axis=1)
 
 
-def inner_kernel(plane, part, out):
+def inner_kernel(flags, plane, box, up, down, low, high, out, part):
     table = plane[...]
+    extend_y(flags, y_fluxes(up, down, low, high), box, low, high, part, 0, C)
     for x in range(1, C - 1, 2):
         at, then = pl.ds(x * EXT, EXT), pl.ds((x + 1) * EXT, EXT)
         value = along_rows(table, beside(part[at, :], part[then, :]))
@@ -546,7 +573,9 @@
     return roll(message[rows_at(at + 8 * q, 8), :], -9 * (index - q * PER), 1)
 
 
-def fold_x_kernel(flags, sol, strip, one, two, out, out_strip, up, down, line):
+def fold_x_kernel(
+    flags, sol, strip, one, two, _, out, out_strip, up, down, across, across_up, across_down, line
+):
     size = 42 * EXT
     narrow = lanes(8) < 9
     before, after = by_parity(flags, one, two)
@@ -575,58 +604,69 @@
         values = [out_strip[p * EXT + 8 * tile : p * EXT + 8 * tile + 8, :] for p in range(42)]
         values += [line[8 * j : 8 * j + 8, :] for j in range(6)]
         pack_tiles(message, 384, values)
-
-
-def fold_y_kernel(flags, sol, strip, low, high, resid, out, work, message, line):
-    narrow = lanes(8) < 9
-    for source, tile, single, flag in ((low, 1, 7, 2), (high, 5, 48, 3)):
-        for p in range(42):
-            at = p * EXT + 8 * tile
-            out[at : at + 8, :] = out[at : at + 8, :] + source[8 * p : 8 * p + 8, :]
-            value = jnp.where(narrow, unpack_tile(source, 384, p), 0.0)
-            work[at : at + 8, :] = work[at : at + 8, :] + value
-        at = pl.ds(single, 42, stride=EXT)
-        out[at, :] = (out[at, :] + source[336:378, :]) * flags[flag]
-        for j in range(6):
-            line[8 * j : 8 * j + 8, :] = jnp.where(narrow, unpack_tile(source, 384, 42 + j), 0.0)
-        work[at, :] = (work[at, :] + line[0:42, :]) * flags[flag]
+    across_up[...] = up[384:416, :]
+    across_down[...] = down[384:416, :]
     values = []
     for p in range(42):
         for t in range(1, 6):
             at = p * EXT + 8 * t
-            values.append(work[at : at + 8, :])
+            values.append(out_strip[at : at + 8, :])
     for k, single in enumerate((7, 48)):
-        line[48 * k + 40 : 48 * k + 48, :] = jnp.zeros((8, CZ), F32)
-        line[48 * k : 48 * k + 42, :] = work[pl.ds(single, 42, stride=EXT), :]
-        values += [line[48 * k + 8 * j : 48 * k + 8 * j + 8, :] for j in range(6)]
-    pack_tiles(message, 0, values)
+        at = 48 * (k + 1)
+        line[at + 40 : at + 48, :] = jnp.zeros((8, CZ), F32)
+        line[at : at + 42, :] = out_strip[pl.ds(single, 42, stride=EXT), :] * flags[2 + k]
+        values += [line[at + 8 * j : at + 8 * j + 8, :] for j in range(6)]
+    pack_tiles(across, 0, values)
+
+
+def fold_y_kernel(flags, sol, low, high, out):
+    for p in range(42):
+        for message, tile in ((low, 1), (high, 5)):
+            at = p * EXT + 8 * tile
+            out[at : at + 8, :] = out[at : at + 8, :] + message[8 * p : 8 * p + 8, :]
+    for k, (single, message) in enumerate(((7, low), (48, high))):
+        at = pl.ds(single, 42, stride=EXT)
+        out[at, :] = (out[at, :] + message[336:378, :]) * flags[2 + k]
 
 
 def apply_kernel(
-    sol, own_z, far_z, resid, c_x, c_down, c_up, c_z, c_face, h,
+    sol, low, high, own_z, far_z, far_low, far_high, resid, c_x, c_down, c_up, c_z, c_face, h,
     out, applied, sums, field, pack, line,
 ):
     gz = lax.axis_index("gz")
-    lane = lanes(ZROWS2)
+    end = YROWS2 - 384
+    lane = lanes(ZROWS2 + 2 * end)
     at_face = lax.rem(lane, 9) == jnp.where(gz == 0, 8, 0)
     shift = jnp.where(gz == 0, 7, 121)
-    packed = far_z[...] + jnp.where(at_face, roll(own_z[...], shift, 1), 0.0)
-    pack[...] = roll(packed, jnp.where(gz == 0, 120, 127), 1)
+    near = jnp.concatenate([own_z[...], low[384:YROWS2, :], high[384:YROWS2, :]], axis=0)
+    got = jnp.concatenate([far_z[...], far_low[...], far_high[...]], axis=0)
+    got = got + jnp.where(at_face, roll(near, shift, 1), 0.0)
+    pack[...] = roll(got, jnp.where(gz == 0, 120, 127), 1)
     toward = jnp.where(gz == 0, 127, 1)
     lane8 = lanes(8)
     folded = jnp.where(gz == 0, lane8 - 120, 7 - lane8) >= 0
 
-    def tile(index):
+    def tile(index, start=0):
         q, j = divmod(index, PER)
-        return roll(pack[8 * q : 8 * q + 8, :], -9 * j, 1)
+        return roll(pack[start + 8 * q : start + 8 * q + 8, :], -9 * j, 1)
+
+    def along_z(p, t):
+        value = tile(p * 5 + t - 1)
+        if t == 1:
+            value = value + tile(p, ZROWS2)
+        if t == 5:
+            value = value + tile(p, ZROWS2 + end)
+        return value
 
     for p in range(42):
-        for t in range(5):
-            at = p * EXT + 8 * t + 8
-            field[at : at + 8, :] = sol[at : at + 8, :] + jnp.where(folded, tile(p * 5 + t), 0.0)
+        for t in range(1, 6):
+            at = p * EXT + 8 * t
+            value = sol[at : at + 8, :] + jnp.where(folded, along_z(p, t), 0.0)
+            field[at : at + 8, :] = value
     for k, single in enumerate((7, 48)):
         for j in range(6):
-            line[8 * j : 8 * j + 8, :] = jnp.where(folded, tile(210 + 6 * k + j), 0.0)
+            value = tile(210 + 6 * k + j) + tile(42 + j, ZROWS2 + k * end)
+            line[8 * j : 8 * j + 8, :] = jnp.where(folded, value, 0.0)
         at = pl.ds(single, 42, stride=EXT)
         field[at, :] = sol[at, :] + line[0:42, :]
     pack[...] = roll(pack[...], toward, 1)
@@ -657,7 +697,7 @@
 
     for x in range(C):
         for t in range(5):
-            out[x * C + 8 * t : x * C + 8 * t + 8, :] = tile((x + 1) * 5 + t)
+            out[x * C + 8 * t : x * C + 8 * t + 8, :] = along_z(x + 1, t + 1)
     _, sum_a, sum_b = lax.fori_loop(0, C, visit, (flux_x, sum_a, sum_b), unroll=8)
     total_a = jnp.sum(sum_a, axis=0, keepdims=True)
     total_b = jnp.sum(sum_b, axis=0, keepdims=True)
@@ -708,23 +748,27 @@
     def buffer(rows):
         return pltpu.VMEM((rows, CZ), F32)
 
-    part, up, down, edge = call(
-        residual_kernel, (own, YROWS, YROWS, 160), v, h, b,
-        scratch=[buffer(own)] * 4 + [pltpu.SemaphoreType.DMA((4, CHUNKS))],
-        hbm=(0, 1, 2), hbm_out=(0,), limit=56, name="residual", work=2,
-    )
+    up, down = call(
+        strips_kernel, (YROWS, YROWS), guess_field, conduct_field, right_side,
+        scratch=[pltpu.VMEM((C, C, CZ), F32)] * 3 + [pltpu.SemaphoreType.DMA((3, 2))],
+        hbm=(0, 1, 2), limit=56, name="strips", work=2,
+    )
+    part, edge = call(residual_kernel, (own, 160), v, h, b, name="residual", work=2)
     low, high = exchange("gy", up, down)
     pairs, scale_a, scale_b = call(
         prepare_kernel, (own, box, box), eigen, v, h, denom, smem=(0,), name="prepare", work=2
     )
-    part, right, left, faces = call(
-        extend_y_kernel, (C * EXT, XROWS, XROWS, 4 * EXT),
+    right, left, faces = call(
+        extend_y_kernel, (XROWS, XROWS, 4 * EXT),
         flags, part, pairs, up, down, edge, low, high,
         scratch=[buffer(XROWS)] * 2, smem=(0,), name="extend_y", work=1,
     )
     one, two = exchange_x(right, left)
+    inner, part = call(
+        inner_kernel, (38 * EXT, C * EXT),
+        flags, plane, part, up, down, low, high, smem=(0,), name="inner", work=1,
+    )
     (packed,) = call(pack_z_kernel, (ZROWS,), part, pairs, low, high, name="pack_z", work=2)
-    (inner,) = call(inner_kernel, (38 * EXT,), plane, part, name="inner", work=1)
     own_z, fluxes = call(
         extend_x_kernel, (ZROWS, 2 * EXT), flags, packed, faces, one, two, inner,
         smem=(0,), name="extend_x", work=1,
@@ -749,23 +793,25 @@
         rest_kernel, (42 * EXT, 42 * EXT),
         plane, inverse, second_a, second_b, sides, side_strip, name="rest", work=2,
     )
-    sol, strip, up, down = call(
-        fold_x_kernel, (42 * EXT, 42 * EXT, YROWS2, YROWS2),
-        flags, sol, strip, one, two,
-        scratch=[buffer(48)], smem=(0,), alias={1: 0, 2: 1}, name="fold_x", work=1,
+    sol, _, up, down, own_z, across_up, across_down = call(
+        fold_x_kernel, (42 * EXT, 42 * EXT, YROWS2, YROWS2, ZROWS2, 32, 32),
+        flags, sol, strip, one, two, resid,
+        scratch=[buffer(144)], smem=(0,), alias={1: 0, 2: 1}, name="fold_x", work=1,
     )
     low, high = exchange("gy", up, down)
-    sol, _, own_z = call(
-        fold_y_kernel, (42 * EXT, 42 * EXT, ZROWS2),
-        flags, sol, strip, low, high, resid,
-        scratch=[buffer(96)], smem=(0,), alias={1: 0, 2: 1}, name="fold_y", work=1,
-    )
     far_z = swap(own_z)
+    diagonal = [((j, k), (j + 1, 1 - k)) for j in range(n_gy - 1) for k in range(2)]
+    pairs = [(2 * a + b, 2 * c + d) for (a, b), (c, d) in diagonal]
+    far_low = lax.ppermute(across_up, ("gy", "gz"), pairs)
+    far_high = lax.ppermute(across_down, ("gy", "gz"), [(b, a) for a, b in pairs])
+    (sol,) = call(
+        fold_y_kernel, (42 * EXT,), flags, sol, low, high, smem=(0,), alias={1: 0}, name="fold_y", work=1
+    )
     first, last = splits
     field, applied, sums = call(
         apply_kernel, (own, own, lax.axis_size(first)),
-        sol, own_z, far_z, resid, c_x, c_down, c_up, c_z, c_face, h,
-        scratch=[buffer(42 * EXT), buffer(ZROWS2), buffer(48)], name="apply", work=3,
+        sol, low, high, own_z, far_z, far_low, far_high, resid, c_x, c_down, c_up, c_z, c_face, h,
+        scratch=[buffer(42 * EXT), buffer(ZROWS2 + 64), buffer(48)], name="apply", work=3,
     )
     sums = lax.all_to_all(sums, first, 0, 0, tiled=True)
     (sums,) = call(gather_kernel, (lax.axis_size(last),), sums, name="gather")

time: 124 us -> 122 us (0.984)
  waiting for transfers between devices: 33.5 us -> 21 us
  starting transfers between devices: 30.7 us -> 37.7 us
  blocking collectives: 31.6 us -> 33.5 us
    ppermute x4, waiting for transfers between devices: 25.3 us -> 16.5 us  [exchange(): return (lax.ppermute(up, axis, forward), lax.ppermute(down, axis, backward))]
    ppermute x0 -> x2, starting transfers between devices: none -> 5.9 us  [the longest x1 4.61 us: on_device(): far_low = lax.ppermute(across_up, ('gy', 'gz'), pairs)]
    ppermute x2, waiting for transfers between devices: 6.93 us -> 4.17 us  [swap(): return lax.ppermute(value, 'gz', [(0, 1), (1, 0)])]
    all_to_all x1, blocking collectives: 13.5 us -> 15.9 us  [on_device(): sums = lax.all_to_all(sums, last, 0, 0, tiled=True)]
    pallas_call x15 -> x16, Pallas kernels: 26.8 us -> 27.7 us  [call(): pl.pallas_call(body, out_shape=[jax.ShapeDtypeStruct((rows, CZ), F32) for...]
  transfers between devices with their start and end apart: 10 -> 12, of which waited for: 8 -> 6; matrix products, arithmetic and copies ran while one was open for 0% -> 0% of each run, Pallas kernels for 7% -> 10%
where the time goes in v3:
time: 122 us; the launch traced here: 121 us
  starting transfers between devices  37.7 us (31%)
  blocking collectives  33.5 us (27%)
  Pallas kernels  27.7 us (23%)
  waiting for transfers between devices  21 us (17%)
    pallas_call x16, Pallas kernels, call(): pl.pallas_call(body, out_shape=[jax.ShapeDtypeStruct((rows, CZ), F32) for...  27.7 us
    all_to_all x1, blocking collectives, on_device(): sums = lax.all_to_all(sums, first, 0, 0, tiled=True)  17.6 us
    ppermute x4, waiting for transfers between devices, exchange(): return (lax.ppermute(up, axis, forward), lax.ppermute(down, axis, backward))  16.5 us
    all_to_all x1, blocking collectives, on_device(): sums = lax.all_to_all(sums, last, 0, 0, tiled=True)  15.9 us
    ppermute x4, starting transfers between devices, exchange(): return (lax.ppermute(up, axis, forward), lax.ppermute(down, axis, backward))  14.7 us
    ppermute x2, starting transfers between devices, exchange_x(): lax.ppermute(first, gx, pairs[0])  8.9 us
    ppermute x1, starting transfers between devices, on_device(): far_low = lax.ppermute(across_up, ('gy', 'gz'), pairs)  4.61 us
    ppermute x2, starting transfers between devices, swap(): return lax.ppermute(value, 'gz', [(0, 1), (1, 0)])  4.39 us
  transfers between devices with their start and end apart: 12, of which 6 were waited for; matrix products, arithmetic and copies ran while one was open for 0% of the time, Pallas kernels for 10%

profile of v3, /device:TPU:1, one launch (start us, length us, event | category | flops | bytes accessed | tf_op | source)
XLA Modules:
  0.0 121.1 jit_solution(17022001792280433689)
XLA Ops:
  0.7 3.4 %strips.1 = (f32[440,128]{1,0:T(8,128)}, f32[440,128]{1,0:T(8,128)}) custom-call(f32[40,40,128]{2,1,0:T(8,128)} %v_in.1, f32[40,40,128]{2,1,0:T(8,128)} %h_in.1, f32[40,40,128]{2,1,0:T(8,128)} %b_in.1), custom_call_target="tpu_custom_call" | custom-call | flops 2000000000 | bytes 4000000 | tf_op jit(solution)/shard_map/strips/pallas_call | solution.py:110
  4.0 6.6 %collective-permute-start = (f32[440,128]{1,0:T(8,128)}, f32[440,128]{1,0:T(8,128)S(1)}, u32[]{:S(2)}, u32[]{:S(2)}) collective-permute-start(f32[440,128]{1,0:T(8,128)} %get-tuple-element.42.up), channel_id=1, source_target_pairs={{0,2},{2,4},{4,6},{1,3},{3,5},{5,7},{8,10},{10,12},{12,14},{9,11},... | collective-permute-start | bytes 675848 | tf_op jit(solution)/shard_map/ppermute | solution.py:735
  10.7 1.3 %collective-permute-start.1 = (f32[440,128]{1,0:T(8,128)}, f32[440,128]{1,0:T(8,128)S(1)}, u32[]{:S(2)}, u32[]{:S(2)}) collective-permute-start(f32[440,128]{1,0:T(8,128)} %get-tuple-element.43.down), channel_id=1, source_target_pairs={{2,0},{4,2},{6,4},{3,1},{5,3},{7,5},{10,8},{12,10},{14,12},{11,9},... | collective-permute-start | bytes 675848 | tf_op jit(solution)/shard_map/ppermute | solution.py:735
  12.1 1.8 %residual.1 = (f32[1600,128]{1,0:T(8,128)S(1)}, f32[160,128]{1,0:T(8,128)S(1)}) custom-call(f32[1600,128]{1,0:T(8,128)S(1)} %bitcast.27, f32[1600,128]{1,0:T(8,128)S(1)} %bitcast.23, f32[1600,128]{1,0:T(8,128)S(1)} %bitcast.22), custom_call_target="tpu_custom_call" | custom-call | flops 2000000000 | bytes 4000000 | tf_op jit(solution)/shard_map/residual/pallas_call | solution.py:110
  14.1 1.9 %prepare.1 = (f32[1600,128]{1,0:T(8,128)S(1)}, f32[3136,128]{1,0:T(8,128)S(1)}, f32[3136,128]{1,0:T(8,128)S(1)}) custom-call(f32[56]{0:T(128)S(1)} %copy-done.9, f32[1600,128]{1,0:T(8,128)S(1)} %bitcast.28, f32[1600,128]{1,0:T(8,128)S(1)} %bitcast.24, f32[56,256]{1,0:T(8,128)S(1)} %copy-done.7), custom_call_target="tpu_custom_call" | custom-call | flops 2000000000 | bytes 4000000 | tf_op jit(solution)/shard_map/prepare/pallas_call | solution.py:110
  16.0 11.8 %collective-permute-done.1.high = f32[440,128]{1,0:T(8,128)S(1)} collective-permute-done((f32[440,128]{1,0:T(8,128)}, f32[440,128]{1,0:T(8,128)S(1)}, u32[]{:S(2)}, u32[]{:S(2)}) %collective-permute-start.1) | collective-permute-done | bytes 225312 | tf_op jit(solution)/shard_map/ppermute | solution.py:735
  27.8 0.9 extend_y.1
  28.7 4.5 %collective-permute-start.2 = (f32[616,128]{1,0:T(8,128)S(1)}, f32[616,128]{1,0:T(8,128)S(1)}, u32[]{:S(2)}, u32[]{:S(2)}) collective-permute-start(f32[616,128]{1,0:T(8,128)S(1)} %get-tuple-element.48), channel_id=1, source_target_pairs={{8,16},{16,8},{24,32},{32,24},{40,48},{48,40},{56,64},{64,56},{72,... | collective-permute-start | bytes 946184 | tf_op jit(solution)/shard_map/ppermute | solution.py:739
  33.2 1.9 %collective-permute-start.3 = (f32[616,128]{1,0:T(8,128)S(1)}, f32[616,128]{1,0:T(8,128)S(1)}, u32[]{:S(2)}, u32[]{:S(2)}) collective-permute-start(f32[616,128]{1,0:T(8,128)S(1)} %get-tuple-element.49), channel_id=1, source_target_pairs={{0,8},{8,0},{16,24},{24,16},{32,40},{40,32},{48,56},{56,48},{64,72... | collective-permute-start | bytes 946184 | tf_op jit(solution)/shard_map/ppermute | solution.py:739
  35.1 1.1 inner.1
  36.2 1.4 %pack_z.1.packed = f32[280,128]{1,0:T(8,128)S(1)} custom-call(f32[2240,128]{1,0:T(8,128)S(1)} %get-tuple-element.44.part, f32[1600,128]{1,0:T(8,128)S(1)} %get-tuple-element.45.vh, f32[440,128]{1,0:T(8,128)S(1)} %collective-permute-done.low, f32[440,128]{1,0:T(8,128)S(1)} %collective-permute-done.1.high), custom_call_target="tpu_custom_call" | custom-call | flops 2000000000 | bytes 4000000 | tf_op jit(solution)/shard_map/pack_z/pallas_call | solution.py:110
  37.8 0.7 extend_x.1
  38.5 1.9 %collective-permute-start.4 = (f32[280,128]{1,0:T(8,128)S(1)}, f32[280,128]{1,0:T(8,128)S(1)}, u32[]{:S(2)}, u32[]{:S(2)}) collective-permute-start(f32[280,128]{1,0:T(8,128)S(1)} %get-tuple-element.51.own_z), channel_id=1, source_target_pairs={{0,1},{1,0},{2,3},{3,2},{4,5},{5,4},{6,7},{7,6},{8,9},{9,8},{10,11... | collective-permute-start | bytes 430088 | tf_op jit(solution)/shard_map/ppermute | solution.py:742
  40.5 1.7 %forward.2.main = f32[3136,128]{1,0:T(8,128)S(1)} custom-call(f32[5]{0:T(128)S(1)} %convert_element_type.3.flags, bf16[56,192]{1,0:T(8,128)(2,1)S(1)} %copy-done.8, f32[2240,128]{1,0:T(8,128)S(1)} %get-tuple-element.44.part, f32[2128,128]{1,0:T(8,128)S(1)} %get-tuple-element.50.inner, f32[112,128]{1,0:T(8,128)S(1)} %get-tuple-element.52.fluxes, ...), custom_call_target="tpu_custom_call" | custom-call | flops 2000000000 | bytes 4000000 | tf_op jit(solution)/shard_map/forward/pallas_call | solution.py:110
  42.2 3.3 %collective-permute-done.4.far_z = f32[280,128]{1,0:T(8,128)S(1)} collective-permute-done((f32[280,128]{1,0:T(8,128)S(1)}, f32[280,128]{1,0:T(8,128)S(1)}, u32[]{:S(2)}, u32[]{:S(2)}) %collective-permute-start.4) | collective-permute-done | bytes 143392 | tf_op jit(solution)/shard_map/ppermute | solution.py:742
  45.5 6.2 %solve.1 = (f32[3136,128]{1,0:T(8,128)S(1)}, f32[3136,128]{1,0:T(8,128)S(1)}, f32[1008,128]{1,0:T(8,128)S(1)}, f32[1008,128]{1,0:T(8,128)S(1)}, f32[544,128]{1,0:T(8,128)S(1)}, /*index=5*/f32[544,128]{1,0:T(8,128)S(1)}) custom-call(f32[5]{0:T(128)S(1)} %convert_element_type.3.flags, f32[280,128]{1,0:T(8,128)S(1)} %get-tuple-element.51.own_z, ...), custom_call_target="tpu_custom_call" | custom-call | flops 6000000000 | bytes 12000000 | tf_op jit(solution)/shard_map/solve/pallas_call | solution.py:110
  51.7 4.4 %collective-permute-start.5 = (f32[544,128]{1,0:T(8,128)S(1)}, f32[544,128]{1,0:T(8,128)S(1)}, u32[]{:S(2)}, u32[]{:S(2)}) collective-permute-start(f32[544,128]{1,0:T(8,128)S(1)} %get-tuple-element.61), channel_id=1, source_target_pairs={{8,16},{16,8},{24,32},{32,24},{40,48},{48,40},{56,64},{64,56},{72,... | collective-permute-start | bytes 835592 | tf_op jit(solution)/shard_map/ppermute | solution.py:739
  56.1 1.9 %collective-permute-start.6 = (f32[544,128]{1,0:T(8,128)S(1)}, f32[544,128]{1,0:T(8,128)S(1)}, u32[]{:S(2)}, u32[]{:S(2)}) collective-permute-start(f32[544,128]{1,0:T(8,128)S(1)} %get-tuple-element.62), channel_id=1, source_target_pairs={{0,8},{8,0},{16,24},{24,16},{32,40},{40,32},{48,56},{56,48},{64,72... | collective-permute-start | bytes 835592 | tf_op jit(solution)/shard_map/ppermute | solution.py:739
  58.0 1.7 %rest.1 = (f32[2352,128]{1,0:T(8,128)S(1)}, f32[2352,128]{1,0:T(8,128)S(1)}) custom-call(bf16[56,192]{1,0:T(8,128)(2,1)S(1)} %copy-done.8, bf16[2,768,256]{2,1,0:T(8,128)(2,1)S(1)} %copy-done.5, f32[3136,128]{1,0:T(8,128)S(1)} %get-tuple-element.55.second_a, f32[3136,128]{1,0:T(8,128)S(1)} %get-tuple-element.56.second_b, ...), custom_call_target="tpu_custom_call" | custom-call | flops 2000000000 | bytes 4000000 | tf_op jit(solution)/shard_map/rest/pallas_call | solution.py:110
  59.8 1.4 %own.1 = (f32[1600,128]{1,0:T(8,128)S(1)}, f32[1640,128]{1,0:T(8,128)S(1)}, f32[1600,128]{1,0:T(8,128)S(1)}, f32[1600,128]{1,0:T(8,128)S(1)}, f32[1600,128]{1,0:T(8,128)S(1)}, /*index=5*/f32[1600,128]{1,0:T(8,128)S(1)}) custom-call(f32[5]{0:T(128)S(1)} %convert_element_type.3.flags, f32[1600,128]{1,0:T(8,128)S(1)} %bitcast.25, ...), custom_call_target="tpu_custom_call" | custom-call | flops 2000000000 | bytes 4000000 | tf_op jit(solution)/shard_map/own/pallas_call | solution.py:110
  61.2 1.2 %fold_x.1 = (f32[2352,128]{1,0:T(8,128)S(1)}, f32[2352,128]{1,0:T(8,128)S(1)}, f32[416,128]{1,0:T(8,128)S(1)}, f32[416,128]{1,0:T(8,128)S(1)}, f32[128,128]{1,0:...) custom-call(f32[5]{0:T(128)S(1)} %convert_element_type.3.flags, ...), custom_call_target="tpu_custom_call", output_to_operand_aliasing={{0}: (1, {}), {1}: (2, {})} | custom-call | flops 1000000000 | bytes 2000000 | tf_op jit(solution)/shard_map/fold_x/pallas_call | solution.py:110
  62.4 5.5 %collective-permute-start.7 = (f32[416,128]{1,0:T(8,128)S(1)}, f32[416,128]{1,0:T(8,128)S(1)}, u32[]{:S(2)}, u32[]{:S(2)}) collective-permute-start(f32[416,128]{1,0:T(8,128)S(1)} %get-tuple-element.65), channel_id=1, source_target_pairs={{0,2},{2,4},{4,6},{1,3},{3,5},{5,7},{8,10},{10,12},{12,14},{9,11},... | collective-permute-start | bytes 638984 | tf_op jit(solution)/shard_map/ppermute | solution.py:735
  67.9 1.3 %collective-permute-start.8 = (f32[416,128]{1,0:T(8,128)S(1)}, f32[416,128]{1,0:T(8,128)S(1)}, u32[]{:S(2)}, u32[]{:S(2)}) collective-permute-start(f32[416,128]{1,0:T(8,128)S(1)} %get-tuple-element.66), channel_id=1, source_target_pairs={{2,0},{4,2},{6,4},{3,1},{5,3},{7,5},{10,8},{12,10},{14,12},{11,9},... | collective-permute-start | bytes 638984 | tf_op jit(solution)/shard_map/ppermute | solution.py:735
  69.2 4.6 %collective-permute-start.10 = (f32[32,128]{1,0:T(8,128)S(1)}, f32[32,128]{1,0:T(8,128)S(1)}, u32[]{:S(2)}, u32[]{:S(2)}) collective-permute-start(f32[32,128]{1,0:T(8,128)S(1)} %get-tuple-element.68), channel_id=1, source_target_pairs={{0,3},{1,2},{2,5},{3,4},{4,7},{5,6},{8,11},{9,10},{10,13},{11,12},... | collective-permute-start | bytes 49160 | tf_op jit(solution)/shard_map/ppermute | solution.py:805
  73.8 1.3 %collective-permute-start.11 = (f32[32,128]{1,0:T(8,128)S(1)}, f32[32,128]{1,0:T(8,128)S(1)}, u32[]{:S(2)}, u32[]{:S(2)}) collective-permute-start(f32[32,128]{1,0:T(8,128)S(1)} %get-tuple-element.69), channel_id=1, source_target_pairs={{3,0},{2,1},{5,2},{4,3},{7,4},{6,5},{11,8},{10,9},{13,10},{12,11},... | collective-permute-start | bytes 49160 | tf_op jit(solution)/shard_map/ppermute | solution.py:806
  75.1 2.5 %collective-permute-start.9 = (f32[128,128]{1,0:T(8,128)S(1)}, f32[128,128]{1,0:T(8,128)S(1)}, u32[]{:S(2)}, u32[]{:S(2)}) collective-permute-start(f32[128,128]{1,0:T(8,128)S(1)} %get-tuple-element.67.own_z), channel_id=1, source_target_pairs={{0,1},{1,0},{2,3},{3,2},{4,5},{5,4},{6,7},{7,6},{8,9},{9,8},{10,11... | collective-permute-start | bytes 196616 | tf_op jit(solution)/shard_map/ppermute | solution.py:742
  77.6 4.7 %collective-permute-done.8.high = f32[416,128]{1,0:T(8,128)S(1)} collective-permute-done((f32[416,128]{1,0:T(8,128)S(1)}, f32[416,128]{1,0:T(8,128)S(1)}, u32[]{:S(2)}, u32[]{:S(2)}) %collective-permute-start.8) | collective-permute-done | bytes 213024 | tf_op jit(solution)/shard_map/ppermute | solution.py:735
  83.1 0.9 collective-permute-done.9.far_z
  83.9 2.2 %apply.1 = (f32[1600,128]{1,0:T(8,128)S(1)}, f32[1600,128]{1,0:T(8,128)S(1)}, f32[32,128]{1,0:T(8,128)S(1)}) custom-call(f32[2352,128]{1,0:T(8,128)S(1)} %fold_y.1.sol, f32[416,128]{1,0:T(8,128)S(1)} %collective-permute-done.7.low, f32[416,128]{1,0:T(8,128)S(1)} %collective-permute-done.8.high, f32[128,128]{1,0:T(8,128)S(1)} %get-tuple-element.67.own_z, ...), custom_call_target="tpu_custom_call" | custom-call | flops 3000000000 | bytes 6000000 | tf_op jit(solution)/shard_map/apply/pallas_call | solution.py:110
  86.2 17.6 %all_to_all.22 = f32[32,1,128]{2,1,0:T(1,128)S(1)} all-to-all(f32[32,1,128]{2,1,0:T(1,128)S(1)} %bitcast.20), channel_id=1, replica_groups=mesh['gx_x'=4,'gx_y'=8,'gx_c'=2,'gy'=4,'gz'=2] {'gx_x','gx_y'}, dimensions={0} | all-to-all | bytes 32768 | tf_op jit(solution)/shard_map/all_to_all | solution.py:816
  103.8 15.9 %all_to_all.23 = f32[16,1,128]{2,1,0:T(1,128)S(1)} all-to-all(f32[16,1,128]{2,1,0:T(1,128)S(1)} %bitcast.19), channel_id=1, replica_groups=mesh['gx_x'=4,'gx_y'=8,'gx_c'=2,'gy'=4,'gz'=2] {'gx_c','gy','gz'}, dimensions={0} | all-to-all | bytes 16384 | tf_op jit(solution)/shard_map/all_to_all | solution.py:818
  119.7 1.4 %update.1 = (f32[1600,128]{1,0:T(8,128)}, f32[1600,128]{1,0:T(8,128)}) custom-call(f32[16,128]{1,0:T(8,128)S(1)} %bitcast.21, f32[1600,128]{1,0:T(8,128)S(1)} %bitcast.29, f32[1600,128]{1,0:T(8,128)S(1)} %get-tuple-element.63._.resid, f32[1600,128]{1,0:T(8,128)S(1)} %get-tuple-element.76.field, f32[1600,128]{1,0:T(8,128)S(1)} %get-tuple-element.77.applied), custom_call_target="tpu_custom_call" | custom-call | flops 2000000000 | bytes 4000000 | tf_op jit(solution)/shard_map/update/pallas_call | solution.py:110
  (32 shorter events, 1.1 us)
Async XLA Ops:
  0.6 11.4 %copy-start.1 = (f32[40,40,128]{2,1,0:T(8,128)S(1)}, f32[40,40,128]{2,1,0:T(8,128)}, u32[]{:S(2)}) copy-start(f32[40,40,128]{2,1,0:T(8,128)} %h_in.1) | copy-start | bytes 2457604
  0.6 11.4 %copy-start.2 = (f32[40,40,128]{2,1,0:T(8,128)S(1)}, f32[40,40,128]{2,1,0:T(8,128)}, u32[]{:S(2)}) copy-start(f32[40,40,128]{2,1,0:T(8,128)} %v_in.1) | copy-start | bytes 2457604
  0.6 11.4 %copy-start = (f32[40,40,128]{2,1,0:T(8,128)S(1)}, f32[40,40,128]{2,1,0:T(8,128)}, u32[]{:S(2)}) copy-start(f32[40,40,128]{2,1,0:T(8,128)} %b_in.1) | copy-start | bytes 2457604
  4.0 11.9 %collective-permute-start = (f32[440,128]{1,0:T(8,128)}, f32[440,128]{1,0:T(8,128)S(1)}, u32[]{:S(2)}, u32[]{:S(2)}) collective-permute-start(f32[440,128]{1,0:T(8,128)} %get-tuple-element.42.up), channel_id=1, source_target_pairs={{0,2},{2,4},{4,6},{1,3},{3,5},{5,7},{8,10},{10,12},{12,14},{9,11},... | collective-permute-start | bytes 675848 | tf_op jit(solution)/shard_map/ppermute | solution.py:735
  10.7 17.1 %collective-permute-start.1 = (f32[440,128]{1,0:T(8,128)}, f32[440,128]{1,0:T(8,128)S(1)}, u32[]{:S(2)}, u32[]{:S(2)}) collective-permute-start(f32[440,128]{1,0:T(8,128)} %get-tuple-element.43.down), channel_id=1, source_target_pairs={{2,0},{4,2},{6,4},{3,1},{5,3},{7,5},{10,8},{12,10},{14,12},{11,9},... | collective-permute-start | bytes 675848 | tf_op jit(solution)/shard_map/ppermute | solution.py:735
  12.0 2.0 %copy-start.7 = (f32[56,256]{1,0:T(8,128)S(1)}, f32[56,256]{1,0:T(8,128)}, u32[]{:S(2)}) copy-start(f32[56,256]{1,0:T(8,128)} %constant.49.clone.denom) | copy-start | bytes 172036
  12.0 2.0 %copy-start.9 = (f32[56]{0:T(128)S(1)}, f32[56]{0:T(128)}, u32[]{:S(2)}) copy-start(f32[56]{0:T(128)} %constant.48.clone.eigen) | copy-start | bytes 676
  14.1 13.7 %copy-start.3 = (f32[440,128]{1,0:T(8,128)S(1)}, f32[440,128]{1,0:T(8,128)}, u32[]{:S(2)}) copy-start(f32[440,128]{1,0:T(8,128)} %get-tuple-element.42.up) | copy-start | bytes 675844
  14.1 13.7 %copy-start.4 = (f32[440,128]{1,0:T(8,128)S(1)}, f32[440,128]{1,0:T(8,128)}, u32[]{:S(2)}) copy-start(f32[440,128]{1,0:T(8,128)} %get-tuple-element.43.down) | copy-start | bytes 675844
  27.8 7.3 %copy-start.8 = (bf16[56,192]{1,0:T(8,128)(2,1)S(1)}, bf16[56,192]{1,0:T(8,128)(2,1)}, u32[]{:S(2)}) copy-start(bf16[56,192]{1,0:T(8,128)(2,1)} %constant.50.clone.plane) | copy-start | bytes 64516
  28.7 9.1 %collective-permute-start.2 = (f32[616,128]{1,0:T(8,128)S(1)}, f32[616,128]{1,0:T(8,128)S(1)}, u32[]{:S(2)}, u32[]{:S(2)}) collective-permute-start(f32[616,128]{1,0:T(8,128)S(1)} %get-tuple-element.48), channel_id=1, source_target_pairs={{8,16},{16,8},{24,32},{32,24},{40,48},{48,40},{56,64},{64,56},{72,... | collective-permute-start | bytes 946184 | tf_op jit(solution)/shard_map/ppermute | solution.py:739
  33.2 4.6 %collective-permute-start.3 = (f32[616,128]{1,0:T(8,128)S(1)}, f32[616,128]{1,0:T(8,128)S(1)}, u32[]{:S(2)}, u32[]{:S(2)}) collective-permute-start(f32[616,128]{1,0:T(8,128)S(1)} %get-tuple-element.49), channel_id=1, source_target_pairs={{0,8},{8,0},{16,24},{24,16},{32,40},{40,32},{48,56},{56,48},{64,72... | collective-permute-start | bytes 946184 | tf_op jit(solution)/shard_map/ppermute | solution.py:739
  38.5 6.9 %collective-permute-start.4 = (f32[280,128]{1,0:T(8,128)S(1)}, f32[280,128]{1,0:T(8,128)S(1)}, u32[]{:S(2)}, u32[]{:S(2)}) collective-permute-start(f32[280,128]{1,0:T(8,128)S(1)} %get-tuple-element.51.own_z), channel_id=1, source_target_pairs={{0,1},{1,0},{2,3},{3,2},{4,5},{5,4},{6,7},{7,6},{8,9},{9,8},{10,11... | collective-permute-start | bytes 430088 | tf_op jit(solution)/shard_map/ppermute | solution.py:742
  40.5 5.0 %copy-start.5 = (bf16[2,768,256]{2,1,0:T(8,128)(2,1)S(1)}, bf16[2,768,256]{2,1,0:T(8,128)(2,1)}, u32[]{:S(2)}) copy-start(bf16[2,768,256]{2,1,0:T(8,128)(2,1)} %constant.52.clone.inverse) | copy-start | bytes 2359300
  40.5 5.0 %copy-start.6 = (bf16[2,768,256]{2,1,0:T(8,128)(2,1)S(1)}, bf16[2,768,256]{2,1,0:T(8,128)(2,1)}, u32[]{:S(2)}) copy-start(bf16[2,768,256]{2,1,0:T(8,128)(2,1)} %constant.51.clone.forward) | copy-start | bytes 2359300
  51.7 9.5 %collective-permute-start.5 = (f32[544,128]{1,0:T(8,128)S(1)}, f32[544,128]{1,0:T(8,128)S(1)}, u32[]{:S(2)}, u32[]{:S(2)}) collective-permute-start(f32[544,128]{1,0:T(8,128)S(1)} %get-tuple-element.61), channel_id=1, source_target_pairs={{8,16},{16,8},{24,32},{32,24},{40,48},{48,40},{56,64},{64,56},{72,... | collective-permute-start | bytes 835592 | tf_op jit(solution)/shard_map/ppermute | solution.py:739
  56.1 5.1 %collective-permute-start.6 = (f32[544,128]{1,0:T(8,128)S(1)}, f32[544,128]{1,0:T(8,128)S(1)}, u32[]{:S(2)}, u32[]{:S(2)}) collective-permute-start(f32[544,128]{1,0:T(8,128)S(1)} %get-tuple-element.62), channel_id=1, source_target_pairs={{0,8},{8,0},{16,24},{24,16},{32,40},{40,32},{48,56},{56,48},{64,72... | collective-permute-start | bytes 835592 | tf_op jit(solution)/shard_map/ppermute | solution.py:739
  62.4 15.2 %collective-permute-start.7 = (f32[416,128]{1,0:T(8,128)S(1)}, f32[416,128]{1,0:T(8,128)S(1)}, u32[]{:S(2)}, u32[]{:S(2)}) collective-permute-start(f32[416,128]{1,0:T(8,128)S(1)} %get-tuple-element.65), channel_id=1, source_target_pairs={{0,2},{2,4},{4,6},{1,3},{3,5},{5,7},{8,10},{10,12},{12,14},{9,11},... | collective-permute-start | bytes 638984 | tf_op jit(solution)/shard_map/ppermute | solution.py:735
  67.9 14.4 %collective-permute-start.8 = (f32[416,128]{1,0:T(8,128)S(1)}, f32[416,128]{1,0:T(8,128)S(1)}, u32[]{:S(2)}, u32[]{:S(2)}) collective-permute-start(f32[416,128]{1,0:T(8,128)S(1)} %get-tuple-element.66), channel_id=1, source_target_pairs={{2,0},{4,2},{6,4},{3,1},{5,3},{7,5},{10,8},{12,10},{14,12},{11,9},... | collective-permute-start | bytes 638984 | tf_op jit(solution)/shard_map/ppermute | solution.py:735
  69.2 13.7 %collective-permute-start.10 = (f32[32,128]{1,0:T(8,128)S(1)}, f32[32,128]{1,0:T(8,128)S(1)}, u32[]{:S(2)}, u32[]{:S(2)}) collective-permute-start(f32[32,128]{1,0:T(8,128)S(1)} %get-tuple-element.68), channel_id=1, source_target_pairs={{0,3},{1,2},{2,5},{3,4},{4,7},{5,6},{8,11},{9,10},{10,13},{11,12},... | collective-permute-start | bytes 49160 | tf_op jit(solution)/shard_map/ppermute | solution.py:805
  73.8 9.2 %collective-permute-start.11 = (f32[32,128]{1,0:T(8,128)S(1)}, f32[32,128]{1,0:T(8,128)S(1)}, u32[]{:S(2)}, u32[]{:S(2)}) collective-permute-start(f32[32,128]{1,0:T(8,128)S(1)} %get-tuple-element.69), channel_id=1, source_target_pairs={{3,0},{2,1},{5,2},{4,3},{7,4},{6,5},{11,8},{10,9},{13,10},{12,11},... | collective-permute-start | bytes 49160 | tf_op jit(solution)/shard_map/ppermute | solution.py:806
  75.1 8.8 %collective-permute-start.9 = (f32[128,128]{1,0:T(8,128)S(1)}, f32[128,128]{1,0:T(8,128)S(1)}, u32[]{:S(2)}, u32[]{:S(2)}) collective-permute-start(f32[128,128]{1,0:T(8,128)S(1)} %get-tuple-element.67.own_z), channel_id=1, source_target_pairs={{0,1},{1,0},{2,3},{3,2},{4,5},{5,4},{6,7},{7,6},{8,9},{9,8},{10,11... | collective-permute-start | bytes 196616 | tf_op jit(solution)/shard_map/ppermute | solution.py:742

commit v4 on v3

--- a/solution.py
+++ b/solution.py
@@ -105,14 +105,13 @@
     return rows_at(index * 8, 8)
 
 
-def call(body, out_rows, *args, scratch=(), limit=16, name=None, smem=(), hbm=(), hbm_out=(), alias=(), work=0):
+def call(body, out_rows, *args, scratch=(), limit=16, name=None, smem=(), hbm=(), work=0):
     place = {**{i: SMEM for i in smem}, **{i: HBM for i in hbm}}
     return pl.pallas_call(
         body,
         out_shape=[jax.ShapeDtypeStruct((rows, CZ), F32) for rows in out_rows],
         in_specs=[place.get(i, VMEM) for i in range(len(args))],
-        out_specs=[HBM if i in hbm_out else VMEM for i in range(len(out_rows))],
-        input_output_aliases=dict(alias),
+        out_specs=[VMEM] * len(out_rows),
         scratch_shapes=list(scratch),
         compiler_params=pltpu.CompilerParams(vmem_limit_bytes=limit * 2**20),
         cost_estimate=pl.CostEstimate(
@@ -573,22 +572,22 @@
     return roll(message[rows_at(at + 8 * q, 8), :], -9 * (index - q * PER), 1)
 
 
-def fold_x_kernel(
-    flags, sol, strip, one, two, _, out, out_strip, up, down, across, across_up, across_down, line
-):
+def fold_x_kernel(flags, sol, strip, one, two, _, out, out_strip, up, down, line):
     size = 42 * EXT
     narrow = lanes(8) < 9
     before, after = by_parity(flags, one, two)
-    out[0 : 9 * EXT, :] = out[0 : 9 * EXT, :] + before(0, 9 * EXT)
     tail = 33 * EXT
-    out[tail:size, :] = out[tail:size, :] + after(0, 9 * EXT)
+    out[0 : 9 * EXT, :] = sol[0 : 9 * EXT, :] + before(0, 9 * EXT)
+    out[9 * EXT : tail, :] = sol[9 * EXT : tail, :]
+    out[tail:size, :] = sol[tail:size, :] + after(0, 9 * EXT)
+    out_strip[9 * EXT : tail, :] = strip[9 * EXT : tail, :]
     packs = [side(9 * EXT, XROWS2) for side in (before, after)]
 
     for j in range(63):
         q, i = divmod(j, PER)
         for pack, at in ((packs[0], 8 * j), (packs[1], tail + 8 * j)):
             value = jnp.where(narrow, roll(pack[8 * q : 8 * q + 8], -9 * i, 1), 0.0)
-            out_strip[at : at + 8, :] = out_strip[at : at + 8, :] + value
+            out_strip[at : at + 8, :] = strip[at : at + 8, :] + value
 
     for array in (out, out_strip):
         array[0:EXT, :] = array[0:EXT, :] * flags[0]
@@ -604,69 +603,80 @@
         values = [out_strip[p * EXT + 8 * tile : p * EXT + 8 * tile + 8, :] for p in range(42)]
         values += [line[8 * j : 8 * j + 8, :] for j in range(6)]
         pack_tiles(message, 384, values)
-    across_up[...] = up[384:416, :]
-    across_down[...] = down[384:416, :]
+
+
+def pack_own_kernel(flags, strip, message, line):
     values = []
     for p in range(42):
         for t in range(1, 6):
             at = p * EXT + 8 * t
-            values.append(out_strip[at : at + 8, :])
+            values.append(strip[at : at + 8, :])
     for k, single in enumerate((7, 48)):
-        at = 48 * (k + 1)
+        at = 48 * k
         line[at + 40 : at + 48, :] = jnp.zeros((8, CZ), F32)
-        line[at : at + 42, :] = out_strip[pl.ds(single, 42, stride=EXT), :] * flags[2 + k]
+        line[at : at + 42, :] = strip[pl.ds(single, 42, stride=EXT), :] * flags[2 + k]
         values += [line[at + 8 * j : at + 8 * j + 8, :] for j in range(6)]
-    pack_tiles(across, 0, values)
+    pack_tiles(message, 0, values)
+
+
+def add_y_kernel(flags, packed, low, high, message):
+    place = lax.div(lanes(8), 9)
+    rows = [packed[8 * q : 8 * q + 8, :] for q in range(ZROWS2 // 8)]
+
+    def add(source, index, target, factor=None):
+        q, j = divmod(index, PER)
+        to, k = divmod(target, PER)
+        value = roll(jnp.where(place == j, source[384 + 8 * q : 392 + 8 * q, :], 0.0), 9 * (k - j), 1)
+        rows[to] = rows[to] + (value if factor is None else value * factor)
+
+    for source, t, single, flag in ((low, 1, 210, 2), (high, 5, 216, 3)):
+        for p in range(42):
+            add(source, p, p * 5 + t - 1)
+        for j in range(6):
+            add(source, 42 + j, single + j, flags[flag])
+    for q, value in enumerate(rows):
+        message[8 * q : 8 * q + 8, :] = value
 
 
 def fold_y_kernel(flags, sol, low, high, out):
     for p in range(42):
         for message, tile in ((low, 1), (high, 5)):
             at = p * EXT + 8 * tile
-            out[at : at + 8, :] = out[at : at + 8, :] + message[8 * p : 8 * p + 8, :]
+            out[at : at + 8, :] = sol[at : at + 8, :] + message[8 * p : 8 * p + 8, :]
+        at = p * EXT
+        out[at : at + 8, :] = sol[at : at + 8, :]
+        out[at + 16 : at + 40, :] = sol[at + 16 : at + 40, :]
+        out[at + 48 : at + 56, :] = sol[at + 48 : at + 56, :]
     for k, (single, message) in enumerate(((7, low), (48, high))):
         at = pl.ds(single, 42, stride=EXT)
         out[at, :] = (out[at, :] + message[336:378, :]) * flags[2 + k]
 
 
 def apply_kernel(
-    sol, low, high, own_z, far_z, far_low, far_high, resid, c_x, c_down, c_up, c_z, c_face, h,
+    sol, own_z, far_z, resid, c_x, c_down, c_up, c_z, c_face, h,
     out, applied, sums, field, pack, line,
 ):
     gz = lax.axis_index("gz")
-    end = YROWS2 - 384
-    lane = lanes(ZROWS2 + 2 * end)
+    lane = lanes(ZROWS2)
     at_face = lax.rem(lane, 9) == jnp.where(gz == 0, 8, 0)
     shift = jnp.where(gz == 0, 7, 121)
-    near = jnp.concatenate([own_z[...], low[384:YROWS2, :], high[384:YROWS2, :]], axis=0)
-    got = jnp.concatenate([far_z[...], far_low[...], far_high[...]], axis=0)
-    got = got + jnp.where(at_face, roll(near, shift, 1), 0.0)
-    pack[...] = roll(got, jnp.where(gz == 0, 120, 127), 1)
+    packed = far_z[...] + jnp.where(at_face, roll(own_z[...], shift, 1), 0.0)
+    pack[...] = roll(packed, jnp.where(gz == 0, 120, 127), 1)
     toward = jnp.where(gz == 0, 127, 1)
     lane8 = lanes(8)
     folded = jnp.where(gz == 0, lane8 - 120, 7 - lane8) >= 0
 
-    def tile(index, start=0):
+    def tile(index):
         q, j = divmod(index, PER)
-        return roll(pack[start + 8 * q : start + 8 * q + 8, :], -9 * j, 1)
-
-    def along_z(p, t):
-        value = tile(p * 5 + t - 1)
-        if t == 1:
-            value = value + tile(p, ZROWS2)
-        if t == 5:
-            value = value + tile(p, ZROWS2 + end)
-        return value
+        return roll(pack[8 * q : 8 * q + 8, :], -9 * j, 1)
 
     for p in range(42):
-        for t in range(1, 6):
-            at = p * EXT + 8 * t
-            value = sol[at : at + 8, :] + jnp.where(folded, along_z(p, t), 0.0)
-            field[at : at + 8, :] = value
+        for t in range(5):
+            at = p * EXT + 8 * t + 8
+            field[at : at + 8, :] = sol[at : at + 8, :] + jnp.where(folded, tile(p * 5 + t), 0.0)
     for k, single in enumerate((7, 48)):
         for j in range(6):
-            value = tile(210 + 6 * k + j) + tile(42 + j, ZROWS2 + k * end)
-            line[8 * j : 8 * j + 8, :] = jnp.where(folded, value, 0.0)
+            line[8 * j : 8 * j + 8, :] = jnp.where(folded, tile(210 + 6 * k + j), 0.0)
         at = pl.ds(single, 42, stride=EXT)
         field[at, :] = sol[at, :] + line[0:42, :]
     pack[...] = roll(pack[...], toward, 1)
@@ -697,7 +707,7 @@
 
     for x in range(C):
         for t in range(5):
-            out[x * C + 8 * t : x * C + 8 * t + 8, :] = along_z(x + 1, t + 1)
+            out[x * C + 8 * t : x * C + 8 * t + 8, :] = tile((x + 1) * 5 + t)
     _, sum_a, sum_b = lax.fori_loop(0, C, visit, (flux_x, sum_a, sum_b), unroll=8)
     total_a = jnp.sum(sum_a, axis=0, keepdims=True)
     total_b = jnp.sum(sum_b, axis=0, keepdims=True)
@@ -793,25 +803,28 @@
         rest_kernel, (42 * EXT, 42 * EXT),
         plane, inverse, second_a, second_b, sides, side_strip, name="rest", work=2,
     )
-    sol, _, up, down, own_z, across_up, across_down = call(
-        fold_x_kernel, (42 * EXT, 42 * EXT, YROWS2, YROWS2, ZROWS2, 32, 32),
+    sol, strip, up, down = call(
+        fold_x_kernel, (42 * EXT, 42 * EXT, YROWS2, YROWS2),
         flags, sol, strip, one, two, resid,
-        scratch=[buffer(144)], smem=(0,), alias={1: 0, 2: 1}, name="fold_x", work=1,
+        scratch=[buffer(48)], smem=(0,), name="fold_x", work=1,
     )
     low, high = exchange("gy", up, down)
+    (packed,) = call(
+        pack_own_kernel, (ZROWS2,), flags, strip,
+        scratch=[buffer(96)], smem=(0,), name="pack_own", work=1,
+    )
+    (own_z,) = call(
+        add_y_kernel, (ZROWS2,), flags, packed, low, high, smem=(0,), name="add_y", work=1
+    )
     far_z = swap(own_z)
-    diagonal = [((j, k), (j + 1, 1 - k)) for j in range(n_gy - 1) for k in range(2)]
-    pairs = [(2 * a + b, 2 * c + d) for (a, b), (c, d) in diagonal]
-    far_low = lax.ppermute(across_up, ("gy", "gz"), pairs)
-    far_high = lax.ppermute(across_down, ("gy", "gz"), [(b, a) for a, b in pairs])
     (sol,) = call(
-        fold_y_kernel, (42 * EXT,), flags, sol, low, high, smem=(0,), alias={1: 0}, name="fold_y", work=1
+        fold_y_kernel, (42 * EXT,), flags, sol, low, high, smem=(0,), name="fold_y", work=1
     )
     first, last = splits
     field, applied, sums = call(
         apply_kernel, (own, own, lax.axis_size(first)),
-        sol, low, high, own_z, far_z, far_low, far_high, resid, c_x, c_down, c_up, c_z, c_face, h,
-        scratch=[buffer(42 * EXT), buffer(ZROWS2 + 64), buffer(48)], name="apply", work=3,
+        sol, own_z, far_z, resid, c_x, c_down, c_up, c_z, c_face, h,
+        scratch=[buffer(42 * EXT), buffer(ZROWS2), buffer(48)], name="apply", work=3,
     )
     sums = lax.all_to_all(sums, first, 0, 0, tiled=True)
     (sums,) = call(gather_kernel, (lax.axis_size(last),), sums, name="gather")

time: 122 us -> 123 us (level)
  waiting for transfers between devices: 21 us -> 29.8 us
  starting transfers between devices: 37.7 us -> 31.3 us
  blocking collectives: 33.5 us -> 31.2 us
  Pallas kernels: 27.7 us -> 29 us
    ppermute x4, waiting for transfers between devices: 16.5 us -> 24 us  [exchange(): return (lax.ppermute(up, axis, forward), lax.ppermute(down, axis, backward))]
    ppermute x2 -> x0, starting transfers between devices: 5.9 us -> none  [the longest x1 4.61 us: on_device(): far_low = lax.ppermute(across_up, ('gy', 'gz'), pairs)]
    all_to_all x1, blocking collectives: 15.9 us -> 13.6 us  [on_device(): sums = lax.all_to_all(sums, last, 0, 0, tiled=True)]
    ppermute x2, waiting for transfers between devices: 4.17 us -> 5.69 us  [swap(): return lax.ppermute(value, 'gz', [(0, 1), (1, 0)])]
    pallas_call x16 -> x18, Pallas kernels: 27.7 us -> 29 us  [call(): pl.pallas_call(body, out_shape=[jax.ShapeDtypeStruct((rows, CZ), F32) for...]
  transfers between devices with their start and end apart: 12 -> 10, of which waited for: 6 -> 6; matrix products, arithmetic and copies ran while one was open for 0% -> 0% of each run, Pallas kernels for 10% -> 10%
where the time goes in v4:
time: 123 us
  starting transfers between devices  31.3 us (25%)
  blocking collectives  31.2 us (25%)
  waiting for transfers between devices  29.8 us (24%)
  Pallas kernels  29 us (24%)
    pallas_call x18, Pallas kernels, call(): pl.pallas_call(body, out_shape=[jax.ShapeDtypeStruct((rows, CZ), F32) for...  29 us
    ppermute x4, waiting for transfers between devices, exchange(): return (lax.ppermute(up, axis, forward), lax.ppermute(down, axis, backward))  24 us
    all_to_all x1, blocking collectives, on_device(): sums = lax.all_to_all(sums, first, 0, 0, tiled=True)  17.7 us
    ppermute x4, starting transfers between devices, exchange(): return (lax.ppermute(up, axis, forward), lax.ppermute(down, axis, backward))  14.7 us
    all_to_all x1, blocking collectives, on_device(): sums = lax.all_to_all(sums, last, 0, 0, tiled=True)  13.6 us
    ppermute x2, starting transfers between devices, exchange_x(): lax.ppermute(first, gx, pairs[0])  8.92 us
    ppermute x2, waiting for transfers between devices, swap(): return lax.ppermute(value, 'gz', [(0, 1), (1, 0)])  5.69 us
    ppermute x2, starting transfers between devices, exchange_x(): lax.ppermute(second, gx, pairs[1])  3.84 us
  transfers between devices with their start and end apart: 10, of which 6 were waited for; matrix products, arithmetic and copies ran while one was open for 0% of the time, Pallas kernels for 10%

profile of v4, /device:TPU:1, one launch (start us, length us, event | category | flops | bytes accessed | tf_op | source)
XLA Modules:
  0.0 122.5 jit_solution(4300195715678808602)
XLA Ops:
  0.7 3.4 %strips.1 = (f32[440,128]{1,0:T(8,128)}, f32[440,128]{1,0:T(8,128)}) custom-call(f32[40,40,128]{2,1,0:T(8,128)} %v_in.1, f32[40,40,128]{2,1,0:T(8,128)} %h_in.1, f32[40,40,128]{2,1,0:T(8,128)} %b_in.1), custom_call_target="tpu_custom_call" | custom-call | flops 2000000000 | bytes 4000000 | tf_op jit(solution)/shard_map/strips/pallas_call | solution.py:110
  4.0 6.6 %collective-permute-start = (f32[440,128]{1,0:T(8,128)}, f32[440,128]{1,0:T(8,128)S(1)}, u32[]{:S(2)}, u32[]{:S(2)}) collective-permute-start(f32[440,128]{1,0:T(8,128)} %get-tuple-element.40.up), channel_id=1, source_target_pairs={{0,2},{2,4},{4,6},{1,3},{3,5},{5,7},{8,10},{10,12},{12,14},{9,11},... | collective-permute-start | bytes 675848 | tf_op jit(solution)/shard_map/ppermute | solution.py:745
  10.7 1.3 %collective-permute-start.1 = (f32[440,128]{1,0:T(8,128)}, f32[440,128]{1,0:T(8,128)S(1)}, u32[]{:S(2)}, u32[]{:S(2)}) collective-permute-start(f32[440,128]{1,0:T(8,128)} %get-tuple-element.41.down), channel_id=1, source_target_pairs={{2,0},{4,2},{6,4},{3,1},{5,3},{7,5},{10,8},{12,10},{14,12},{11,9},... | collective-permute-start | bytes 675848 | tf_op jit(solution)/shard_map/ppermute | solution.py:745
  12.1 1.8 %residual.1 = (f32[1600,128]{1,0:T(8,128)S(1)}, f32[160,128]{1,0:T(8,128)S(1)}) custom-call(f32[1600,128]{1,0:T(8,128)S(1)} %bitcast.27, f32[1600,128]{1,0:T(8,128)S(1)} %bitcast.23, f32[1600,128]{1,0:T(8,128)S(1)} %bitcast.22), custom_call_target="tpu_custom_call" | custom-call | flops 2000000000 | bytes 4000000 | tf_op jit(solution)/shard_map/residual/pallas_call | solution.py:110
  14.1 1.9 %prepare.1 = (f32[1600,128]{1,0:T(8,128)S(1)}, f32[3136,128]{1,0:T(8,128)S(1)}, f32[3136,128]{1,0:T(8,128)S(1)}) custom-call(f32[56]{0:T(128)S(1)} %copy-done.9, f32[1600,128]{1,0:T(8,128)S(1)} %bitcast.28, f32[1600,128]{1,0:T(8,128)S(1)} %bitcast.24, f32[56,256]{1,0:T(8,128)S(1)} %copy-done.7), custom_call_target="tpu_custom_call" | custom-call | flops 2000000000 | bytes 4000000 | tf_op jit(solution)/shard_map/prepare/pallas_call | solution.py:110
  16.0 11.8 %collective-permute-done.1.high = f32[440,128]{1,0:T(8,128)S(1)} collective-permute-done((f32[440,128]{1,0:T(8,128)}, f32[440,128]{1,0:T(8,128)S(1)}, u32[]{:S(2)}, u32[]{:S(2)}) %collective-permute-start.1) | collective-permute-done | bytes 225312 | tf_op jit(solution)/shard_map/ppermute | solution.py:745
  27.8 0.9 extend_y.1
  28.7 4.5 %collective-permute-start.2 = (f32[616,128]{1,0:T(8,128)S(1)}, f32[616,128]{1,0:T(8,128)S(1)}, u32[]{:S(2)}, u32[]{:S(2)}) collective-permute-start(f32[616,128]{1,0:T(8,128)S(1)} %get-tuple-element.46), channel_id=1, source_target_pairs={{8,16},{16,8},{24,32},{32,24},{40,48},{48,40},{56,64},{64,56},{72,... | collective-permute-start | bytes 946184 | tf_op jit(solution)/shard_map/ppermute | solution.py:749
  33.2 1.9 %collective-permute-start.3 = (f32[616,128]{1,0:T(8,128)S(1)}, f32[616,128]{1,0:T(8,128)S(1)}, u32[]{:S(2)}, u32[]{:S(2)}) collective-permute-start(f32[616,128]{1,0:T(8,128)S(1)} %get-tuple-element.47), channel_id=1, source_target_pairs={{0,8},{8,0},{16,24},{24,16},{32,40},{40,32},{48,56},{56,48},{64,72... | collective-permute-start | bytes 946184 | tf_op jit(solution)/shard_map/ppermute | solution.py:749
  35.1 1.1 inner.1
  36.2 1.4 %pack_z.1.packed = f32[280,128]{1,0:T(8,128)S(1)} custom-call(f32[2240,128]{1,0:T(8,128)S(1)} %get-tuple-element.42.part, f32[1600,128]{1,0:T(8,128)S(1)} %get-tuple-element.43.vh, f32[440,128]{1,0:T(8,128)S(1)} %collective-permute-done.low, f32[440,128]{1,0:T(8,128)S(1)} %collective-permute-done.1.high), custom_call_target="tpu_custom_call" | custom-call | flops 2000000000 | bytes 4000000 | tf_op jit(solution)/shard_map/pack_z/pallas_call | solution.py:110
  37.8 0.7 extend_x.1
  38.5 1.9 %collective-permute-start.4 = (f32[280,128]{1,0:T(8,128)S(1)}, f32[280,128]{1,0:T(8,128)S(1)}, u32[]{:S(2)}, u32[]{:S(2)}) collective-permute-start(f32[280,128]{1,0:T(8,128)S(1)} %get-tuple-element.49.own_z), channel_id=1, source_target_pairs={{0,1},{1,0},{2,3},{3,2},{4,5},{5,4},{6,7},{7,6},{8,9},{9,8},{10,11... | collective-permute-start | bytes 430088 | tf_op jit(solution)/shard_map/ppermute | solution.py:752
  40.5 1.7 %forward.2.main = f32[3136,128]{1,0:T(8,128)S(1)} custom-call(f32[5]{0:T(128)S(1)} %convert_element_type.3.flags, bf16[56,192]{1,0:T(8,128)(2,1)S(1)} %copy-done.8, f32[2240,128]{1,0:T(8,128)S(1)} %get-tuple-element.42.part, f32[2128,128]{1,0:T(8,128)S(1)} %get-tuple-element.48.inner, f32[112,128]{1,0:T(8,128)S(1)} %get-tuple-element.50.fluxes, ...), custom_call_target="tpu_custom_call" | custom-call | flops 2000000000 | bytes 4000000 | tf_op jit(solution)/shard_map/forward/pallas_call | solution.py:110
  42.2 3.3 %collective-permute-done.4.far_z = f32[280,128]{1,0:T(8,128)S(1)} collective-permute-done((f32[280,128]{1,0:T(8,128)S(1)}, f32[280,128]{1,0:T(8,128)S(1)}, u32[]{:S(2)}, u32[]{:S(2)}) %collective-permute-start.4) | collective-permute-done | bytes 143392 | tf_op jit(solution)/shard_map/ppermute | solution.py:752
  45.4 6.3 %solve.1 = (f32[3136,128]{1,0:T(8,128)S(1)}, f32[3136,128]{1,0:T(8,128)S(1)}, f32[1008,128]{1,0:T(8,128)S(1)}, f32[1008,128]{1,0:T(8,128)S(1)}, f32[544,128]{1,0:T(8,128)S(1)}, /*index=5*/f32[544,128]{1,0:T(8,128)S(1)}) custom-call(f32[5]{0:T(128)S(1)} %convert_element_type.3.flags, f32[280,128]{1,0:T(8,128)S(1)} %get-tuple-element.49.own_z, ...), custom_call_target="tpu_custom_call" | custom-call | flops 6000000000 | bytes 12000000 | tf_op jit(solution)/shard_map/solve/pallas_call | solution.py:110
  51.7 4.4 %collective-permute-start.5 = (f32[544,128]{1,0:T(8,128)S(1)}, f32[544,128]{1,0:T(8,128)S(1)}, u32[]{:S(2)}, u32[]{:S(2)}) collective-permute-start(f32[544,128]{1,0:T(8,128)S(1)} %get-tuple-element.59), channel_id=1, source_target_pairs={{8,16},{16,8},{24,32},{32,24},{40,48},{48,40},{56,64},{64,56},{72,... | collective-permute-start | bytes 835592 | tf_op jit(solution)/shard_map/ppermute | solution.py:749
  56.1 1.9 %collective-permute-start.6 = (f32[544,128]{1,0:T(8,128)S(1)}, f32[544,128]{1,0:T(8,128)S(1)}, u32[]{:S(2)}, u32[]{:S(2)}) collective-permute-start(f32[544,128]{1,0:T(8,128)S(1)} %get-tuple-element.60), channel_id=1, source_target_pairs={{0,8},{8,0},{16,24},{24,16},{32,40},{40,32},{48,56},{56,48},{64,72... | collective-permute-start | bytes 835592 | tf_op jit(solution)/shard_map/ppermute | solution.py:749
  58.1 1.8 %rest.1 = (f32[2352,128]{1,0:T(8,128)S(1)}, f32[2352,128]{1,0:T(8,128)S(1)}) custom-call(bf16[56,192]{1,0:T(8,128)(2,1)S(1)} %copy-done.8, bf16[2,768,256]{2,1,0:T(8,128)(2,1)S(1)} %copy-done.5, f32[3136,128]{1,0:T(8,128)S(1)} %get-tuple-element.53.second_a, f32[3136,128]{1,0:T(8,128)S(1)} %get-tuple-element.54.second_b, ...), custom_call_target="tpu_custom_call" | custom-call | flops 2000000000 | bytes 4000000 | tf_op jit(solution)/shard_map/rest/pallas_call | solution.py:110
  59.9 1.4 %own.1 = (f32[1600,128]{1,0:T(8,128)S(1)}, f32[1640,128]{1,0:T(8,128)S(1)}, f32[1600,128]{1,0:T(8,128)S(1)}, f32[1600,128]{1,0:T(8,128)S(1)}, f32[1600,128]{1,0:T(8,128)S(1)}, /*index=5*/f32[1600,128]{1,0:T(8,128)S(1)}) custom-call(f32[5]{0:T(128)S(1)} %convert_element_type.3.flags, f32[1600,128]{1,0:T(8,128)S(1)} %bitcast.25, ...), custom_call_target="tpu_custom_call" | custom-call | flops 2000000000 | bytes 4000000 | tf_op jit(solution)/shard_map/own/pallas_call | solution.py:110
  61.3 1.0 fold_x.1
  62.3 5.5 %collective-permute-start.7 = (f32[416,128]{1,0:T(8,128)S(1)}, f32[416,128]{1,0:T(8,128)S(1)}, u32[]{:S(2)}, u32[]{:S(2)}) collective-permute-start(f32[416,128]{1,0:T(8,128)S(1)} %get-tuple-element.63), channel_id=1, source_target_pairs={{0,2},{2,4},{4,6},{1,3},{3,5},{5,7},{8,10},{10,12},{12,14},{9,11},... | collective-permute-start | bytes 638984 | tf_op jit(solution)/shard_map/ppermute | solution.py:745
  67.8 1.3 %collective-permute-start.8 = (f32[416,128]{1,0:T(8,128)S(1)}, f32[416,128]{1,0:T(8,128)S(1)}, u32[]{:S(2)}, u32[]{:S(2)}) collective-permute-start(f32[416,128]{1,0:T(8,128)S(1)} %get-tuple-element.64), channel_id=1, source_target_pairs={{2,0},{4,2},{6,4},{3,1},{5,3},{7,5},{10,8},{12,10},{14,12},{11,9},... | collective-permute-start | bytes 638984 | tf_op jit(solution)/shard_map/ppermute | solution.py:745
  69.1 0.8 pack_own.1.packed
  69.9 2.0 %collective-permute-done.7.low = f32[416,128]{1,0:T(8,128)S(1)} collective-permute-done((f32[416,128]{1,0:T(8,128)S(1)}, f32[416,128]{1,0:T(8,128)S(1)}, u32[]{:S(2)}, u32[]{:S(2)}) %collective-permute-start.7) | collective-permute-done | bytes 213024 | tf_op jit(solution)/shard_map/ppermute | solution.py:745
  71.9 10.1 %collective-permute-done.8.high = f32[416,128]{1,0:T(8,128)S(1)} collective-permute-done((f32[416,128]{1,0:T(8,128)S(1)}, f32[416,128]{1,0:T(8,128)S(1)}, u32[]{:S(2)}, u32[]{:S(2)}) %collective-permute-start.8) | collective-permute-done | bytes 213024 | tf_op jit(solution)/shard_map/ppermute | solution.py:745
  82.8 1.9 %collective-permute-start.9 = (f32[128,128]{1,0:T(8,128)S(1)}, f32[128,128]{1,0:T(8,128)S(1)}, u32[]{:S(2)}, u32[]{:S(2)}) collective-permute-start(f32[128,128]{1,0:T(8,128)S(1)} %add_y.1.own_z), channel_id=1, source_target_pairs={{0,1},{1,0},{2,3},{3,2},{4,5},{5,4},{6,7},{7,6},{8,9},{9,8},{10,11... | collective-permute-start | bytes 196616 | tf_op jit(solution)/shard_map/ppermute | solution.py:752
  85.4 2.4 %collective-permute-done.9.far_z = f32[128,128]{1,0:T(8,128)S(1)} collective-permute-done((f32[128,128]{1,0:T(8,128)S(1)}, f32[128,128]{1,0:T(8,128)S(1)}, u32[]{:S(2)}, u32[]{:S(2)}) %collective-permute-start.9) | collective-permute-done | bytes 65568 | tf_op jit(solution)/shard_map/ppermute | solution.py:752
  87.8 2.1 %apply.1 = (f32[1600,128]{1,0:T(8,128)S(1)}, f32[1600,128]{1,0:T(8,128)S(1)}, f32[32,128]{1,0:T(8,128)S(1)}) custom-call(f32[2352,128]{1,0:T(8,128)S(1)} %fold_y.1.sol, f32[128,128]{1,0:T(8,128)S(1)} %add_y.1.own_z, f32[128,128]{1,0:T(8,128)S(1)} %collective-permute-done.9.far_z, f32[1600,128]{1,0:T(8,128)S(1)} %get-tuple-element.61._.resid, ...), custom_call_target="tpu_custom_call" | custom-call | flops 3000000000 | bytes 6000000 | tf_op jit(solution)/shard_map/apply/pallas_call | solution.py:110
  89.9 17.7 %all_to_all.22 = f32[32,1,128]{2,1,0:T(1,128)S(1)} all-to-all(f32[32,1,128]{2,1,0:T(1,128)S(1)} %bitcast.20), channel_id=1, replica_groups=mesh['gx_x'=4,'gx_y'=8,'gx_c'=2,'gy'=4,'gz'=2] {'gx_x','gx_y'}, dimensions={0} | all-to-all | bytes 32768 | tf_op jit(solution)/shard_map/all_to_all | solution.py:829
  107.6 13.6 %all_to_all.23 = f32[16,1,128]{2,1,0:T(1,128)S(1)} all-to-all(f32[16,1,128]{2,1,0:T(1,128)S(1)} %bitcast.19), channel_id=1, replica_groups=mesh['gx_x'=4,'gx_y'=8,'gx_c'=2,'gy'=4,'gz'=2] {'gx_c','gy','gz'}, dimensions={0} | all-to-all | bytes 16384 | tf_op jit(solution)/shard_map/all_to_all | solution.py:831
  121.1 1.4 %update.1 = (f32[1600,128]{1,0:T(8,128)}, f32[1600,128]{1,0:T(8,128)}) custom-call(f32[16,128]{1,0:T(8,128)S(1)} %bitcast.21, f32[1600,128]{1,0:T(8,128)S(1)} %bitcast.29, f32[1600,128]{1,0:T(8,128)S(1)} %get-tuple-element.61._.resid, f32[1600,128]{1,0:T(8,128)S(1)} %get-tuple-element.72.field, f32[1600,128]{1,0:T(8,128)S(1)} %get-tuple-element.73.applied), custom_call_target="tpu_custom_call" | custom-call | flops 2000000000 | bytes 4000000 | tf_op jit(solution)/shard_map/update/pallas_call | solution.py:110
  (30 shorter events, 1.7 us)
Async XLA Ops:
  0.6 11.4 %copy-start.1 = (f32[40,40,128]{2,1,0:T(8,128)S(1)}, f32[40,40,128]{2,1,0:T(8,128)}, u32[]{:S(2)}) copy-start(f32[40,40,128]{2,1,0:T(8,128)} %h_in.1) | copy-start | bytes 2457604
  0.6 11.4 %copy-start.2 = (f32[40,40,128]{2,1,0:T(8,128)S(1)}, f32[40,40,128]{2,1,0:T(8,128)}, u32[]{:S(2)}) copy-start(f32[40,40,128]{2,1,0:T(8,128)} %v_in.1) | copy-start | bytes 2457604
  0.6 11.4 %copy-start = (f32[40,40,128]{2,1,0:T(8,128)S(1)}, f32[40,40,128]{2,1,0:T(8,128)}, u32[]{:S(2)}) copy-start(f32[40,40,128]{2,1,0:T(8,128)} %b_in.1) | copy-start | bytes 2457604
  4.0 11.9 %collective-permute-start = (f32[440,128]{1,0:T(8,128)}, f32[440,128]{1,0:T(8,128)S(1)}, u32[]{:S(2)}, u32[]{:S(2)}) collective-permute-start(f32[440,128]{1,0:T(8,128)} %get-tuple-element.40.up), channel_id=1, source_target_pairs={{0,2},{2,4},{4,6},{1,3},{3,5},{5,7},{8,10},{10,12},{12,14},{9,11},... | collective-permute-start | bytes 675848 | tf_op jit(solution)/shard_map/ppermute | solution.py:745
  10.7 17.1 %collective-permute-start.1 = (f32[440,128]{1,0:T(8,128)}, f32[440,128]{1,0:T(8,128)S(1)}, u32[]{:S(2)}, u32[]{:S(2)}) collective-permute-start(f32[440,128]{1,0:T(8,128)} %get-tuple-element.41.down), channel_id=1, source_target_pairs={{2,0},{4,2},{6,4},{3,1},{5,3},{7,5},{10,8},{12,10},{14,12},{11,9},... | collective-permute-start | bytes 675848 | tf_op jit(solution)/shard_map/ppermute | solution.py:745
  12.0 2.0 %copy-start.7 = (f32[56,256]{1,0:T(8,128)S(1)}, f32[56,256]{1,0:T(8,128)}, u32[]{:S(2)}) copy-start(f32[56,256]{1,0:T(8,128)} %constant.49.clone.denom) | copy-start | bytes 172036
  12.0 2.0 %copy-start.9 = (f32[56]{0:T(128)S(1)}, f32[56]{0:T(128)}, u32[]{:S(2)}) copy-start(f32[56]{0:T(128)} %constant.48.clone.eigen) | copy-start | bytes 676
  14.1 13.7 %copy-start.3 = (f32[440,128]{1,0:T(8,128)S(1)}, f32[440,128]{1,0:T(8,128)}, u32[]{:S(2)}) copy-start(f32[440,128]{1,0:T(8,128)} %get-tuple-element.40.up) | copy-start | bytes 675844
  14.1 13.7 %copy-start.4 = (f32[440,128]{1,0:T(8,128)S(1)}, f32[440,128]{1,0:T(8,128)}, u32[]{:S(2)}) copy-start(f32[440,128]{1,0:T(8,128)} %get-tuple-element.41.down) | copy-start | bytes 675844
  27.8 7.3 %copy-start.8 = (bf16[56,192]{1,0:T(8,128)(2,1)S(1)}, bf16[56,192]{1,0:T(8,128)(2,1)}, u32[]{:S(2)}) copy-start(bf16[56,192]{1,0:T(8,128)(2,1)} %constant.50.clone.plane) | copy-start | bytes 64516
  28.7 9.1 %collective-permute-start.2 = (f32[616,128]{1,0:T(8,128)S(1)}, f32[616,128]{1,0:T(8,128)S(1)}, u32[]{:S(2)}, u32[]{:S(2)}) collective-permute-start(f32[616,128]{1,0:T(8,128)S(1)} %get-tuple-element.46), channel_id=1, source_target_pairs={{8,16},{16,8},{24,32},{32,24},{40,48},{48,40},{56,64},{64,56},{72,... | collective-permute-start | bytes 946184 | tf_op jit(solution)/shard_map/ppermute | solution.py:749
  33.2 4.6 %collective-permute-start.3 = (f32[616,128]{1,0:T(8,128)S(1)}, f32[616,128]{1,0:T(8,128)S(1)}, u32[]{:S(2)}, u32[]{:S(2)}) collective-permute-start(f32[616,128]{1,0:T(8,128)S(1)} %get-tuple-element.47), channel_id=1, source_target_pairs={{0,8},{8,0},{16,24},{24,16},{32,40},{40,32},{48,56},{56,48},{64,72... | collective-permute-start | bytes 946184 | tf_op jit(solution)/shard_map/ppermute | solution.py:749
  38.5 6.9 %collective-permute-start.4 = (f32[280,128]{1,0:T(8,128)S(1)}, f32[280,128]{1,0:T(8,128)S(1)}, u32[]{:S(2)}, u32[]{:S(2)}) collective-permute-start(f32[280,128]{1,0:T(8,128)S(1)} %get-tuple-element.49.own_z), channel_id=1, source_target_pairs={{0,1},{1,0},{2,3},{3,2},{4,5},{5,4},{6,7},{7,6},{8,9},{9,8},{10,11... | collective-permute-start | bytes 430088 | tf_op jit(solution)/shard_map/ppermute | solution.py:752
  40.5 5.0 %copy-start.5 = (bf16[2,768,256]{2,1,0:T(8,128)(2,1)S(1)}, bf16[2,768,256]{2,1,0:T(8,128)(2,1)}, u32[]{:S(2)}) copy-start(bf16[2,768,256]{2,1,0:T(8,128)(2,1)} %constant.52.clone.inverse) | copy-start | bytes 2359300
  40.5 5.0 %copy-start.6 = (bf16[2,768,256]{2,1,0:T(8,128)(2,1)S(1)}, bf16[2,768,256]{2,1,0:T(8,128)(2,1)}, u32[]{:S(2)}) copy-start(bf16[2,768,256]{2,1,0:T(8,128)(2,1)} %constant.51.clone.forward) | copy-start | bytes 2359300
  51.7 9.6 %collective-permute-start.5 = (f32[544,128]{1,0:T(8,128)S(1)}, f32[544,128]{1,0:T(8,128)S(1)}, u32[]{:S(2)}, u32[]{:S(2)}) collective-permute-start(f32[544,128]{1,0:T(8,128)S(1)} %get-tuple-element.59), channel_id=1, source_target_pairs={{8,16},{16,8},{24,32},{32,24},{40,48},{48,40},{56,64},{64,56},{72,... | collective-permute-start | bytes 835592 | tf_op jit(solution)/shard_map/ppermute | solution.py:749
  56.1 5.1 %collective-permute-start.6 = (f32[544,128]{1,0:T(8,128)S(1)}, f32[544,128]{1,0:T(8,128)S(1)}, u32[]{:S(2)}, u32[]{:S(2)}) collective-permute-start(f32[544,128]{1,0:T(8,128)S(1)} %get-tuple-element.60), channel_id=1, source_target_pairs={{0,8},{8,0},{16,24},{24,16},{32,40},{40,32},{48,56},{56,48},{64,72... | collective-permute-start | bytes 835592 | tf_op jit(solution)/shard_map/ppermute | solution.py:749
  62.3 9.6 %collective-permute-start.7 = (f32[416,128]{1,0:T(8,128)S(1)}, f32[416,128]{1,0:T(8,128)S(1)}, u32[]{:S(2)}, u32[]{:S(2)}) collective-permute-start(f32[416,128]{1,0:T(8,128)S(1)} %get-tuple-element.63), channel_id=1, source_target_pairs={{0,2},{2,4},{4,6},{1,3},{3,5},{5,7},{8,10},{10,12},{12,14},{9,11},... | collective-permute-start | bytes 638984 | tf_op jit(solution)/shard_map/ppermute | solution.py:745
  67.8 14.3 %collective-permute-start.8 = (f32[416,128]{1,0:T(8,128)S(1)}, f32[416,128]{1,0:T(8,128)S(1)}, u32[]{:S(2)}, u32[]{:S(2)}) collective-permute-start(f32[416,128]{1,0:T(8,128)S(1)} %get-tuple-element.64), channel_id=1, source_target_pairs={{2,0},{4,2},{6,4},{3,1},{5,3},{7,5},{10,8},{12,10},{14,12},{11,9},... | collective-permute-start | bytes 638984 | tf_op jit(solution)/shard_map/ppermute | solution.py:745
  82.8 5.0 %collective-permute-start.9 = (f32[128,128]{1,0:T(8,128)S(1)}, f32[128,128]{1,0:T(8,128)S(1)}, u32[]{:S(2)}, u32[]{:S(2)}) collective-permute-start(f32[128,128]{1,0:T(8,128)S(1)} %add_y.1.own_z), channel_id=1, source_target_pairs={{0,1},{1,0},{2,3},{3,2},{4,5},{5,4},{6,7},{7,6},{8,9},{9,8},{10,11... | collective-permute-start | bytes 196616 | tf_op jit(solution)/shard_map/ppermute | solution.py:752

commit v5 on v3

--- a/solution.py
+++ b/solution.py
@@ -105,14 +105,13 @@
     return rows_at(index * 8, 8)
 
 
-def call(body, out_rows, *args, scratch=(), limit=16, name=None, smem=(), hbm=(), hbm_out=(), alias=(), work=0):
+def call(body, out_rows, *args, scratch=(), limit=16, name=None, smem=(), hbm=(), work=0):
     place = {**{i: SMEM for i in smem}, **{i: HBM for i in hbm}}
     return pl.pallas_call(
         body,
         out_shape=[jax.ShapeDtypeStruct((rows, CZ), F32) for rows in out_rows],
         in_specs=[place.get(i, VMEM) for i in range(len(args))],
-        out_specs=[HBM if i in hbm_out else VMEM for i in range(len(out_rows))],
-        input_output_aliases=dict(alias),
+        out_specs=[VMEM] * len(out_rows),
         scratch_shapes=list(scratch),
         compiler_params=pltpu.CompilerParams(vmem_limit_bytes=limit * 2**20),
         cost_estimate=pl.CostEstimate(
@@ -574,21 +573,23 @@
 
 
 def fold_x_kernel(
-    flags, sol, strip, one, two, _, out, out_strip, up, down, across, across_up, across_down, line
+    flags, sol, strip, one, two, _, out, up, down, across, across_up, across_down, out_strip, line
 ):
     size = 42 * EXT
     narrow = lanes(8) < 9
     before, after = by_parity(flags, one, two)
-    out[0 : 9 * EXT, :] = out[0 : 9 * EXT, :] + before(0, 9 * EXT)
     tail = 33 * EXT
-    out[tail:size, :] = out[tail:size, :] + after(0, 9 * EXT)
+    out[0 : 9 * EXT, :] = sol[0 : 9 * EXT, :] + before(0, 9 * EXT)
+    out[9 * EXT : tail, :] = sol[9 * EXT : tail, :]
+    out[tail:size, :] = sol[tail:size, :] + after(0, 9 * EXT)
+    out_strip[9 * EXT : tail, :] = strip[9 * EXT : tail, :]
     packs = [side(9 * EXT, XROWS2) for side in (before, after)]
 
     for j in range(63):
         q, i = divmod(j, PER)
         for pack, at in ((packs[0], 8 * j), (packs[1], tail + 8 * j)):
             value = jnp.where(narrow, roll(pack[8 * q : 8 * q + 8], -9 * i, 1), 0.0)
-            out_strip[at : at + 8, :] = out_strip[at : at + 8, :] + value
+            out_strip[at : at + 8, :] = strip[at : at + 8, :] + value
 
     for array in (out, out_strip):
         array[0:EXT, :] = array[0:EXT, :] * flags[0]
@@ -623,7 +624,11 @@
     for p in range(42):
         for message, tile in ((low, 1), (high, 5)):
             at = p * EXT + 8 * tile
-            out[at : at + 8, :] = out[at : at + 8, :] + message[8 * p : 8 * p + 8, :]
+            out[at : at + 8, :] = sol[at : at + 8, :] + message[8 * p : 8 * p + 8, :]
+        at = p * EXT
+        out[at : at + 8, :] = sol[at : at + 8, :]
+        out[at + 16 : at + 40, :] = sol[at + 16 : at + 40, :]
+        out[at + 48 : at + 56, :] = sol[at + 48 : at + 56, :]
     for k, (single, message) in enumerate(((7, low), (48, high))):
         at = pl.ds(single, 42, stride=EXT)
         out[at, :] = (out[at, :] + message[336:378, :]) * flags[2 + k]
@@ -793,10 +798,10 @@
         rest_kernel, (42 * EXT, 42 * EXT),
         plane, inverse, second_a, second_b, sides, side_strip, name="rest", work=2,
     )
-    sol, _, up, down, own_z, across_up, across_down = call(
-        fold_x_kernel, (42 * EXT, 42 * EXT, YROWS2, YROWS2, ZROWS2, 32, 32),
+    sol, up, down, own_z, across_up, across_down = call(
+        fold_x_kernel, (42 * EXT, YROWS2, YROWS2, ZROWS2, 32, 32),
         flags, sol, strip, one, two, resid,
-        scratch=[buffer(144)], smem=(0,), alias={1: 0, 2: 1}, name="fold_x", work=1,
+        scratch=[buffer(42 * EXT), buffer(144)], smem=(0,), name="fold_x", work=1,
     )
     low, high = exchange("gy", up, down)
     far_z = swap(own_z)
@@ -805,7 +810,7 @@
     far_low = lax.ppermute(across_up, ("gy", "gz"), pairs)
     far_high = lax.ppermute(across_down, ("gy", "gz"), [(b, a) for a, b in pairs])
     (sol,) = call(
-        fold_y_kernel, (42 * EXT,), flags, sol, low, high, smem=(0,), alias={1: 0}, name="fold_y", work=1
+        fold_y_kernel, (42 * EXT,), flags, sol, low, high, smem=(0,), name="fold_y", work=1
     )
     first, last = splits
     field, applied, sums = call(
@@ -825,7 +830,7 @@
     if n_gx == 64:
         mesh = Mesh(mesh.devices.reshape(4, 8, 2, n_gy, n_gz), ("gx_x", "gx_y", "gx_c", "gy", "gz"))
         gx = ("gx_x", "gx_y", "gx_c")
-        splits = (("gx_x", "gx_y"), ("gx_c", "gy", "gz"))
+        splits = (("gx_c", "gy", "gz"), ("gx_x", "gx_y"))
     else:
         gx = "gx"
         splits = (("gx",), ("gy", "gz"))

time: 122 us -> 120 us (0.984)
  blocking collectives: 33.5 us -> 32 us
    all_to_all x1, blocking collectives: 17.6 us -> 13.4 us  [on_device(): sums = lax.all_to_all(sums, first, 0, 0, tiled=True)]
    all_to_all x1, blocking collectives: 15.9 us -> 18.7 us  [on_device(): sums = lax.all_to_all(sums, last, 0, 0, tiled=True)]
where the time goes in v5:
time: 120 us
  starting transfers between devices  37.8 us (31%)
  blocking collectives  32 us (27%)
  Pallas kernels  28 us (23%)
  waiting for transfers between devices  20.9 us (17%)
    pallas_call x16, Pallas kernels, call(): pl.pallas_call(body, out_shape=[jax.ShapeDtypeStruct((rows, CZ), F32) for...  28 us
    all_to_all x1, blocking collectives, on_device(): sums = lax.all_to_all(sums, last, 0, 0, tiled=True)  18.7 us
    ppermute x4, waiting for transfers between devices, exchange(): return (lax.ppermute(up, axis, forward), lax.ppermute(down, axis, backward))  16.5 us
    ppermute x4, starting transfers between devices, exchange(): return (lax.ppermute(up, axis, forward), lax.ppermute(down, axis, backward))  14.7 us
    all_to_all x1, blocking collectives, on_device(): sums = lax.all_to_all(sums, first, 0, 0, tiled=True)  13.4 us
    ppermute x2, starting transfers between devices, exchange_x(): lax.ppermute(first, gx, pairs[0])  8.92 us
    ppermute x1, starting transfers between devices, on_device(): far_low = lax.ppermute(across_up, ('gy', 'gz'), pairs)  4.62 us
    ppermute x2, starting transfers between devices, swap(): return lax.ppermute(value, 'gz', [(0, 1), (1, 0)])  4.38 us
  transfers between devices with their start and end apart: 12, of which 6 were waited for; matrix products, arithmetic and copies ran while one was open for 0% of the time, Pallas kernels for 10%

profile of v5, /device:TPU:1, one launch (start us, length us, event | category | flops | bytes accessed | tf_op | source)
XLA Modules:
  0.0 119.8 jit_solution(755278529185194394)
XLA Ops:
  0.7 3.4 %strips.1 = (f32[440,128]{1,0:T(8,128)}, f32[440,128]{1,0:T(8,128)}) custom-call(f32[40,40,128]{2,1,0:T(8,128)} %v_in.1, f32[40,40,128]{2,1,0:T(8,128)} %h_in.1, f32[40,40,128]{2,1,0:T(8,128)} %b_in.1), custom_call_target="tpu_custom_call" | custom-call | flops 2000000000 | bytes 4000000 | tf_op jit(solution)/shard_map/strips/pallas_call | solution.py:110
  4.0 6.6 %collective-permute-start = (f32[440,128]{1,0:T(8,128)}, f32[440,128]{1,0:T(8,128)S(1)}, u32[]{:S(2)}, u32[]{:S(2)}) collective-permute-start(f32[440,128]{1,0:T(8,128)} %get-tuple-element.42.up), channel_id=1, source_target_pairs={{0,2},{2,4},{4,6},{1,3},{3,5},{5,7},{8,10},{10,12},{12,14},{9,11},... | collective-permute-start | bytes 675848 | tf_op jit(solution)/shard_map/ppermute | solution.py:740
  10.7 1.3 %collective-permute-start.1 = (f32[440,128]{1,0:T(8,128)}, f32[440,128]{1,0:T(8,128)S(1)}, u32[]{:S(2)}, u32[]{:S(2)}) collective-permute-start(f32[440,128]{1,0:T(8,128)} %get-tuple-element.43.down), channel_id=1, source_target_pairs={{2,0},{4,2},{6,4},{3,1},{5,3},{7,5},{10,8},{12,10},{14,12},{11,9},... | collective-permute-start | bytes 675848 | tf_op jit(solution)/shard_map/ppermute | solution.py:740
  12.1 1.8 %residual.1 = (f32[1600,128]{1,0:T(8,128)S(1)}, f32[160,128]{1,0:T(8,128)S(1)}) custom-call(f32[1600,128]{1,0:T(8,128)S(1)} %bitcast.27, f32[1600,128]{1,0:T(8,128)S(1)} %bitcast.23, f32[1600,128]{1,0:T(8,128)S(1)} %bitcast.22), custom_call_target="tpu_custom_call" | custom-call | flops 2000000000 | bytes 4000000 | tf_op jit(solution)/shard_map/residual/pallas_call | solution.py:110
  14.1 1.9 %prepare.1 = (f32[1600,128]{1,0:T(8,128)S(1)}, f32[3136,128]{1,0:T(8,128)S(1)}, f32[3136,128]{1,0:T(8,128)S(1)}) custom-call(f32[56]{0:T(128)S(1)} %copy-done.9, f32[1600,128]{1,0:T(8,128)S(1)} %bitcast.28, f32[1600,128]{1,0:T(8,128)S(1)} %bitcast.24, f32[56,256]{1,0:T(8,128)S(1)} %copy-done.7), custom_call_target="tpu_custom_call" | custom-call | flops 2000000000 | bytes 4000000 | tf_op jit(solution)/shard_map/prepare/pallas_call | solution.py:110
  16.0 11.8 %collective-permute-done.1.high = f32[440,128]{1,0:T(8,128)S(1)} collective-permute-done((f32[440,128]{1,0:T(8,128)}, f32[440,128]{1,0:T(8,128)S(1)}, u32[]{:S(2)}, u32[]{:S(2)}) %collective-permute-start.1) | collective-permute-done | bytes 225312 | tf_op jit(solution)/shard_map/ppermute | solution.py:740
  27.8 0.9 extend_y.1
  28.7 4.5 %collective-permute-start.2 = (f32[616,128]{1,0:T(8,128)S(1)}, f32[616,128]{1,0:T(8,128)S(1)}, u32[]{:S(2)}, u32[]{:S(2)}) collective-permute-start(f32[616,128]{1,0:T(8,128)S(1)} %get-tuple-element.48), channel_id=1, source_target_pairs={{8,16},{16,8},{24,32},{32,24},{40,48},{48,40},{56,64},{64,56},{72,... | collective-permute-start | bytes 946184 | tf_op jit(solution)/shard_map/ppermute | solution.py:744
  33.2 1.9 %collective-permute-start.3 = (f32[616,128]{1,0:T(8,128)S(1)}, f32[616,128]{1,0:T(8,128)S(1)}, u32[]{:S(2)}, u32[]{:S(2)}) collective-permute-start(f32[616,128]{1,0:T(8,128)S(1)} %get-tuple-element.49), channel_id=1, source_target_pairs={{0,8},{8,0},{16,24},{24,16},{32,40},{40,32},{48,56},{56,48},{64,72... | collective-permute-start | bytes 946184 | tf_op jit(solution)/shard_map/ppermute | solution.py:744
  35.1 1.1 inner.1
  36.2 1.4 %pack_z.1.packed = f32[280,128]{1,0:T(8,128)S(1)} custom-call(f32[2240,128]{1,0:T(8,128)S(1)} %get-tuple-element.44.part, f32[1600,128]{1,0:T(8,128)S(1)} %get-tuple-element.45.vh, f32[440,128]{1,0:T(8,128)S(1)} %collective-permute-done.low, f32[440,128]{1,0:T(8,128)S(1)} %collective-permute-done.1.high), custom_call_target="tpu_custom_call" | custom-call | flops 2000000000 | bytes 4000000 | tf_op jit(solution)/shard_map/pack_z/pallas_call | solution.py:110
  37.8 0.7 extend_x.1
  38.5 1.9 %collective-permute-start.4 = (f32[280,128]{1,0:T(8,128)S(1)}, f32[280,128]{1,0:T(8,128)S(1)}, u32[]{:S(2)}, u32[]{:S(2)}) collective-permute-start(f32[280,128]{1,0:T(8,128)S(1)} %get-tuple-element.51.own_z), channel_id=1, source_target_pairs={{0,1},{1,0},{2,3},{3,2},{4,5},{5,4},{6,7},{7,6},{8,9},{9,8},{10,11... | collective-permute-start | bytes 430088 | tf_op jit(solution)/shard_map/ppermute | solution.py:747
  40.5 1.7 %forward.2.main = f32[3136,128]{1,0:T(8,128)S(1)} custom-call(f32[5]{0:T(128)S(1)} %convert_element_type.3.flags, bf16[56,192]{1,0:T(8,128)(2,1)S(1)} %copy-done.8, f32[2240,128]{1,0:T(8,128)S(1)} %get-tuple-element.44.part, f32[2128,128]{1,0:T(8,128)S(1)} %get-tuple-element.50.inner, f32[112,128]{1,0:T(8,128)S(1)} %get-tuple-element.52.fluxes, ...), custom_call_target="tpu_custom_call" | custom-call | flops 2000000000 | bytes 4000000 | tf_op jit(solution)/shard_map/forward/pallas_call | solution.py:110
  42.2 3.3 %collective-permute-done.4.far_z = f32[280,128]{1,0:T(8,128)S(1)} collective-permute-done((f32[280,128]{1,0:T(8,128)S(1)}, f32[280,128]{1,0:T(8,128)S(1)}, u32[]{:S(2)}, u32[]{:S(2)}) %collective-permute-start.4) | collective-permute-done | bytes 143392 | tf_op jit(solution)/shard_map/ppermute | solution.py:747
  45.4 6.3 %solve.1 = (f32[3136,128]{1,0:T(8,128)S(1)}, f32[3136,128]{1,0:T(8,128)S(1)}, f32[1008,128]{1,0:T(8,128)S(1)}, f32[1008,128]{1,0:T(8,128)S(1)}, f32[544,128]{1,0:T(8,128)S(1)}, /*index=5*/f32[544,128]{1,0:T(8,128)S(1)}) custom-call(f32[5]{0:T(128)S(1)} %convert_element_type.3.flags, f32[280,128]{1,0:T(8,128)S(1)} %get-tuple-element.51.own_z, ...), custom_call_target="tpu_custom_call" | custom-call | flops 6000000000 | bytes 12000000 | tf_op jit(solution)/shard_map/solve/pallas_call | solution.py:110
  51.7 4.4 %collective-permute-start.5 = (f32[544,128]{1,0:T(8,128)S(1)}, f32[544,128]{1,0:T(8,128)S(1)}, u32[]{:S(2)}, u32[]{:S(2)}) collective-permute-start(f32[544,128]{1,0:T(8,128)S(1)} %get-tuple-element.61), channel_id=1, source_target_pairs={{8,16},{16,8},{24,32},{32,24},{40,48},{48,40},{56,64},{64,56},{72,... | collective-permute-start | bytes 835592 | tf_op jit(solution)/shard_map/ppermute | solution.py:744
  56.1 1.9 %collective-permute-start.6 = (f32[544,128]{1,0:T(8,128)S(1)}, f32[544,128]{1,0:T(8,128)S(1)}, u32[]{:S(2)}, u32[]{:S(2)}) collective-permute-start(f32[544,128]{1,0:T(8,128)S(1)} %get-tuple-element.62), channel_id=1, source_target_pairs={{0,8},{8,0},{16,24},{24,16},{32,40},{40,32},{48,56},{56,48},{64,72... | collective-permute-start | bytes 835592 | tf_op jit(solution)/shard_map/ppermute | solution.py:744
  58.1 1.8 %rest.1 = (f32[2352,128]{1,0:T(8,128)S(1)}, f32[2352,128]{1,0:T(8,128)S(1)}) custom-call(bf16[56,192]{1,0:T(8,128)(2,1)S(1)} %copy-done.8, bf16[2,768,256]{2,1,0:T(8,128)(2,1)S(1)} %copy-done.5, f32[3136,128]{1,0:T(8,128)S(1)} %get-tuple-element.55.second_a, f32[3136,128]{1,0:T(8,128)S(1)} %get-tuple-element.56.second_b, ...), custom_call_target="tpu_custom_call" | custom-call | flops 2000000000 | bytes 4000000 | tf_op jit(solution)/shard_map/rest/pallas_call | solution.py:110
  59.9 1.4 %own.1 = (f32[1600,128]{1,0:T(8,128)S(1)}, f32[1640,128]{1,0:T(8,128)S(1)}, f32[1600,128]{1,0:T(8,128)S(1)}, f32[1600,128]{1,0:T(8,128)S(1)}, f32[1600,128]{1,0:T(8,128)S(1)}, /*index=5*/f32[1600,128]{1,0:T(8,128)S(1)}) custom-call(f32[5]{0:T(128)S(1)} %convert_element_type.3.flags, f32[1600,128]{1,0:T(8,128)S(1)} %bitcast.25, ...), custom_call_target="tpu_custom_call" | custom-call | flops 2000000000 | bytes 4000000 | tf_op jit(solution)/shard_map/own/pallas_call | solution.py:110
  61.3 1.2 %fold_x.1 = (f32[2352,128]{1,0:T(8,128)S(1)}, f32[416,128]{1,0:T(8,128)S(1)}, f32[416,128]{1,0:T(8,128)S(1)}, f32[128,128]{1,0:T(8,128)S(1)}, f32[32,128]{1,0:T(8,128)S(1)}, /*index=5*/f32[32,128]{1,0:T(8,128)S(1)}) custom-call(f32[5]{0:T(128)S(1)} %convert_element_type.3.flags, f32[2352,128]{1,0:T(8,128)S(1)} %get-tuple-element.59.sol, ...), custom_call_target="tpu_custom_call" | custom-call | flops 1000000000 | bytes 2000000 | tf_op jit(solution)/shard_map/fold_x/pallas_call | solution.py:110
  62.5 5.5 %collective-permute-start.7 = (f32[416,128]{1,0:T(8,128)S(1)}, f32[416,128]{1,0:T(8,128)S(1)}, u32[]{:S(2)}, u32[]{:S(2)}) collective-permute-start(f32[416,128]{1,0:T(8,128)S(1)} %get-tuple-element.65), channel_id=1, source_target_pairs={{0,2},{2,4},{4,6},{1,3},{3,5},{5,7},{8,10},{10,12},{12,14},{9,11},... | collective-permute-start | bytes 638984 | tf_op jit(solution)/shard_map/ppermute | solution.py:740
  68.0 1.3 %collective-permute-start.8 = (f32[416,128]{1,0:T(8,128)S(1)}, f32[416,128]{1,0:T(8,128)S(1)}, u32[]{:S(2)}, u32[]{:S(2)}) collective-permute-start(f32[416,128]{1,0:T(8,128)S(1)} %get-tuple-element.66), channel_id=1, source_target_pairs={{2,0},{4,2},{6,4},{3,1},{5,3},{7,5},{10,8},{12,10},{14,12},{11,9},... | collective-permute-start | bytes 638984 | tf_op jit(solution)/shard_map/ppermute | solution.py:740
  69.3 4.6 %collective-permute-start.10 = (f32[32,128]{1,0:T(8,128)S(1)}, f32[32,128]{1,0:T(8,128)S(1)}, u32[]{:S(2)}, u32[]{:S(2)}) collective-permute-start(f32[32,128]{1,0:T(8,128)S(1)} %get-tuple-element.68), channel_id=1, source_target_pairs={{0,3},{1,2},{2,5},{3,4},{4,7},{5,6},{8,11},{9,10},{10,13},{11,12},... | collective-permute-start | bytes 49160 | tf_op jit(solution)/shard_map/ppermute | solution.py:810
  74.0 1.3 %collective-permute-start.11 = (f32[32,128]{1,0:T(8,128)S(1)}, f32[32,128]{1,0:T(8,128)S(1)}, u32[]{:S(2)}, u32[]{:S(2)}) collective-permute-start(f32[32,128]{1,0:T(8,128)S(1)} %get-tuple-element.69), channel_id=1, source_target_pairs={{3,0},{2,1},{5,2},{4,3},{7,4},{6,5},{11,8},{10,9},{13,10},{12,11},... | collective-permute-start | bytes 49160 | tf_op jit(solution)/shard_map/ppermute | solution.py:811
  75.2 2.5 %collective-permute-start.9 = (f32[128,128]{1,0:T(8,128)S(1)}, f32[128,128]{1,0:T(8,128)S(1)}, u32[]{:S(2)}, u32[]{:S(2)}) collective-permute-start(f32[128,128]{1,0:T(8,128)S(1)} %get-tuple-element.67.own_z), channel_id=1, source_target_pairs={{0,1},{1,0},{2,3},{3,2},{4,5},{5,4},{6,7},{7,6},{8,9},{9,8},{10,11... | collective-permute-start | bytes 196616 | tf_op jit(solution)/shard_map/ppermute | solution.py:747
  77.7 4.7 %collective-permute-done.8.high = f32[416,128]{1,0:T(8,128)S(1)} collective-permute-done((f32[416,128]{1,0:T(8,128)S(1)}, f32[416,128]{1,0:T(8,128)S(1)}, u32[]{:S(2)}, u32[]{:S(2)}) %collective-permute-start.8) | collective-permute-done | bytes 213024 | tf_op jit(solution)/shard_map/ppermute | solution.py:740
  83.2 0.9 collective-permute-done.9.far_z
  84.0 2.3 %apply.1 = (f32[1600,128]{1,0:T(8,128)S(1)}, f32[1600,128]{1,0:T(8,128)S(1)}, f32[16,128]{1,0:T(8,128)S(1)}) custom-call(f32[2352,128]{1,0:T(8,128)S(1)} %fold_y.1.sol, f32[416,128]{1,0:T(8,128)S(1)} %collective-permute-done.7.low, f32[416,128]{1,0:T(8,128)S(1)} %collective-permute-done.8.high, f32[128,128]{1,0:T(8,128)S(1)} %get-tuple-element.67.own_z, ...), custom_call_target="tpu_custom_call" | custom-call | flops 3000000000 | bytes 6000000 | tf_op jit(solution)/shard_map/apply/pallas_call | solution.py:110
  86.4 13.4 %all_to_all.22 = f32[16,1,128]{2,1,0:T(1,128)S(1)} all-to-all(f32[16,1,128]{2,1,0:T(1,128)S(1)} %bitcast.21), channel_id=1, replica_groups=mesh['gx_x'=4,'gx_y'=8,'gx_c'=2,'gy'=4,'gz'=2] {'gx_c','gy','gz'}, dimensions={0} | all-to-all | bytes 16384 | tf_op jit(solution)/shard_map/all_to_all | solution.py:821
  99.8 18.7 %all_to_all.23 = f32[32,1,128]{2,1,0:T(1,128)S(1)} all-to-all(f32[32,1,128]{2,1,0:T(1,128)S(1)} %bitcast.18), channel_id=1, replica_groups=mesh['gx_x'=4,'gx_y'=8,'gx_c'=2,'gy'=4,'gz'=2] {'gx_x','gx_y'}, dimensions={0} | all-to-all | bytes 32768 | tf_op jit(solution)/shard_map/all_to_all | solution.py:823
  118.4 1.4 %update.1 = (f32[1600,128]{1,0:T(8,128)}, f32[1600,128]{1,0:T(8,128)}) custom-call(f32[32,128]{1,0:T(8,128)S(1)} %bitcast.20, f32[1600,128]{1,0:T(8,128)S(1)} %bitcast.29, f32[1600,128]{1,0:T(8,128)S(1)} %get-tuple-element.63._.resid, f32[1600,128]{1,0:T(8,128)S(1)} %get-tuple-element.76.field, f32[1600,128]{1,0:T(8,128)S(1)} %get-tuple-element.77.applied), custom_call_target="tpu_custom_call" | custom-call | flops 2000000000 | bytes 4000000 | tf_op jit(solution)/shard_map/update/pallas_call | solution.py:110
  (32 shorter events, 1.1 us)
Async XLA Ops:
  0.6 11.4 %copy-start.1 = (f32[40,40,128]{2,1,0:T(8,128)S(1)}, f32[40,40,128]{2,1,0:T(8,128)}, u32[]{:S(2)}) copy-start(f32[40,40,128]{2,1,0:T(8,128)} %h_in.1) | copy-start | bytes 2457604
  0.6 11.4 %copy-start.2 = (f32[40,40,128]{2,1,0:T(8,128)S(1)}, f32[40,40,128]{2,1,0:T(8,128)}, u32[]{:S(2)}) copy-start(f32[40,40,128]{2,1,0:T(8,128)} %v_in.1) | copy-start | bytes 2457604
  0.6 11.4 %copy-start = (f32[40,40,128]{2,1,0:T(8,128)S(1)}, f32[40,40,128]{2,1,0:T(8,128)}, u32[]{:S(2)}) copy-start(f32[40,40,128]{2,1,0:T(8,128)} %b_in.1) | copy-start | bytes 2457604
  4.0 11.9 %collective-permute-start = (f32[440,128]{1,0:T(8,128)}, f32[440,128]{1,0:T(8,128)S(1)}, u32[]{:S(2)}, u32[]{:S(2)}) collective-permute-start(f32[440,128]{1,0:T(8,128)} %get-tuple-element.42.up), channel_id=1, source_target_pairs={{0,2},{2,4},{4,6},{1,3},{3,5},{5,7},{8,10},{10,12},{12,14},{9,11},... | collective-permute-start | bytes 675848 | tf_op jit(solution)/shard_map/ppermute | solution.py:740
  10.7 17.1 %collective-permute-start.1 = (f32[440,128]{1,0:T(8,128)}, f32[440,128]{1,0:T(8,128)S(1)}, u32[]{:S(2)}, u32[]{:S(2)}) collective-permute-start(f32[440,128]{1,0:T(8,128)} %get-tuple-element.43.down), channel_id=1, source_target_pairs={{2,0},{4,2},{6,4},{3,1},{5,3},{7,5},{10,8},{12,10},{14,12},{11,9},... | collective-permute-start | bytes 675848 | tf_op jit(solution)/shard_map/ppermute | solution.py:740
  12.0 2.0 %copy-start.7 = (f32[56,256]{1,0:T(8,128)S(1)}, f32[56,256]{1,0:T(8,128)}, u32[]{:S(2)}) copy-start(f32[56,256]{1,0:T(8,128)} %constant.49.clone.denom) | copy-start | bytes 172036
  12.0 2.0 %copy-start.9 = (f32[56]{0:T(128)S(1)}, f32[56]{0:T(128)}, u32[]{:S(2)}) copy-start(f32[56]{0:T(128)} %constant.48.clone.eigen) | copy-start | bytes 676
  14.1 13.7 %copy-start.3 = (f32[440,128]{1,0:T(8,128)S(1)}, f32[440,128]{1,0:T(8,128)}, u32[]{:S(2)}) copy-start(f32[440,128]{1,0:T(8,128)} %get-tuple-element.42.up) | copy-start | bytes 675844
  14.1 13.7 %copy-start.4 = (f32[440,128]{1,0:T(8,128)S(1)}, f32[440,128]{1,0:T(8,128)}, u32[]{:S(2)}) copy-start(f32[440,128]{1,0:T(8,128)} %get-tuple-element.43.down) | copy-start | bytes 675844
  27.8 7.3 %copy-start.8 = (bf16[56,192]{1,0:T(8,128)(2,1)S(1)}, bf16[56,192]{1,0:T(8,128)(2,1)}, u32[]{:S(2)}) copy-start(bf16[56,192]{1,0:T(8,128)(2,1)} %constant.50.clone.plane) | copy-start | bytes 64516
  28.7 9.1 %collective-permute-start.2 = (f32[616,128]{1,0:T(8,128)S(1)}, f32[616,128]{1,0:T(8,128)S(1)}, u32[]{:S(2)}, u32[]{:S(2)}) collective-permute-start(f32[616,128]{1,0:T(8,128)S(1)} %get-tuple-element.48), channel_id=1, source_target_pairs={{8,16},{16,8},{24,32},{32,24},{40,48},{48,40},{56,64},{64,56},{72,... | collective-permute-start | bytes 946184 | tf_op jit(solution)/shard_map/ppermute | solution.py:744
  33.2 4.6 %collective-permute-start.3 = (f32[616,128]{1,0:T(8,128)S(1)}, f32[616,128]{1,0:T(8,128)S(1)}, u32[]{:S(2)}, u32[]{:S(2)}) collective-permute-start(f32[616,128]{1,0:T(8,128)S(1)} %get-tuple-element.49), channel_id=1, source_target_pairs={{0,8},{8,0},{16,24},{24,16},{32,40},{40,32},{48,56},{56,48},{64,72... | collective-permute-start | bytes 946184 | tf_op jit(solution)/shard_map/ppermute | solution.py:744
  38.5 6.9 %collective-permute-start.4 = (f32[280,128]{1,0:T(8,128)S(1)}, f32[280,128]{1,0:T(8,128)S(1)}, u32[]{:S(2)}, u32[]{:S(2)}) collective-permute-start(f32[280,128]{1,0:T(8,128)S(1)} %get-tuple-element.51.own_z), channel_id=1, source_target_pairs={{0,1},{1,0},{2,3},{3,2},{4,5},{5,4},{6,7},{7,6},{8,9},{9,8},{10,11... | collective-permute-start | bytes 430088 | tf_op jit(solution)/shard_map/ppermute | solution.py:747
  40.5 5.0 %copy-start.5 = (bf16[2,768,256]{2,1,0:T(8,128)(2,1)S(1)}, bf16[2,768,256]{2,1,0:T(8,128)(2,1)}, u32[]{:S(2)}) copy-start(bf16[2,768,256]{2,1,0:T(8,128)(2,1)} %constant.52.clone.inverse) | copy-start | bytes 2359300
  40.5 5.0 %copy-start.6 = (bf16[2,768,256]{2,1,0:T(8,128)(2,1)S(1)}, bf16[2,768,256]{2,1,0:T(8,128)(2,1)}, u32[]{:S(2)}) copy-start(bf16[2,768,256]{2,1,0:T(8,128)(2,1)} %constant.51.clone.forward) | copy-start | bytes 2359300
  51.7 9.6 %collective-permute-start.5 = (f32[544,128]{1,0:T(8,128)S(1)}, f32[544,128]{1,0:T(8,128)S(1)}, u32[]{:S(2)}, u32[]{:S(2)}) collective-permute-start(f32[544,128]{1,0:T(8,128)S(1)} %get-tuple-element.61), channel_id=1, source_target_pairs={{8,16},{16,8},{24,32},{32,24},{40,48},{48,40},{56,64},{64,56},{72,... | collective-permute-start | bytes 835592 | tf_op jit(solution)/shard_map/ppermute | solution.py:744
  56.1 5.1 %collective-permute-start.6 = (f32[544,128]{1,0:T(8,128)S(1)}, f32[544,128]{1,0:T(8,128)S(1)}, u32[]{:S(2)}, u32[]{:S(2)}) collective-permute-start(f32[544,128]{1,0:T(8,128)S(1)} %get-tuple-element.62), channel_id=1, source_target_pairs={{0,8},{8,0},{16,24},{24,16},{32,40},{40,32},{48,56},{56,48},{64,72... | collective-permute-start | bytes 835592 | tf_op jit(solution)/shard_map/ppermute | solution.py:744
  62.5 15.2 %collective-permute-start.7 = (f32[416,128]{1,0:T(8,128)S(1)}, f32[416,128]{1,0:T(8,128)S(1)}, u32[]{:S(2)}, u32[]{:S(2)}) collective-permute-start(f32[416,128]{1,0:T(8,128)S(1)} %get-tuple-element.65), channel_id=1, source_target_pairs={{0,2},{2,4},{4,6},{1,3},{3,5},{5,7},{8,10},{10,12},{12,14},{9,11},... | collective-permute-start | bytes 638984 | tf_op jit(solution)/shard_map/ppermute | solution.py:740
  68.0 14.4 %collective-permute-start.8 = (f32[416,128]{1,0:T(8,128)S(1)}, f32[416,128]{1,0:T(8,128)S(1)}, u32[]{:S(2)}, u32[]{:S(2)}) collective-permute-start(f32[416,128]{1,0:T(8,128)S(1)} %get-tuple-element.66), channel_id=1, source_target_pairs={{2,0},{4,2},{6,4},{3,1},{5,3},{7,5},{10,8},{12,10},{14,12},{11,9},... | collective-permute-start | bytes 638984 | tf_op jit(solution)/shard_map/ppermute | solution.py:740
  69.3 13.8 %collective-permute-start.10 = (f32[32,128]{1,0:T(8,128)S(1)}, f32[32,128]{1,0:T(8,128)S(1)}, u32[]{:S(2)}, u32[]{:S(2)}) collective-permute-start(f32[32,128]{1,0:T(8,128)S(1)} %get-tuple-element.68), channel_id=1, source_target_pairs={{0,3},{1,2},{2,5},{3,4},{4,7},{5,6},{8,11},{9,10},{10,13},{11,12},... | collective-permute-start | bytes 49160 | tf_op jit(solution)/shard_map/ppermute | solution.py:810
  74.0 9.2 %collective-permute-start.11 = (f32[32,128]{1,0:T(8,128)S(1)}, f32[32,128]{1,0:T(8,128)S(1)}, u32[]{:S(2)}, u32[]{:S(2)}) collective-permute-start(f32[32,128]{1,0:T(8,128)S(1)} %get-tuple-element.69), channel_id=1, source_target_pairs={{3,0},{2,1},{5,2},{4,3},{7,4},{6,5},{11,8},{10,9},{13,10},{12,11},... | collective-permute-start | bytes 49160 | tf_op jit(solution)/shard_map/ppermute | solution.py:811
  75.2 8.8 %collective-permute-start.9 = (f32[128,128]{1,0:T(8,128)S(1)}, f32[128,128]{1,0:T(8,128)S(1)}, u32[]{:S(2)}, u32[]{:S(2)}) collective-permute-start(f32[128,128]{1,0:T(8,128)S(1)} %get-tuple-element.67.own_z), channel_id=1, source_target_pairs={{0,1},{1,0},{2,3},{3,2},{4,5},{5,4},{6,7},{7,6},{8,9},{9,8},{10,11... | collective-permute-start | bytes 196616 | tf_op jit(solution)/shard_map/ppermute | solution.py:747

commit v6 on v5

--- a/solution.py
+++ b/solution.py
@@ -298,7 +298,7 @@
         out[at, :] = out[at, :] + value
 
 
-def extend_y_kernel(flags, part, vh, up, down, edge, low, high, first, second, faces, right, left):
+def extend_y_kernel(flags, part, vh, up, down, edge, low, high, _, first, second, faces, right, left):
     base, strip_lanes = strip_base(), strip_mask()
     fluxes = y_fluxes(up, down, low, high)
     for message, start, strip, own in ((left, 0, 400, 0), (right, 32, 416, 80)):
@@ -329,26 +329,52 @@
     second[...] = choose(flags[4], left[...], right[...])
 
 
-def pack_z_kernel(part, vh, low, high, message):
-    base, strip_lanes = strip_base(), strip_mask()
+def pack_planes(tiles, value_of, taken_of):
+    base = strip_base()
+    packs = {}
     for q in range(BLOCKS_Z):
-        for t in range(TILES):
+        for t in tiles:
             near = jnp.zeros((8, CZ), F32)
             taken = jnp.zeros((8, CZ), F32)
             for j in range(PER_Z):
                 x = q * PER_Z + j - OVER
-                if not 0 <= x < C:
-                    continue
-                value = jnp.where(strip_lanes, part[x * EXT + 8 * t : x * EXT + 8 * t + 8, :], 0.0)
-                if t == 0:
-                    taken = taken + pick(low[432:440, :], x, 10 * j)
-                elif t == 6:
-                    taken = taken + pick(high[432:440, :], x, 10 * j)
-                else:
-                    value = value + vh[x * C + 8 * t - 8 : x * C + 8 * t, :]
-                near = near + roll(value, 10 * j, 1)
-            at = q * EXT + 8 * t
-            message[at : at + 8, :] = roll(near, -base, 1) + taken
+                if 0 <= x < C:
+                    near = near + roll(value_of(x, t), 10 * j, 1)
+                    if t in (0, 6):
+                        taken = taken + taken_of(x, t, 10 * j)
+            packs[q, t] = roll(near, -base, 1) + taken
+    return packs
+
+
+def pack_middle_kernel(part, vh, out):
+    strip_lanes = strip_mask()
+
+    def value_of(x, t):
+        at = pl.ds(x * C + 8 * t - 8, 8)
+        return jnp.where(strip_lanes, part[at, :], 0.0) + vh[at, :]
+
+    for (q, t), value in pack_planes((2, 3, 4), value_of, None).items():
+        at = q * 24 + 8 * (t - 2)
+        out[at : at + 8, :] = value
+
+
+def pack_z_kernel(part, vh, low, high, middle, message):
+    strip_lanes = strip_mask()
+
+    def value_of(x, t):
+        value = jnp.where(strip_lanes, part[x * EXT + 8 * t : x * EXT + 8 * t + 8, :], 0.0)
+        if t in (1, 5):
+            value = value + vh[x * C + 8 * t - 8 : x * C + 8 * t, :]
+        return value
+
+    def taken_of(x, t, lane):
+        return pick((low if t == 0 else high)[432:440, :], x, lane)
+
+    for q in range(BLOCKS_Z):
+        message[q * EXT + 16 : q * EXT + 40, :] = middle[24 * q : 24 * q + 24, :]
+    for (q, t), value in pack_planes((0, 1, 5, 6), value_of, taken_of).items():
+        at = q * EXT + 8 * t
+        message[at : at + 8, :] = value
 
 
 def extend_x_kernel(flags, packed, faces, first, second, inner, message, fluxes):
@@ -763,9 +789,10 @@
     pairs, scale_a, scale_b = call(
         prepare_kernel, (own, box, box), eigen, v, h, denom, smem=(0,), name="prepare", work=2
     )
+    (middle,) = call(pack_middle_kernel, (24 * BLOCKS_Z,), part, pairs, name="pack_middle", work=1)
     right, left, faces = call(
         extend_y_kernel, (XROWS, XROWS, 4 * EXT),
-        flags, part, pairs, up, down, edge, low, high,
+        flags, part, pairs, up, down, edge, low, high, middle,
         scratch=[buffer(XROWS)] * 2, smem=(0,), name="extend_y", work=1,
     )
     one, two = exchange_x(right, left)
@@ -773,7 +800,7 @@
         inner_kernel, (38 * EXT, C * EXT),
         flags, plane, part, up, down, low, high, smem=(0,), name="inner", work=1,
     )
-    (packed,) = call(pack_z_kernel, (ZROWS,), part, pairs, low, high, name="pack_z", work=2)
+    (packed,) = call(pack_z_kernel, (ZROWS,), part, pairs, low, high, middle, name="pack_z", work=2)
     own_z, fluxes = call(
         extend_x_kernel, (ZROWS, 2 * EXT), flags, packed, faces, one, two, inner,
         smem=(0,), name="extend_x", work=1,

time: 120 us -> 120 us (level)
  waiting for transfers between devices: 20.9 us -> 22.2 us
    pallas_call x16 -> x17, Pallas kernels: 28 us -> 27.4 us  [call(): pl.pallas_call(body, out_shape=[jax.ShapeDtypeStruct((rows, CZ), F32) for...]
  transfers between devices with their start and end apart: 12 -> 12, of which waited for: 6 -> 6; matrix products, arithmetic and copies ran while one was open for 0% -> 0% of each run, Pallas kernels for 10% -> 9%
where the time goes in v6:
time: 120 us
  starting transfers between devices  37 us (31%)
  blocking collectives  32 us (27%)
  Pallas kernels  27.4 us (23%)
  waiting for transfers between devices  22.2 us (18%)
    pallas_call x17, Pallas kernels, call(): pl.pallas_call(body, out_shape=[jax.ShapeDtypeStruct((rows, CZ), F32) for...  27.4 us
    all_to_all x1, blocking collectives, on_device(): sums = lax.all_to_all(sums, last, 0, 0, tiled=True)  18.7 us
    ppermute x4, waiting for transfers between devices, exchange(): return (lax.ppermute(up, axis, forward), lax.ppermute(down, axis, backward))  16.2 us
    ppermute x4, starting transfers between devices, exchange(): return (lax.ppermute(up, axis, forward), lax.ppermute(down, axis, backward))  14.7 us
    all_to_all x1, blocking collectives, on_device(): sums = lax.all_to_all(sums, first, 0, 0, tiled=True)  13.4 us
    ppermute x2, starting transfers between devices, exchange_x(): lax.ppermute(first, gx, pairs[0])  8.17 us
    ppermute x2, waiting for transfers between devices, swap(): return lax.ppermute(value, 'gz', [(0, 1), (1, 0)])  4.89 us
    ppermute x1, starting transfers between devices, on_device(): far_low = lax.ppermute(across_up, ('gy', 'gz'), pairs)  4.61 us
  transfers between devices with their start and end apart: 12, of which 6 were waited for; matrix products, arithmetic and copies ran while one was open for 0% of the time, Pallas kernels for 9%

profile of v6, /device:TPU:1, one launch (start us, length us, event | category | flops | bytes accessed | tf_op | source)
XLA Modules:
  0.0 119.8 jit_solution(17994126743737549639)
XLA Ops:
  0.7 3.4 %strips.1 = (f32[440,128]{1,0:T(8,128)}, f32[440,128]{1,0:T(8,128)}) custom-call(f32[40,40,128]{2,1,0:T(8,128)} %v_in.1, f32[40,40,128]{2,1,0:T(8,128)} %h_in.1, f32[40,40,128]{2,1,0:T(8,128)} %b_in.1), custom_call_target="tpu_custom_call" | custom-call | flops 2000000000 | bytes 4000000 | tf_op jit(solution)/shard_map/strips/pallas_call | solution.py:110
  4.0 6.6 %collective-permute-start = (f32[440,128]{1,0:T(8,128)}, f32[440,128]{1,0:T(8,128)S(1)}, u32[]{:S(2)}, u32[]{:S(2)}) collective-permute-start(f32[440,128]{1,0:T(8,128)} %get-tuple-element.42.up), channel_id=1, source_target_pairs={{0,2},{2,4},{4,6},{1,3},{3,5},{5,7},{8,10},{10,12},{12,14},{9,11},... | collective-permute-start | bytes 675848 | tf_op jit(solution)/shard_map/ppermute | solution.py:766
  10.7 1.3 %collective-permute-start.1 = (f32[440,128]{1,0:T(8,128)}, f32[440,128]{1,0:T(8,128)S(1)}, u32[]{:S(2)}, u32[]{:S(2)}) collective-permute-start(f32[440,128]{1,0:T(8,128)} %get-tuple-element.43.down), channel_id=1, source_target_pairs={{2,0},{4,2},{6,4},{3,1},{5,3},{7,5},{10,8},{12,10},{14,12},{11,9},... | collective-permute-start | bytes 675848 | tf_op jit(solution)/shard_map/ppermute | solution.py:766
  12.2 1.8 %residual.1 = (f32[1600,128]{1,0:T(8,128)S(1)}, f32[160,128]{1,0:T(8,128)S(1)}) custom-call(f32[1600,128]{1,0:T(8,128)S(1)} %bitcast.27, f32[1600,128]{1,0:T(8,128)S(1)} %bitcast.23, f32[1600,128]{1,0:T(8,128)S(1)} %bitcast.22), custom_call_target="tpu_custom_call" | custom-call | flops 2000000000 | bytes 4000000 | tf_op jit(solution)/shard_map/residual/pallas_call | solution.py:110
  14.0 1.9 %prepare.1 = (f32[1600,128]{1,0:T(8,128)S(1)}, f32[3136,128]{1,0:T(8,128)S(1)}, f32[3136,128]{1,0:T(8,128)S(1)}) custom-call(f32[56]{0:T(128)S(1)} %copy-done.9, f32[1600,128]{1,0:T(8,128)S(1)} %bitcast.28, f32[1600,128]{1,0:T(8,128)S(1)} %bitcast.24, f32[56,256]{1,0:T(8,128)S(1)} %copy-done.7), custom_call_target="tpu_custom_call" | custom-call | flops 2000000000 | bytes 4000000 | tf_op jit(solution)/shard_map/prepare/pallas_call | solution.py:110
  16.2 11.5 %collective-permute-done.1.high = f32[440,128]{1,0:T(8,128)S(1)} collective-permute-done((f32[440,128]{1,0:T(8,128)}, f32[440,128]{1,0:T(8,128)S(1)}, u32[]{:S(2)}, u32[]{:S(2)}) %collective-permute-start.1) | collective-permute-done | bytes 225312 | tf_op jit(solution)/shard_map/ppermute | solution.py:766
  27.8 0.9 extend_y.1
  28.7 4.5 %collective-permute-start.2 = (f32[616,128]{1,0:T(8,128)S(1)}, f32[616,128]{1,0:T(8,128)S(1)}, u32[]{:S(2)}, u32[]{:S(2)}) collective-permute-start(f32[616,128]{1,0:T(8,128)S(1)} %get-tuple-element.48), channel_id=1, source_target_pairs={{8,16},{16,8},{24,32},{32,24},{40,48},{48,40},{56,64},{64,56},{72,... | collective-permute-start | bytes 946184 | tf_op jit(solution)/shard_map/ppermute | solution.py:770
  33.2 1.9 %collective-permute-start.3 = (f32[616,128]{1,0:T(8,128)S(1)}, f32[616,128]{1,0:T(8,128)S(1)}, u32[]{:S(2)}, u32[]{:S(2)}) collective-permute-start(f32[616,128]{1,0:T(8,128)S(1)} %get-tuple-element.49), channel_id=1, source_target_pairs={{0,8},{8,0},{16,24},{24,16},{32,40},{40,32},{48,56},{56,48},{64,72... | collective-permute-start | bytes 946184 | tf_op jit(solution)/shard_map/ppermute | solution.py:770
  35.1 1.1 inner.1
  36.8 1.0 collective-permute-done.2.first.one
  37.8 0.7 extend_x.1
  38.5 1.9 %collective-permute-start.4 = (f32[280,128]{1,0:T(8,128)S(1)}, f32[280,128]{1,0:T(8,128)S(1)}, u32[]{:S(2)}, u32[]{:S(2)}) collective-permute-start(f32[280,128]{1,0:T(8,128)S(1)} %get-tuple-element.51.own_z), channel_id=1, source_target_pairs={{0,1},{1,0},{2,3},{3,2},{4,5},{5,4},{6,7},{7,6},{8,9},{9,8},{10,11... | collective-permute-start | bytes 430088 | tf_op jit(solution)/shard_map/ppermute | solution.py:773
  40.5 1.7 %forward.2.main = f32[3136,128]{1,0:T(8,128)S(1)} custom-call(f32[5]{0:T(128)S(1)} %convert_element_type.3.flags, bf16[56,192]{1,0:T(8,128)(2,1)S(1)} %copy-done.8, f32[2240,128]{1,0:T(8,128)S(1)} %get-tuple-element.44.part, f32[2128,128]{1,0:T(8,128)S(1)} %get-tuple-element.50.inner, f32[112,128]{1,0:T(8,128)S(1)} %get-tuple-element.52.fluxes, ...), custom_call_target="tpu_custom_call" | custom-call | flops 2000000000 | bytes 4000000 | tf_op jit(solution)/shard_map/forward/pallas_call | solution.py:110
  42.2 4.0 %collective-permute-done.4.far_z = f32[280,128]{1,0:T(8,128)S(1)} collective-permute-done((f32[280,128]{1,0:T(8,128)S(1)}, f32[280,128]{1,0:T(8,128)S(1)}, u32[]{:S(2)}, u32[]{:S(2)}) %collective-permute-start.4) | collective-permute-done | bytes 143392 | tf_op jit(solution)/shard_map/ppermute | solution.py:773
  46.2 6.2 %solve.1 = (f32[3136,128]{1,0:T(8,128)S(1)}, f32[3136,128]{1,0:T(8,128)S(1)}, f32[1008,128]{1,0:T(8,128)S(1)}, f32[1008,128]{1,0:T(8,128)S(1)}, f32[544,128]{1,0:T(8,128)S(1)}, /*index=5*/f32[544,128]{1,0:T(8,128)S(1)}) custom-call(f32[5]{0:T(128)S(1)} %convert_element_type.3.flags, f32[280,128]{1,0:T(8,128)S(1)} %get-tuple-element.51.own_z, ...), custom_call_target="tpu_custom_call" | custom-call | flops 6000000000 | bytes 12000000 | tf_op jit(solution)/shard_map/solve/pallas_call | solution.py:110
  52.4 3.7 %collective-permute-start.5 = (f32[544,128]{1,0:T(8,128)S(1)}, f32[544,128]{1,0:T(8,128)S(1)}, u32[]{:S(2)}, u32[]{:S(2)}) collective-permute-start(f32[544,128]{1,0:T(8,128)S(1)} %get-tuple-element.61), channel_id=1, source_target_pairs={{8,16},{16,8},{24,32},{32,24},{40,48},{48,40},{56,64},{64,56},{72,... | collective-permute-start | bytes 835592 | tf_op jit(solution)/shard_map/ppermute | solution.py:770
  56.1 1.9 %collective-permute-start.6 = (f32[544,128]{1,0:T(8,128)S(1)}, f32[544,128]{1,0:T(8,128)S(1)}, u32[]{:S(2)}, u32[]{:S(2)}) collective-permute-start(f32[544,128]{1,0:T(8,128)S(1)} %get-tuple-element.62), channel_id=1, source_target_pairs={{0,8},{8,0},{16,24},{24,16},{32,40},{40,32},{48,56},{56,48},{64,72... | collective-permute-start | bytes 835592 | tf_op jit(solution)/shard_map/ppermute | solution.py:770
  58.0 1.8 %rest.1 = (f32[2352,128]{1,0:T(8,128)S(1)}, f32[2352,128]{1,0:T(8,128)S(1)}) custom-call(bf16[56,192]{1,0:T(8,128)(2,1)S(1)} %copy-done.8, bf16[2,768,256]{2,1,0:T(8,128)(2,1)S(1)} %copy-done.5, f32[3136,128]{1,0:T(8,128)S(1)} %get-tuple-element.55.second_a, f32[3136,128]{1,0:T(8,128)S(1)} %get-tuple-element.56.second_b, ...), custom_call_target="tpu_custom_call" | custom-call | flops 2000000000 | bytes 4000000 | tf_op jit(solution)/shard_map/rest/pallas_call | solution.py:110
  59.8 1.4 %own.1 = (f32[1600,128]{1,0:T(8,128)S(1)}, f32[1640,128]{1,0:T(8,128)S(1)}, f32[1600,128]{1,0:T(8,128)S(1)}, f32[1600,128]{1,0:T(8,128)S(1)}, f32[1600,128]{1,0:T(8,128)S(1)}, /*index=5*/f32[1600,128]{1,0:T(8,128)S(1)}) custom-call(f32[5]{0:T(128)S(1)} %convert_element_type.3.flags, f32[1600,128]{1,0:T(8,128)S(1)} %bitcast.25, ...), custom_call_target="tpu_custom_call" | custom-call | flops 2000000000 | bytes 4000000 | tf_op jit(solution)/shard_map/own/pallas_call | solution.py:110
  61.3 1.2 %fold_x.1 = (f32[2352,128]{1,0:T(8,128)S(1)}, f32[416,128]{1,0:T(8,128)S(1)}, f32[416,128]{1,0:T(8,128)S(1)}, f32[128,128]{1,0:T(8,128)S(1)}, f32[32,128]{1,0:T(8,128)S(1)}, /*index=5*/f32[32,128]{1,0:T(8,128)S(1)}) custom-call(f32[5]{0:T(128)S(1)} %convert_element_type.3.flags, f32[2352,128]{1,0:T(8,128)S(1)} %get-tuple-element.59.sol, ...), custom_call_target="tpu_custom_call" | custom-call | flops 1000000000 | bytes 2000000 | tf_op jit(solution)/shard_map/fold_x/pallas_call | solution.py:110
  62.5 5.5 %collective-permute-start.7 = (f32[416,128]{1,0:T(8,128)S(1)}, f32[416,128]{1,0:T(8,128)S(1)}, u32[]{:S(2)}, u32[]{:S(2)}) collective-permute-start(f32[416,128]{1,0:T(8,128)S(1)} %get-tuple-element.65), channel_id=1, source_target_pairs={{0,2},{2,4},{4,6},{1,3},{3,5},{5,7},{8,10},{10,12},{12,14},{9,11},... | collective-permute-start | bytes 638984 | tf_op jit(solution)/shard_map/ppermute | solution.py:766
  68.0 1.3 %collective-permute-start.8 = (f32[416,128]{1,0:T(8,128)S(1)}, f32[416,128]{1,0:T(8,128)S(1)}, u32[]{:S(2)}, u32[]{:S(2)}) collective-permute-start(f32[416,128]{1,0:T(8,128)S(1)} %get-tuple-element.66), channel_id=1, source_target_pairs={{2,0},{4,2},{6,4},{3,1},{5,3},{7,5},{10,8},{12,10},{14,12},{11,9},... | collective-permute-start | bytes 638984 | tf_op jit(solution)/shard_map/ppermute | solution.py:766
  69.3 4.6 %collective-permute-start.10 = (f32[32,128]{1,0:T(8,128)S(1)}, f32[32,128]{1,0:T(8,128)S(1)}, u32[]{:S(2)}, u32[]{:S(2)}) collective-permute-start(f32[32,128]{1,0:T(8,128)S(1)} %get-tuple-element.68), channel_id=1, source_target_pairs={{0,3},{1,2},{2,5},{3,4},{4,7},{5,6},{8,11},{9,10},{10,13},{11,12},... | collective-permute-start | bytes 49160 | tf_op jit(solution)/shard_map/ppermute | solution.py:837
  73.9 1.3 %collective-permute-start.11 = (f32[32,128]{1,0:T(8,128)S(1)}, f32[32,128]{1,0:T(8,128)S(1)}, u32[]{:S(2)}, u32[]{:S(2)}) collective-permute-start(f32[32,128]{1,0:T(8,128)S(1)} %get-tuple-element.69), channel_id=1, source_target_pairs={{3,0},{2,1},{5,2},{4,3},{7,4},{6,5},{11,8},{10,9},{13,10},{12,11},... | collective-permute-start | bytes 49160 | tf_op jit(solution)/shard_map/ppermute | solution.py:838
  75.2 2.5 %collective-permute-start.9 = (f32[128,128]{1,0:T(8,128)S(1)}, f32[128,128]{1,0:T(8,128)S(1)}, u32[]{:S(2)}, u32[]{:S(2)}) collective-permute-start(f32[128,128]{1,0:T(8,128)S(1)} %get-tuple-element.67.own_z), channel_id=1, source_target_pairs={{0,1},{1,0},{2,3},{3,2},{4,5},{5,4},{6,7},{7,6},{8,9},{9,8},{10,11... | collective-permute-start | bytes 196616 | tf_op jit(solution)/shard_map/ppermute | solution.py:773
  77.7 4.7 %collective-permute-done.8.high = f32[416,128]{1,0:T(8,128)S(1)} collective-permute-done((f32[416,128]{1,0:T(8,128)S(1)}, f32[416,128]{1,0:T(8,128)S(1)}, u32[]{:S(2)}, u32[]{:S(2)}) %collective-permute-start.8) | collective-permute-done | bytes 213024 | tf_op jit(solution)/shard_map/ppermute | solution.py:766
  83.1 0.9 collective-permute-done.9.far_z
  84.0 2.3 %apply.1 = (f32[1600,128]{1,0:T(8,128)S(1)}, f32[1600,128]{1,0:T(8,128)S(1)}, f32[16,128]{1,0:T(8,128)S(1)}) custom-call(f32[2352,128]{1,0:T(8,128)S(1)} %fold_y.1.sol, f32[416,128]{1,0:T(8,128)S(1)} %collective-permute-done.7.low, f32[416,128]{1,0:T(8,128)S(1)} %collective-permute-done.8.high, f32[128,128]{1,0:T(8,128)S(1)} %get-tuple-element.67.own_z, ...), custom_call_target="tpu_custom_call" | custom-call | flops 3000000000 | bytes 6000000 | tf_op jit(solution)/shard_map/apply/pallas_call | solution.py:110
  86.3 13.4 %all_to_all.22 = f32[16,1,128]{2,1,0:T(1,128)S(1)} all-to-all(f32[16,1,128]{2,1,0:T(1,128)S(1)} %bitcast.21), channel_id=1, replica_groups=mesh['gx_x'=4,'gx_y'=8,'gx_c'=2,'gy'=4,'gz'=2] {'gx_c','gy','gz'}, dimensions={0} | all-to-all | bytes 16384 | tf_op jit(solution)/shard_map/all_to_all | solution.py:848
  99.7 18.7 %all_to_all.23 = f32[32,1,128]{2,1,0:T(1,128)S(1)} all-to-all(f32[32,1,128]{2,1,0:T(1,128)S(1)} %bitcast.18), channel_id=1, replica_groups=mesh['gx_x'=4,'gx_y'=8,'gx_c'=2,'gy'=4,'gz'=2] {'gx_x','gx_y'}, dimensions={0} | all-to-all | bytes 32768 | tf_op jit(solution)/shard_map/all_to_all | solution.py:850
  118.4 1.4 %update.1 = (f32[1600,128]{1,0:T(8,128)}, f32[1600,128]{1,0:T(8,128)}) custom-call(f32[32,128]{1,0:T(8,128)S(1)} %bitcast.20, f32[1600,128]{1,0:T(8,128)S(1)} %bitcast.29, f32[1600,128]{1,0:T(8,128)S(1)} %get-tuple-element.63._.resid, f32[1600,128]{1,0:T(8,128)S(1)} %get-tuple-element.76.field, f32[1600,128]{1,0:T(8,128)S(1)} %get-tuple-element.77.applied), custom_call_target="tpu_custom_call" | custom-call | flops 2000000000 | bytes 4000000 | tf_op jit(solution)/shard_map/update/pallas_call | solution.py:110
  (33 shorter events, 1.8 us)
Async XLA Ops:
  0.6 11.5 %copy-start.1 = (f32[40,40,128]{2,1,0:T(8,128)S(1)}, f32[40,40,128]{2,1,0:T(8,128)}, u32[]{:S(2)}) copy-start(f32[40,40,128]{2,1,0:T(8,128)} %h_in.1) | copy-start | bytes 2457604
  0.6 11.5 %copy-start.2 = (f32[40,40,128]{2,1,0:T(8,128)S(1)}, f32[40,40,128]{2,1,0:T(8,128)}, u32[]{:S(2)}) copy-start(f32[40,40,128]{2,1,0:T(8,128)} %v_in.1) | copy-start | bytes 2457604
  0.6 11.5 %copy-start = (f32[40,40,128]{2,1,0:T(8,128)S(1)}, f32[40,40,128]{2,1,0:T(8,128)}, u32[]{:S(2)}) copy-start(f32[40,40,128]{2,1,0:T(8,128)} %b_in.1) | copy-start | bytes 2457604
  4.0 12.2 %collective-permute-start = (f32[440,128]{1,0:T(8,128)}, f32[440,128]{1,0:T(8,128)S(1)}, u32[]{:S(2)}, u32[]{:S(2)}) collective-permute-start(f32[440,128]{1,0:T(8,128)} %get-tuple-element.42.up), channel_id=1, source_target_pairs={{0,2},{2,4},{4,6},{1,3},{3,5},{5,7},{8,10},{10,12},{12,14},{9,11},... | collective-permute-start | bytes 675848 | tf_op jit(solution)/shard_map/ppermute | solution.py:766
  10.7 17.1 %collective-permute-start.1 = (f32[440,128]{1,0:T(8,128)}, f32[440,128]{1,0:T(8,128)S(1)}, u32[]{:S(2)}, u32[]{:S(2)}) collective-permute-start(f32[440,128]{1,0:T(8,128)} %get-tuple-element.43.down), channel_id=1, source_target_pairs={{2,0},{4,2},{6,4},{3,1},{5,3},{7,5},{10,8},{12,10},{14,12},{11,9},... | collective-permute-start | bytes 675848 | tf_op jit(solution)/shard_map/ppermute | solution.py:766
  12.1 1.9 %copy-start.7 = (f32[56,256]{1,0:T(8,128)S(1)}, f32[56,256]{1,0:T(8,128)}, u32[]{:S(2)}) copy-start(f32[56,256]{1,0:T(8,128)} %constant.49.clone.denom) | copy-start | bytes 172036
  12.2 1.9 %copy-start.9 = (f32[56]{0:T(128)S(1)}, f32[56]{0:T(128)}, u32[]{:S(2)}) copy-start(f32[56]{0:T(128)} %constant.48.clone.eigen) | copy-start | bytes 676
  15.9 11.9 %copy-start.3 = (f32[440,128]{1,0:T(8,128)S(1)}, f32[440,128]{1,0:T(8,128)}, u32[]{:S(2)}) copy-start(f32[440,128]{1,0:T(8,128)} %get-tuple-element.42.up) | copy-start | bytes 675844
  15.9 11.8 %copy-start.4 = (f32[440,128]{1,0:T(8,128)S(1)}, f32[440,128]{1,0:T(8,128)}, u32[]{:S(2)}) copy-start(f32[440,128]{1,0:T(8,128)} %get-tuple-element.43.down) | copy-start | bytes 675844
  27.8 7.3 %copy-start.8 = (bf16[56,192]{1,0:T(8,128)(2,1)S(1)}, bf16[56,192]{1,0:T(8,128)(2,1)}, u32[]{:S(2)}) copy-start(bf16[56,192]{1,0:T(8,128)(2,1)} %constant.50.clone.plane) | copy-start | bytes 64516
  28.7 9.1 %collective-permute-start.2 = (f32[616,128]{1,0:T(8,128)S(1)}, f32[616,128]{1,0:T(8,128)S(1)}, u32[]{:S(2)}, u32[]{:S(2)}) collective-permute-start(f32[616,128]{1,0:T(8,128)S(1)} %get-tuple-element.48), channel_id=1, source_target_pairs={{8,16},{16,8},{24,32},{32,24},{40,48},{48,40},{56,64},{64,56},{72,... | collective-permute-start | bytes 946184 | tf_op jit(solution)/shard_map/ppermute | solution.py:770
  33.2 4.6 %collective-permute-start.3 = (f32[616,128]{1,0:T(8,128)S(1)}, f32[616,128]{1,0:T(8,128)S(1)}, u32[]{:S(2)}, u32[]{:S(2)}) collective-permute-start(f32[616,128]{1,0:T(8,128)S(1)} %get-tuple-element.49), channel_id=1, source_target_pairs={{0,8},{8,0},{16,24},{24,16},{32,40},{40,32},{48,56},{56,48},{64,72... | collective-permute-start | bytes 946184 | tf_op jit(solution)/shard_map/ppermute | solution.py:770
  38.5 7.7 %collective-permute-start.4 = (f32[280,128]{1,0:T(8,128)S(1)}, f32[280,128]{1,0:T(8,128)S(1)}, u32[]{:S(2)}, u32[]{:S(2)}) collective-permute-start(f32[280,128]{1,0:T(8,128)S(1)} %get-tuple-element.51.own_z), channel_id=1, source_target_pairs={{0,1},{1,0},{2,3},{3,2},{4,5},{5,4},{6,7},{7,6},{8,9},{9,8},{10,11... | collective-permute-start | bytes 430088 | tf_op jit(solution)/shard_map/ppermute | solution.py:773
  40.5 5.7 %copy-start.5 = (bf16[2,768,256]{2,1,0:T(8,128)(2,1)S(1)}, bf16[2,768,256]{2,1,0:T(8,128)(2,1)}, u32[]{:S(2)}) copy-start(bf16[2,768,256]{2,1,0:T(8,128)(2,1)} %constant.52.clone.inverse) | copy-start | bytes 2359300
  40.5 5.7 %copy-start.6 = (bf16[2,768,256]{2,1,0:T(8,128)(2,1)S(1)}, bf16[2,768,256]{2,1,0:T(8,128)(2,1)}, u32[]{:S(2)}) copy-start(bf16[2,768,256]{2,1,0:T(8,128)(2,1)} %constant.51.clone.forward) | copy-start | bytes 2359300
  52.4 8.8 %collective-permute-start.5 = (f32[544,128]{1,0:T(8,128)S(1)}, f32[544,128]{1,0:T(8,128)S(1)}, u32[]{:S(2)}, u32[]{:S(2)}) collective-permute-start(f32[544,128]{1,0:T(8,128)S(1)} %get-tuple-element.61), channel_id=1, source_target_pairs={{8,16},{16,8},{24,32},{32,24},{40,48},{48,40},{56,64},{64,56},{72,... | collective-permute-start | bytes 835592 | tf_op jit(solution)/shard_map/ppermute | solution.py:770
  56.1 5.1 %collective-permute-start.6 = (f32[544,128]{1,0:T(8,128)S(1)}, f32[544,128]{1,0:T(8,128)S(1)}, u32[]{:S(2)}, u32[]{:S(2)}) collective-permute-start(f32[544,128]{1,0:T(8,128)S(1)} %get-tuple-element.62), channel_id=1, source_target_pairs={{0,8},{8,0},{16,24},{24,16},{32,40},{40,32},{48,56},{56,48},{64,72... | collective-permute-start | bytes 835592 | tf_op jit(solution)/shard_map/ppermute | solution.py:770
  62.5 15.2 %collective-permute-start.7 = (f32[416,128]{1,0:T(8,128)S(1)}, f32[416,128]{1,0:T(8,128)S(1)}, u32[]{:S(2)}, u32[]{:S(2)}) collective-permute-start(f32[416,128]{1,0:T(8,128)S(1)} %get-tuple-element.65), channel_id=1, source_target_pairs={{0,2},{2,4},{4,6},{1,3},{3,5},{5,7},{8,10},{10,12},{12,14},{9,11},... | collective-permute-start | bytes 638984 | tf_op jit(solution)/shard_map/ppermute | solution.py:766
  68.0 14.4 %collective-permute-start.8 = (f32[416,128]{1,0:T(8,128)S(1)}, f32[416,128]{1,0:T(8,128)S(1)}, u32[]{:S(2)}, u32[]{:S(2)}) collective-permute-start(f32[416,128]{1,0:T(8,128)S(1)} %get-tuple-element.66), channel_id=1, source_target_pairs={{2,0},{4,2},{6,4},{3,1},{5,3},{7,5},{10,8},{12,10},{14,12},{11,9},... | collective-permute-start | bytes 638984 | tf_op jit(solution)/shard_map/ppermute | solution.py:766
  69.3 13.8 %collective-permute-start.10 = (f32[32,128]{1,0:T(8,128)S(1)}, f32[32,128]{1,0:T(8,128)S(1)}, u32[]{:S(2)}, u32[]{:S(2)}) collective-permute-start(f32[32,128]{1,0:T(8,128)S(1)} %get-tuple-element.68), channel_id=1, source_target_pairs={{0,3},{1,2},{2,5},{3,4},{4,7},{5,6},{8,11},{9,10},{10,13},{11,12},... | collective-permute-start | bytes 49160 | tf_op jit(solution)/shard_map/ppermute | solution.py:837
  73.9 9.2 %collective-permute-start.11 = (f32[32,128]{1,0:T(8,128)S(1)}, f32[32,128]{1,0:T(8,128)S(1)}, u32[]{:S(2)}, u32[]{:S(2)}) collective-permute-start(f32[32,128]{1,0:T(8,128)S(1)} %get-tuple-element.69), channel_id=1, source_target_pairs={{3,0},{2,1},{5,2},{4,3},{7,4},{6,5},{11,8},{10,9},{13,10},{12,11},... | collective-permute-start | bytes 49160 | tf_op jit(solution)/shard_map/ppermute | solution.py:838
  75.2 8.8 %collective-permute-start.9 = (f32[128,128]{1,0:T(8,128)S(1)}, f32[128,128]{1,0:T(8,128)S(1)}, u32[]{:S(2)}, u32[]{:S(2)}) collective-permute-start(f32[128,128]{1,0:T(8,128)S(1)} %get-tuple-element.67.own_z), channel_id=1, source_target_pairs={{0,1},{1,0},{2,3},{3,2},{4,5},{5,4},{6,7},{7,6},{8,9},{9,8},{10,11... | collective-permute-start | bytes 196616 | tf_op jit(solution)/shard_map/ppermute | solution.py:773

commit v7 on v6

--- a/solution.py
+++ b/solution.py
@@ -476,7 +476,7 @@
 
 
 def solve_kernel(
-    flags, own_z, far_z, main, plane, forward, inverse, scale_a, scale_b,
+    flags, _, own_z, far_z, main, plane, forward, inverse, scale_a, scale_b,
     second_a, second_b, sol, strip, first, second, halo, right, left,
 ):
     gz = lax.axis_index("gz")
@@ -547,8 +547,8 @@
         target[40 * EXT : 42 * EXT, :] = source[9 * EXT : 11 * EXT, :]
 
 
-def own_kernel(flags, h, low, high, one, two, part, fluxes, own_z, far_z, resid, c_x, c_down, c_up, c_z, c_face, cond):
-    face, outer = face_lane(), outer_lane()
+def own_kernel(part, fluxes, own_z, far_z, resid, c_face):
+    face = face_lane()
     half, flux = face_terms(own_z, far_z)
     half, flux = roll(half, face, 1), roll(flux, face, 1)
     lane8 = lanes(8)
@@ -567,6 +567,9 @@
             c_face[to : to + 8, :] = jnp.where(
                 lane8 == face, roll(half[at : at + 8], -10 * j, 1), 0.0
             )
+
+
+def coefficients_kernel(flags, h, low, high, one, two, c_x, c_down, c_up, c_z, cond):
     before, after = by_parity(flags, one, two)
     cond[0:C, :] = before(512, 552)
     cond[C : C + C * C, :] = h[...]
@@ -810,15 +813,17 @@
         forward_kernel, (box,), flags, plane, part, inner, fluxes, one, two,
         scratch=[buffer(box)], smem=(0,), name="forward", work=2,
     )
+    c_x, c_down, c_up, c_z = call(
+        coefficients_kernel, (own + C, own, own, own), flags, h, low, high, one, two,
+        scratch=[buffer(own + 2 * C)], smem=(0,), name="coefficients", work=1,
+    )
     second_a, second_b, sides, side_strip, right, left = call(
         solve_kernel, (box, box, 18 * EXT, 18 * EXT, XROWS2, XROWS2),
-        flags, own_z, far_z, main, plane, forward, inverse, scale_a, scale_b,
+        flags, c_z, own_z, far_z, main, plane, forward, inverse, scale_a, scale_b,
         scratch=[buffer(box), buffer(XROWS2), buffer(XROWS2)], smem=(0,), name="solve", work=6,
     )
-    resid, c_x, c_down, c_up, c_z, c_face = call(
-        own_kernel, (own, own + C, own, own, own, own),
-        flags, h, low, high, one, two, part, fluxes, own_z, far_z,
-        scratch=[buffer(own + 2 * C)], smem=(0,), name="own", work=2,
+    resid, c_face = call(
+        own_kernel, (own, own), part, fluxes, own_z, far_z, name="own", work=1
     )
     one, two = exchange_x(right, left)
     sol, strip = call(

time: 120 us -> 121 us (level)
  blocking collectives: 32 us -> 34.2 us
  waiting for transfers between devices: 22.2 us -> 20.1 us
    ppermute x2, waiting for transfers between devices: 4.89 us -> 3.11 us  [swap(): return lax.ppermute(value, 'gz', [(0, 1), (1, 0)])]
    ppermute x1, starting transfers between devices: 4.61 us -> 6.03 us  [on_device(): far_low = lax.ppermute(across_up, ('gy', 'gz'), pairs)]
    ppermute x4, waiting for transfers between devices: 16.2 us -> 15 us  [exchange(): return (lax.ppermute(up, axis, forward), lax.ppermute(down, axis, backward))]
    pallas_call x17 -> x18, Pallas kernels: 27.4 us -> 27.4 us  [call(): pl.pallas_call(body, out_shape=[jax.ShapeDtypeStruct((rows, CZ), F32) for...]
  transfers between devices with their start and end apart: 12 -> 12, of which waited for: 6 -> 5; matrix products, arithmetic and copies ran while one was open for 0% -> 0% of each run, Pallas kernels for 9% -> 9%
where the time goes in v7:
time: 121 us
  starting transfers between devices  37.9 us (31%)
  blocking collectives  34.2 us (28%)
  Pallas kernels  27.4 us (23%)
  waiting for transfers between devices  20.1 us (17%)
    pallas_call x18, Pallas kernels, call(): pl.pallas_call(body, out_shape=[jax.ShapeDtypeStruct((rows, CZ), F32) for...  27.4 us
    all_to_all x1, blocking collectives, on_device(): sums = lax.all_to_all(sums, last, 0, 0, tiled=True)  19.9 us
    ppermute x4, waiting for transfers between devices, exchange(): return (lax.ppermute(up, axis, forward), lax.ppermute(down, axis, backward))  15 us
    ppermute x4, starting transfers between devices, exchange(): return (lax.ppermute(up, axis, forward), lax.ppermute(down, axis, backward))  14.7 us
    all_to_all x1, blocking collectives, on_device(): sums = lax.all_to_all(sums, first, 0, 0, tiled=True)  14.3 us
    ppermute x2, starting transfers between devices, exchange_x(): lax.ppermute(first, gx, pairs[0])  8.18 us
    ppermute x1, starting transfers between devices, on_device(): far_low = lax.ppermute(across_up, ('gy', 'gz'), pairs)  6.03 us
    ppermute x2, starting transfers between devices, swap(): return lax.ppermute(value, 'gz', [(0, 1), (1, 0)])  3.87 us
  transfers between devices with their start and end apart: 12, of which 5 were waited for; matrix products, arithmetic and copies ran while one was open for 0% of the time, Pallas kernels for 9%

profile of v7, /device:TPU:1, one launch (start us, length us, event | category | flops | bytes accessed | tf_op | source)
XLA Modules:
  0.0 120.7 jit_solution(15340397791814254415)
XLA Ops:
  0.7 3.4 %strips.1 = (f32[440,128]{1,0:T(8,128)}, f32[440,128]{1,0:T(8,128)}) custom-call(f32[40,40,128]{2,1,0:T(8,128)} %v_in.1, f32[40,40,128]{2,1,0:T(8,128)} %h_in.1, f32[40,40,128]{2,1,0:T(8,128)} %b_in.1), custom_call_target="tpu_custom_call" | custom-call | flops 2000000000 | bytes 4000000 | tf_op jit(solution)/shard_map/strips/pallas_call | solution.py:110
  4.0 6.6 %collective-permute-start = (f32[440,128]{1,0:T(8,128)}, f32[440,128]{1,0:T(8,128)S(1)}, u32[]{:S(2)}, u32[]{:S(2)}) collective-permute-start(f32[440,128]{1,0:T(8,128)} %get-tuple-element.41.up), channel_id=1, source_target_pairs={{0,2},{2,4},{4,6},{1,3},{3,5},{5,7},{8,10},{10,12},{12,14},{9,11},... | collective-permute-start | bytes 675848 | tf_op jit(solution)/shard_map/ppermute | solution.py:769
  10.7 1.3 %collective-permute-start.1 = (f32[440,128]{1,0:T(8,128)}, f32[440,128]{1,0:T(8,128)S(1)}, u32[]{:S(2)}, u32[]{:S(2)}) collective-permute-start(f32[440,128]{1,0:T(8,128)} %get-tuple-element.42.down), channel_id=1, source_target_pairs={{2,0},{4,2},{6,4},{3,1},{5,3},{7,5},{10,8},{12,10},{14,12},{11,9},... | collective-permute-start | bytes 675848 | tf_op jit(solution)/shard_map/ppermute | solution.py:769
  12.2 1.8 %residual.1 = (f32[1600,128]{1,0:T(8,128)S(1)}, f32[160,128]{1,0:T(8,128)S(1)}) custom-call(f32[1600,128]{1,0:T(8,128)S(1)} %bitcast.27, f32[1600,128]{1,0:T(8,128)S(1)} %bitcast.23, f32[1600,128]{1,0:T(8,128)S(1)} %bitcast.22), custom_call_target="tpu_custom_call" | custom-call | flops 2000000000 | bytes 4000000 | tf_op jit(solution)/shard_map/residual/pallas_call | solution.py:110
  14.1 1.9 %prepare.1 = (f32[1600,128]{1,0:T(8,128)S(1)}, f32[3136,128]{1,0:T(8,128)S(1)}, f32[3136,128]{1,0:T(8,128)S(1)}) custom-call(f32[56]{0:T(128)S(1)} %copy-done.9, f32[1600,128]{1,0:T(8,128)S(1)} %bitcast.28, f32[1600,128]{1,0:T(8,128)S(1)} %bitcast.24, f32[56,256]{1,0:T(8,128)S(1)} %copy-done.7), custom_call_target="tpu_custom_call" | custom-call | flops 2000000000 | bytes 4000000 | tf_op jit(solution)/shard_map/prepare/pallas_call | solution.py:110
  16.2 11.5 %collective-permute-done.1.high = f32[440,128]{1,0:T(8,128)S(1)} collective-permute-done((f32[440,128]{1,0:T(8,128)}, f32[440,128]{1,0:T(8,128)S(1)}, u32[]{:S(2)}, u32[]{:S(2)}) %collective-permute-start.1) | collective-permute-done | bytes 225312 | tf_op jit(solution)/shard_map/ppermute | solution.py:769
  27.8 0.9 extend_y.1
  28.7 4.5 %collective-permute-start.2 = (f32[616,128]{1,0:T(8,128)S(1)}, f32[616,128]{1,0:T(8,128)S(1)}, u32[]{:S(2)}, u32[]{:S(2)}) collective-permute-start(f32[616,128]{1,0:T(8,128)S(1)} %get-tuple-element.46), channel_id=1, source_target_pairs={{8,16},{16,8},{24,32},{32,24},{40,48},{48,40},{56,64},{64,56},{72,... | collective-permute-start | bytes 946184 | tf_op jit(solution)/shard_map/ppermute | solution.py:773
  33.2 1.9 %collective-permute-start.3 = (f32[616,128]{1,0:T(8,128)S(1)}, f32[616,128]{1,0:T(8,128)S(1)}, u32[]{:S(2)}, u32[]{:S(2)}) collective-permute-start(f32[616,128]{1,0:T(8,128)S(1)} %get-tuple-element.47), channel_id=1, source_target_pairs={{0,8},{8,0},{16,24},{24,16},{32,40},{40,32},{48,56},{56,48},{64,72... | collective-permute-start | bytes 946184 | tf_op jit(solution)/shard_map/ppermute | solution.py:773
  35.1 1.1 inner.1
  36.8 1.0 collective-permute-done.2.one.first
  37.8 0.7 extend_x.1
  38.5 1.9 %collective-permute-start.4 = (f32[280,128]{1,0:T(8,128)S(1)}, f32[280,128]{1,0:T(8,128)S(1)}, u32[]{:S(2)}, u32[]{:S(2)}) collective-permute-start(f32[280,128]{1,0:T(8,128)S(1)} %get-tuple-element.52.own_z), channel_id=1, source_target_pairs={{0,1},{1,0},{2,3},{3,2},{4,5},{5,4},{6,7},{7,6},{8,9},{9,8},{10,11... | collective-permute-start | bytes 430088 | tf_op jit(solution)/shard_map/ppermute | solution.py:776
  40.4 0.9 coefficients.1
  41.4 1.7 %forward.2.main = f32[3136,128]{1,0:T(8,128)S(1)} custom-call(f32[5]{0:T(128)S(1)} %convert_element_type.3.flags, bf16[56,192]{1,0:T(8,128)(2,1)S(1)} %copy-done.8, f32[2240,128]{1,0:T(8,128)S(1)} %get-tuple-element.49.part, f32[2128,128]{1,0:T(8,128)S(1)} %get-tuple-element.51.inner, f32[112,128]{1,0:T(8,128)S(1)} %get-tuple-element.53.fluxes, ...), custom_call_target="tpu_custom_call" | custom-call | flops 2000000000 | bytes 4000000 | tf_op jit(solution)/shard_map/forward/pallas_call | solution.py:110
  43.1 3.1 %collective-permute-done.4.far_z = f32[280,128]{1,0:T(8,128)S(1)} collective-permute-done((f32[280,128]{1,0:T(8,128)S(1)}, f32[280,128]{1,0:T(8,128)S(1)}, u32[]{:S(2)}, u32[]{:S(2)}) %collective-permute-start.4) | collective-permute-done | bytes 143392 | tf_op jit(solution)/shard_map/ppermute | solution.py:776
  46.2 6.3 %solve.1 = (f32[3136,128]{1,0:T(8,128)S(1)}, f32[3136,128]{1,0:T(8,128)S(1)}, f32[1008,128]{1,0:T(8,128)S(1)}, f32[1008,128]{1,0:T(8,128)S(1)}, f32[544,128]{1,0:T(8,128)S(1)}, /*index=5*/f32[544,128]{1,0:T(8,128)S(1)}) custom-call(f32[5]{0:T(128)S(1)} %convert_element_type.3.flags, f32[1600,128]{1,0:T(8,128)S(1)} %get-tuple-element.48._.c_z, ...), custom_call_target="tpu_custom_call" | custom-call | flops 6000000000 | bytes 12000000 | tf_op jit(solution)/shard_map/solve/pallas_call | solution.py:110
  52.5 3.7 %collective-permute-start.5 = (f32[544,128]{1,0:T(8,128)S(1)}, f32[544,128]{1,0:T(8,128)S(1)}, u32[]{:S(2)}, u32[]{:S(2)}) collective-permute-start(f32[544,128]{1,0:T(8,128)S(1)} %get-tuple-element.62), channel_id=1, source_target_pairs={{8,16},{16,8},{24,32},{32,24},{40,48},{48,40},{56,64},{64,56},{72,... | collective-permute-start | bytes 835592 | tf_op jit(solution)/shard_map/ppermute | solution.py:773
  56.1 1.9 %collective-permute-start.6 = (f32[544,128]{1,0:T(8,128)S(1)}, f32[544,128]{1,0:T(8,128)S(1)}, u32[]{:S(2)}, u32[]{:S(2)}) collective-permute-start(f32[544,128]{1,0:T(8,128)S(1)} %get-tuple-element.63), channel_id=1, source_target_pairs={{0,8},{8,0},{16,24},{24,16},{32,40},{40,32},{48,56},{56,48},{64,72... | collective-permute-start | bytes 835592 | tf_op jit(solution)/shard_map/ppermute | solution.py:773
  58.7 1.7 %rest.1 = (f32[2352,128]{1,0:T(8,128)S(1)}, f32[2352,128]{1,0:T(8,128)S(1)}) custom-call(bf16[56,192]{1,0:T(8,128)(2,1)S(1)} %copy-done.8, bf16[2,768,256]{2,1,0:T(8,128)(2,1)S(1)} %copy-done.5, f32[3136,128]{1,0:T(8,128)S(1)} %get-tuple-element.56.second_a, f32[3136,128]{1,0:T(8,128)S(1)} %get-tuple-element.57.second_b, ...), custom_call_target="tpu_custom_call" | custom-call | flops 2000000000 | bytes 4000000 | tf_op jit(solution)/shard_map/rest/pallas_call | solution.py:110
  60.4 1.2 %fold_x.1 = (f32[2352,128]{1,0:T(8,128)S(1)}, f32[416,128]{1,0:T(8,128)S(1)}, f32[416,128]{1,0:T(8,128)S(1)}, f32[128,128]{1,0:T(8,128)S(1)}, f32[32,128]{1,0:T(8,128)S(1)}, /*index=5*/f32[32,128]{1,0:T(8,128)S(1)}) custom-call(f32[5]{0:T(128)S(1)} %convert_element_type.3.flags, f32[2352,128]{1,0:T(8,128)S(1)} %get-tuple-element.60.sol, ...), custom_call_target="tpu_custom_call" | custom-call | flops 1000000000 | bytes 2000000 | tf_op jit(solution)/shard_map/fold_x/pallas_call | solution.py:110
  61.7 5.5 %collective-permute-start.7 = (f32[416,128]{1,0:T(8,128)S(1)}, f32[416,128]{1,0:T(8,128)S(1)}, u32[]{:S(2)}, u32[]{:S(2)}) collective-permute-start(f32[416,128]{1,0:T(8,128)S(1)} %get-tuple-element.66), channel_id=1, source_target_pairs={{0,2},{2,4},{4,6},{1,3},{3,5},{5,7},{8,10},{10,12},{12,14},{9,11},... | collective-permute-start | bytes 638984 | tf_op jit(solution)/shard_map/ppermute | solution.py:769
  67.1 1.3 %collective-permute-start.8 = (f32[416,128]{1,0:T(8,128)S(1)}, f32[416,128]{1,0:T(8,128)S(1)}, u32[]{:S(2)}, u32[]{:S(2)}) collective-permute-start(f32[416,128]{1,0:T(8,128)S(1)} %get-tuple-element.67), channel_id=1, source_target_pairs={{2,0},{4,2},{6,4},{3,1},{5,3},{7,5},{10,8},{12,10},{14,12},{11,9},... | collective-permute-start | bytes 638984 | tf_op jit(solution)/shard_map/ppermute | solution.py:769
  68.4 1.9 %collective-permute-start.9 = (f32[128,128]{1,0:T(8,128)S(1)}, f32[128,128]{1,0:T(8,128)S(1)}, u32[]{:S(2)}, u32[]{:S(2)}) collective-permute-start(f32[128,128]{1,0:T(8,128)S(1)} %get-tuple-element.68.own_z), channel_id=1, source_target_pairs={{0,1},{1,0},{2,3},{3,2},{4,5},{5,4},{6,7},{7,6},{8,9},{9,8},{10,11... | collective-permute-start | bytes 196616 | tf_op jit(solution)/shard_map/ppermute | solution.py:776
  70.4 6.0 %collective-permute-start.10 = (f32[32,128]{1,0:T(8,128)S(1)}, f32[32,128]{1,0:T(8,128)S(1)}, u32[]{:S(2)}, u32[]{:S(2)}) collective-permute-start(f32[32,128]{1,0:T(8,128)S(1)} %get-tuple-element.69), channel_id=1, source_target_pairs={{0,3},{1,2},{2,5},{3,4},{4,7},{5,6},{8,11},{9,10},{10,13},{11,12},... | collective-permute-start | bytes 49160 | tf_op jit(solution)/shard_map/ppermute | solution.py:842
  76.4 1.3 %collective-permute-start.11 = (f32[32,128]{1,0:T(8,128)S(1)}, f32[32,128]{1,0:T(8,128)S(1)}, u32[]{:S(2)}, u32[]{:S(2)}) collective-permute-start(f32[32,128]{1,0:T(8,128)S(1)} %get-tuple-element.70), channel_id=1, source_target_pairs={{3,0},{2,1},{5,2},{4,3},{7,4},{6,5},{11,8},{10,9},{13,10},{12,11},... | collective-permute-start | bytes 49160 | tf_op jit(solution)/shard_map/ppermute | solution.py:843
  77.7 3.5 %collective-permute-done.8.high = f32[416,128]{1,0:T(8,128)S(1)} collective-permute-done((f32[416,128]{1,0:T(8,128)S(1)}, f32[416,128]{1,0:T(8,128)S(1)}, u32[]{:S(2)}, u32[]{:S(2)}) %collective-permute-start.8) | collective-permute-done | bytes 213024 | tf_op jit(solution)/shard_map/ppermute | solution.py:769
  81.9 1.0 collective-permute-done.11.far_high
  82.8 2.3 %apply.1 = (f32[1600,128]{1,0:T(8,128)S(1)}, f32[1600,128]{1,0:T(8,128)S(1)}, f32[16,128]{1,0:T(8,128)S(1)}) custom-call(f32[2352,128]{1,0:T(8,128)S(1)} %fold_y.1.sol, f32[416,128]{1,0:T(8,128)S(1)} %collective-permute-done.7.low, f32[416,128]{1,0:T(8,128)S(1)} %collective-permute-done.8.high, f32[128,128]{1,0:T(8,128)S(1)} %get-tuple-element.68.own_z, ...), custom_call_target="tpu_custom_call" | custom-call | flops 3000000000 | bytes 6000000 | tf_op jit(solution)/shard_map/apply/pallas_call | solution.py:110
  85.1 14.3 %all_to_all.22 = f32[16,1,128]{2,1,0:T(1,128)S(1)} all-to-all(f32[16,1,128]{2,1,0:T(1,128)S(1)} %bitcast.21), channel_id=1, replica_groups=mesh['gx_x'=4,'gx_y'=8,'gx_c'=2,'gy'=4,'gz'=2] {'gx_c','gy','gz'}, dimensions={0} | all-to-all | bytes 16384 | tf_op jit(solution)/shard_map/all_to_all | solution.py:853
  99.4 19.9 %all_to_all.23 = f32[32,1,128]{2,1,0:T(1,128)S(1)} all-to-all(f32[32,1,128]{2,1,0:T(1,128)S(1)} %bitcast.18), channel_id=1, replica_groups=mesh['gx_x'=4,'gx_y'=8,'gx_c'=2,'gy'=4,'gz'=2] {'gx_x','gx_y'}, dimensions={0} | all-to-all | bytes 32768 | tf_op jit(solution)/shard_map/all_to_all | solution.py:855
  119.3 1.4 %update.1 = (f32[1600,128]{1,0:T(8,128)}, f32[1600,128]{1,0:T(8,128)}) custom-call(f32[32,128]{1,0:T(8,128)S(1)} %bitcast.20, f32[1600,128]{1,0:T(8,128)S(1)} %bitcast.29, f32[1600,128]{1,0:T(8,128)S(1)} %get-tuple-element.64._.resid, f32[1600,128]{1,0:T(8,128)S(1)} %get-tuple-element.76.field, f32[1600,128]{1,0:T(8,128)S(1)} %get-tuple-element.77.applied), custom_call_target="tpu_custom_call" | custom-call | flops 2000000000 | bytes 4000000 | tf_op jit(solution)/shard_map/update/pallas_call | solution.py:110
  (34 shorter events, 2.4 us)
Async XLA Ops:
  0.6 11.5 %copy-start.1 = (f32[40,40,128]{2,1,0:T(8,128)S(1)}, f32[40,40,128]{2,1,0:T(8,128)}, u32[]{:S(2)}) copy-start(f32[40,40,128]{2,1,0:T(8,128)} %h_in.1) | copy-start | bytes 2457604
  0.6 11.5 %copy-start.2 = (f32[40,40,128]{2,1,0:T(8,128)S(1)}, f32[40,40,128]{2,1,0:T(8,128)}, u32[]{:S(2)}) copy-start(f32[40,40,128]{2,1,0:T(8,128)} %v_in.1) | copy-start | bytes 2457604
  0.6 11.5 %copy-start = (f32[40,40,128]{2,1,0:T(8,128)S(1)}, f32[40,40,128]{2,1,0:T(8,128)}, u32[]{:S(2)}) copy-start(f32[40,40,128]{2,1,0:T(8,128)} %b_in.1) | copy-start | bytes 2457604
  4.0 12.2 %collective-permute-start = (f32[440,128]{1,0:T(8,128)}, f32[440,128]{1,0:T(8,128)S(1)}, u32[]{:S(2)}, u32[]{:S(2)}) collective-permute-start(f32[440,128]{1,0:T(8,128)} %get-tuple-element.41.up), channel_id=1, source_target_pairs={{0,2},{2,4},{4,6},{1,3},{3,5},{5,7},{8,10},{10,12},{12,14},{9,11},... | collective-permute-start | bytes 675848 | tf_op jit(solution)/shard_map/ppermute | solution.py:769
  10.7 17.1 %collective-permute-start.1 = (f32[440,128]{1,0:T(8,128)}, f32[440,128]{1,0:T(8,128)S(1)}, u32[]{:S(2)}, u32[]{:S(2)}) collective-permute-start(f32[440,128]{1,0:T(8,128)} %get-tuple-element.42.down), channel_id=1, source_target_pairs={{2,0},{4,2},{6,4},{3,1},{5,3},{7,5},{10,8},{12,10},{14,12},{11,9},... | collective-permute-start | bytes 675848 | tf_op jit(solution)/shard_map/ppermute | solution.py:769
  12.1 1.9 %copy-start.7 = (f32[56,256]{1,0:T(8,128)S(1)}, f32[56,256]{1,0:T(8,128)}, u32[]{:S(2)}) copy-start(f32[56,256]{1,0:T(8,128)} %constant.49.clone.denom) | copy-start | bytes 172036
  12.2 1.9 %copy-start.9 = (f32[56]{0:T(128)S(1)}, f32[56]{0:T(128)}, u32[]{:S(2)}) copy-start(f32[56]{0:T(128)} %constant.48.clone.eigen) | copy-start | bytes 676
  15.9 11.9 %copy-start.3 = (f32[440,128]{1,0:T(8,128)S(1)}, f32[440,128]{1,0:T(8,128)}, u32[]{:S(2)}) copy-start(f32[440,128]{1,0:T(8,128)} %get-tuple-element.41.up) | copy-start | bytes 675844
  15.9 11.8 %copy-start.4 = (f32[440,128]{1,0:T(8,128)S(1)}, f32[440,128]{1,0:T(8,128)}, u32[]{:S(2)}) copy-start(f32[440,128]{1,0:T(8,128)} %get-tuple-element.42.down) | copy-start | bytes 675844
  27.8 7.3 %copy-start.8 = (bf16[56,192]{1,0:T(8,128)(2,1)S(1)}, bf16[56,192]{1,0:T(8,128)(2,1)}, u32[]{:S(2)}) copy-start(bf16[56,192]{1,0:T(8,128)(2,1)} %constant.50.clone.plane) | copy-start | bytes 64516
  28.7 9.1 %collective-permute-start.2 = (f32[616,128]{1,0:T(8,128)S(1)}, f32[616,128]{1,0:T(8,128)S(1)}, u32[]{:S(2)}, u32[]{:S(2)}) collective-permute-start(f32[616,128]{1,0:T(8,128)S(1)} %get-tuple-element.46), channel_id=1, source_target_pairs={{8,16},{16,8},{24,32},{32,24},{40,48},{48,40},{56,64},{64,56},{72,... | collective-permute-start | bytes 946184 | tf_op jit(solution)/shard_map/ppermute | solution.py:773
  33.2 4.6 %collective-permute-start.3 = (f32[616,128]{1,0:T(8,128)S(1)}, f32[616,128]{1,0:T(8,128)S(1)}, u32[]{:S(2)}, u32[]{:S(2)}) collective-permute-start(f32[616,128]{1,0:T(8,128)S(1)} %get-tuple-element.47), channel_id=1, source_target_pairs={{0,8},{8,0},{16,24},{24,16},{32,40},{40,32},{48,56},{56,48},{64,72... | collective-permute-start | bytes 946184 | tf_op jit(solution)/shard_map/ppermute | solution.py:773
  38.5 7.7 %collective-permute-start.4 = (f32[280,128]{1,0:T(8,128)S(1)}, f32[280,128]{1,0:T(8,128)S(1)}, u32[]{:S(2)}, u32[]{:S(2)}) collective-permute-start(f32[280,128]{1,0:T(8,128)S(1)} %get-tuple-element.52.own_z), channel_id=1, source_target_pairs={{0,1},{1,0},{2,3},{3,2},{4,5},{5,4},{6,7},{7,6},{8,9},{9,8},{10,11... | collective-permute-start | bytes 430088 | tf_op jit(solution)/shard_map/ppermute | solution.py:776
  41.4 4.8 %copy-start.5 = (bf16[2,768,256]{2,1,0:T(8,128)(2,1)S(1)}, bf16[2,768,256]{2,1,0:T(8,128)(2,1)}, u32[]{:S(2)}) copy-start(bf16[2,768,256]{2,1,0:T(8,128)(2,1)} %constant.52.clone.inverse) | copy-start | bytes 2359300
  41.4 4.8 %copy-start.6 = (bf16[2,768,256]{2,1,0:T(8,128)(2,1)S(1)}, bf16[2,768,256]{2,1,0:T(8,128)(2,1)}, u32[]{:S(2)}) copy-start(bf16[2,768,256]{2,1,0:T(8,128)(2,1)} %constant.51.clone.forward) | copy-start | bytes 2359300
  52.5 7.9 %collective-permute-start.5 = (f32[544,128]{1,0:T(8,128)S(1)}, f32[544,128]{1,0:T(8,128)S(1)}, u32[]{:S(2)}, u32[]{:S(2)}) collective-permute-start(f32[544,128]{1,0:T(8,128)S(1)} %get-tuple-element.62), channel_id=1, source_target_pairs={{8,16},{16,8},{24,32},{32,24},{40,48},{48,40},{56,64},{64,56},{72,... | collective-permute-start | bytes 835592 | tf_op jit(solution)/shard_map/ppermute | solution.py:773
  56.1 4.3 %collective-permute-start.6 = (f32[544,128]{1,0:T(8,128)S(1)}, f32[544,128]{1,0:T(8,128)S(1)}, u32[]{:S(2)}, u32[]{:S(2)}) collective-permute-start(f32[544,128]{1,0:T(8,128)S(1)} %get-tuple-element.63), channel_id=1, source_target_pairs={{0,8},{8,0},{16,24},{24,16},{32,40},{40,32},{48,56},{56,48},{64,72... | collective-permute-start | bytes 835592 | tf_op jit(solution)/shard_map/ppermute | solution.py:773
  61.7 16.1 %collective-permute-start.7 = (f32[416,128]{1,0:T(8,128)S(1)}, f32[416,128]{1,0:T(8,128)S(1)}, u32[]{:S(2)}, u32[]{:S(2)}) collective-permute-start(f32[416,128]{1,0:T(8,128)S(1)} %get-tuple-element.66), channel_id=1, source_target_pairs={{0,2},{2,4},{4,6},{1,3},{3,5},{5,7},{8,10},{10,12},{12,14},{9,11},... | collective-permute-start | bytes 638984 | tf_op jit(solution)/shard_map/ppermute | solution.py:769
  67.1 14.1 %collective-permute-start.8 = (f32[416,128]{1,0:T(8,128)S(1)}, f32[416,128]{1,0:T(8,128)S(1)}, u32[]{:S(2)}, u32[]{:S(2)}) collective-permute-start(f32[416,128]{1,0:T(8,128)S(1)} %get-tuple-element.67), channel_id=1, source_target_pairs={{2,0},{4,2},{6,4},{3,1},{5,3},{7,5},{10,8},{12,10},{14,12},{11,9},... | collective-permute-start | bytes 638984 | tf_op jit(solution)/shard_map/ppermute | solution.py:769
  68.4 14.4 %collective-permute-start.9 = (f32[128,128]{1,0:T(8,128)S(1)}, f32[128,128]{1,0:T(8,128)S(1)}, u32[]{:S(2)}, u32[]{:S(2)}) collective-permute-start(f32[128,128]{1,0:T(8,128)S(1)} %get-tuple-element.68.own_z), channel_id=1, source_target_pairs={{0,1},{1,0},{2,3},{3,2},{4,5},{5,4},{6,7},{7,6},{8,9},{9,8},{10,11... | collective-permute-start | bytes 196616 | tf_op jit(solution)/shard_map/ppermute | solution.py:776
  70.4 11.5 %collective-permute-start.10 = (f32[32,128]{1,0:T(8,128)S(1)}, f32[32,128]{1,0:T(8,128)S(1)}, u32[]{:S(2)}, u32[]{:S(2)}) collective-permute-start(f32[32,128]{1,0:T(8,128)S(1)} %get-tuple-element.69), channel_id=1, source_target_pairs={{0,3},{1,2},{2,5},{3,4},{4,7},{5,6},{8,11},{9,10},{10,13},{11,12},... | collective-permute-start | bytes 49160 | tf_op jit(solution)/shard_map/ppermute | solution.py:842
  76.4 6.4 %collective-permute-start.11 = (f32[32,128]{1,0:T(8,128)S(1)}, f32[32,128]{1,0:T(8,128)S(1)}, u32[]{:S(2)}, u32[]{:S(2)}) collective-permute-start(f32[32,128]{1,0:T(8,128)S(1)} %get-tuple-element.70), channel_id=1, source_target_pairs={{3,0},{2,1},{5,2},{4,3},{7,4},{6,5},{11,8},{10,9},{13,10},{12,11},... | collective-permute-start | bytes 49160 | tf_op jit(solution)/shard_map/ppermute | solution.py:843

commit v8 on v6

--- a/solution.py
+++ b/solution.py
@@ -192,7 +192,7 @@
         return flux_up, flux_down, pack_up, pack_down
 
     zero = jnp.zeros((8, CZ), F32)
-    _, _, pack_up, pack_down = lax.fori_loop(0, C, visit, (zero,) * 4, unroll=8)
+    _, _, pack_up, pack_down = lax.fori_loop(0, C, visit, (zero,) * 4, unroll=20)
     up[432:440, :] = pack_up
     down[432:440, :] = pack_down
     for message, first in ((up, 32), (down, 0)):
@@ -729,7 +729,7 @@
     for x in range(C):
         for t in range(5):
             out[x * C + 8 * t : x * C + 8 * t + 8, :] = along_z(x + 1, t + 1)
-    _, sum_a, sum_b = lax.fori_loop(0, C, visit, (flux_x, sum_a, sum_b), unroll=8)
+    _, sum_a, sum_b = lax.fori_loop(0, C, visit, (flux_x, sum_a, sum_b), unroll=20)
     total_a = jnp.sum(sum_a, axis=0, keepdims=True)
     total_b = jnp.sum(sum_b, axis=0, keepdims=True)
     total_a = total_a + roll(total_a, CZ // 2, 1)

time: 120 us -> 124 us (1.033)
  Pallas kernels: 27.4 us -> 31.1 us
    pallas_call x17, Pallas kernels: 27.4 us -> 31.1 us  [call(): pl.pallas_call(body, out_shape=[jax.ShapeDtypeStruct((rows, CZ), F32) for...]
where the time goes in v8:
time: 124 us
  starting transfers between devices  37 us (30%)
  blocking collectives  32 us (26%)
  Pallas kernels  31.1 us (25%)
  waiting for transfers between devices  22.2 us (18%)
    pallas_call x17, Pallas kernels, call(): pl.pallas_call(body, out_shape=[jax.ShapeDtypeStruct((rows, CZ), F32) for...  31.1 us
    all_to_all x1, blocking collectives, on_device(): sums = lax.all_to_all(sums, last, 0, 0, tiled=True)  18.7 us
    ppermute x4, waiting for transfers between devices, exchange(): return (lax.ppermute(up, axis, forward), lax.ppermute(down, axis, backward))  16.2 us
    ppermute x4, starting transfers between devices, exchange(): return (lax.ppermute(up, axis, forward), lax.ppermute(down, axis, backward))  14.7 us
    all_to_all x1, blocking collectives, on_device(): sums = lax.all_to_all(sums, first, 0, 0, tiled=True)  13.4 us
    ppermute x2, starting transfers between devices, exchange_x(): lax.ppermute(first, gx, pairs[0])  8.17 us
    ppermute x2, waiting for transfers between devices, swap(): return lax.ppermute(value, 'gz', [(0, 1), (1, 0)])  4.9 us
    ppermute x1, starting transfers between devices, on_device(): far_low = lax.ppermute(across_up, ('gy', 'gz'), pairs)  4.61 us
  transfers between devices with their start and end apart: 12, of which 6 were waited for; matrix products, arithmetic and copies ran while one was open for 0% of the time, Pallas kernels for 9%

profile of v8, /device:TPU:1, one launch (start us, length us, event | category | flops | bytes accessed | tf_op | source)
XLA Modules:
  0.0 123.5 jit_solution(17559469348380346128)
XLA Ops:
  0.7 7.2 %strips.1 = (f32[440,128]{1,0:T(8,128)}, f32[440,128]{1,0:T(8,128)}) custom-call(f32[40,40,128]{2,1,0:T(8,128)} %v_in.1, f32[40,40,128]{2,1,0:T(8,128)} %h_in.1, f32[40,40,128]{2,1,0:T(8,128)} %b_in.1), custom_call_target="tpu_custom_call" | custom-call | flops 2000000000 | bytes 4000000 | tf_op jit(solution)/shard_map/strips/pallas_call | solution.py:110
  7.9 6.6 %collective-permute-start = (f32[440,128]{1,0:T(8,128)}, f32[440,128]{1,0:T(8,128)S(1)}, u32[]{:S(2)}, u32[]{:S(2)}) collective-permute-start(f32[440,128]{1,0:T(8,128)} %get-tuple-element.42.up), channel_id=1, source_target_pairs={{0,2},{2,4},{4,6},{1,3},{3,5},{5,7},{8,10},{10,12},{12,14},{9,11},... | collective-permute-start | bytes 675848 | tf_op jit(solution)/shard_map/ppermute | solution.py:766
  14.6 1.3 %collective-permute-start.1 = (f32[440,128]{1,0:T(8,128)}, f32[440,128]{1,0:T(8,128)S(1)}, u32[]{:S(2)}, u32[]{:S(2)}) collective-permute-start(f32[440,128]{1,0:T(8,128)} %get-tuple-element.43.down), channel_id=1, source_target_pairs={{2,0},{4,2},{6,4},{3,1},{5,3},{7,5},{10,8},{12,10},{14,12},{11,9},... | collective-permute-start | bytes 675848 | tf_op jit(solution)/shard_map/ppermute | solution.py:766
  16.0 1.8 %residual.1 = (f32[1600,128]{1,0:T(8,128)S(1)}, f32[160,128]{1,0:T(8,128)S(1)}) custom-call(f32[1600,128]{1,0:T(8,128)S(1)} %bitcast.27, f32[1600,128]{1,0:T(8,128)S(1)} %bitcast.23, f32[1600,128]{1,0:T(8,128)S(1)} %bitcast.22), custom_call_target="tpu_custom_call" | custom-call | flops 2000000000 | bytes 4000000 | tf_op jit(solution)/shard_map/residual/pallas_call | solution.py:110
  17.9 1.9 %prepare.1 = (f32[1600,128]{1,0:T(8,128)S(1)}, f32[3136,128]{1,0:T(8,128)S(1)}, f32[3136,128]{1,0:T(8,128)S(1)}) custom-call(f32[56]{0:T(128)S(1)} %copy-done.9, f32[1600,128]{1,0:T(8,128)S(1)} %bitcast.28, f32[1600,128]{1,0:T(8,128)S(1)} %bitcast.24, f32[56,256]{1,0:T(8,128)S(1)} %copy-done.7), custom_call_target="tpu_custom_call" | custom-call | flops 2000000000 | bytes 4000000 | tf_op jit(solution)/shard_map/prepare/pallas_call | solution.py:110
  20.1 11.5 %collective-permute-done.1.high = f32[440,128]{1,0:T(8,128)S(1)} collective-permute-done((f32[440,128]{1,0:T(8,128)}, f32[440,128]{1,0:T(8,128)S(1)}, u32[]{:S(2)}, u32[]{:S(2)}) %collective-permute-start.1) | collective-permute-done | bytes 225312 | tf_op jit(solution)/shard_map/ppermute | solution.py:766
  31.7 0.9 extend_y.1
  32.5 4.5 %collective-permute-start.2 = (f32[616,128]{1,0:T(8,128)S(1)}, f32[616,128]{1,0:T(8,128)S(1)}, u32[]{:S(2)}, u32[]{:S(2)}) collective-permute-start(f32[616,128]{1,0:T(8,128)S(1)} %get-tuple-element.48), channel_id=1, source_target_pairs={{8,16},{16,8},{24,32},{32,24},{40,48},{48,40},{56,64},{64,56},{72,... | collective-permute-start | bytes 946184 | tf_op jit(solution)/shard_map/ppermute | solution.py:770
  37.1 1.9 %collective-permute-start.3 = (f32[616,128]{1,0:T(8,128)S(1)}, f32[616,128]{1,0:T(8,128)S(1)}, u32[]{:S(2)}, u32[]{:S(2)}) collective-permute-start(f32[616,128]{1,0:T(8,128)S(1)} %get-tuple-element.49), channel_id=1, source_target_pairs={{0,8},{8,0},{16,24},{24,16},{32,40},{40,32},{48,56},{56,48},{64,72... | collective-permute-start | bytes 946184 | tf_op jit(solution)/shard_map/ppermute | solution.py:770
  39.0 1.1 inner.1
  40.7 1.0 collective-permute-done.2.first.one
  41.7 0.7 extend_x.1
  42.4 1.9 %collective-permute-start.4 = (f32[280,128]{1,0:T(8,128)S(1)}, f32[280,128]{1,0:T(8,128)S(1)}, u32[]{:S(2)}, u32[]{:S(2)}) collective-permute-start(f32[280,128]{1,0:T(8,128)S(1)} %get-tuple-element.51.own_z), channel_id=1, source_target_pairs={{0,1},{1,0},{2,3},{3,2},{4,5},{5,4},{6,7},{7,6},{8,9},{9,8},{10,11... | collective-permute-start | bytes 430088 | tf_op jit(solution)/shard_map/ppermute | solution.py:773
  44.4 1.7 %forward.2.main = f32[3136,128]{1,0:T(8,128)S(1)} custom-call(f32[5]{0:T(128)S(1)} %convert_element_type.3.flags, bf16[56,192]{1,0:T(8,128)(2,1)S(1)} %copy-done.8, f32[2240,128]{1,0:T(8,128)S(1)} %get-tuple-element.44.part, f32[2128,128]{1,0:T(8,128)S(1)} %get-tuple-element.50.inner, f32[112,128]{1,0:T(8,128)S(1)} %get-tuple-element.52.fluxes, ...), custom_call_target="tpu_custom_call" | custom-call | flops 2000000000 | bytes 4000000 | tf_op jit(solution)/shard_map/forward/pallas_call | solution.py:110
  46.0 4.0 %collective-permute-done.4.far_z = f32[280,128]{1,0:T(8,128)S(1)} collective-permute-done((f32[280,128]{1,0:T(8,128)S(1)}, f32[280,128]{1,0:T(8,128)S(1)}, u32[]{:S(2)}, u32[]{:S(2)}) %collective-permute-start.4) | collective-permute-done | bytes 143392 | tf_op jit(solution)/shard_map/ppermute | solution.py:773
  50.1 6.2 %solve.1 = (f32[3136,128]{1,0:T(8,128)S(1)}, f32[3136,128]{1,0:T(8,128)S(1)}, f32[1008,128]{1,0:T(8,128)S(1)}, f32[1008,128]{1,0:T(8,128)S(1)}, f32[544,128]{1,0:T(8,128)S(1)}, /*index=5*/f32[544,128]{1,0:T(8,128)S(1)}) custom-call(f32[5]{0:T(128)S(1)} %convert_element_type.3.flags, f32[280,128]{1,0:T(8,128)S(1)} %get-tuple-element.51.own_z, ...), custom_call_target="tpu_custom_call" | custom-call | flops 6000000000 | bytes 12000000 | tf_op jit(solution)/shard_map/solve/pallas_call | solution.py:110
  56.3 3.7 %collective-permute-start.5 = (f32[544,128]{1,0:T(8,128)S(1)}, f32[544,128]{1,0:T(8,128)S(1)}, u32[]{:S(2)}, u32[]{:S(2)}) collective-permute-start(f32[544,128]{1,0:T(8,128)S(1)} %get-tuple-element.61), channel_id=1, source_target_pairs={{8,16},{16,8},{24,32},{32,24},{40,48},{48,40},{56,64},{64,56},{72,... | collective-permute-start | bytes 835592 | tf_op jit(solution)/shard_map/ppermute | solution.py:770
  60.0 1.9 %collective-permute-start.6 = (f32[544,128]{1,0:T(8,128)S(1)}, f32[544,128]{1,0:T(8,128)S(1)}, u32[]{:S(2)}, u32[]{:S(2)}) collective-permute-start(f32[544,128]{1,0:T(8,128)S(1)} %get-tuple-element.62), channel_id=1, source_target_pairs={{0,8},{8,0},{16,24},{24,16},{32,40},{40,32},{48,56},{56,48},{64,72... | collective-permute-start | bytes 835592 | tf_op jit(solution)/shard_map/ppermute | solution.py:770
  61.9 1.8 %rest.1 = (f32[2352,128]{1,0:T(8,128)S(1)}, f32[2352,128]{1,0:T(8,128)S(1)}) custom-call(bf16[56,192]{1,0:T(8,128)(2,1)S(1)} %copy-done.8, bf16[2,768,256]{2,1,0:T(8,128)(2,1)S(1)} %copy-done.5, f32[3136,128]{1,0:T(8,128)S(1)} %get-tuple-element.55.second_a, f32[3136,128]{1,0:T(8,128)S(1)} %get-tuple-element.56.second_b, ...), custom_call_target="tpu_custom_call" | custom-call | flops 2000000000 | bytes 4000000 | tf_op jit(solution)/shard_map/rest/pallas_call | solution.py:110
  63.7 1.4 %own.1 = (f32[1600,128]{1,0:T(8,128)S(1)}, f32[1640,128]{1,0:T(8,128)S(1)}, f32[1600,128]{1,0:T(8,128)S(1)}, f32[1600,128]{1,0:T(8,128)S(1)}, f32[1600,128]{1,0:T(8,128)S(1)}, /*index=5*/f32[1600,128]{1,0:T(8,128)S(1)}) custom-call(f32[5]{0:T(128)S(1)} %convert_element_type.3.flags, f32[1600,128]{1,0:T(8,128)S(1)} %bitcast.25, ...), custom_call_target="tpu_custom_call" | custom-call | flops 2000000000 | bytes 4000000 | tf_op jit(solution)/shard_map/own/pallas_call | solution.py:110
  65.1 1.2 %fold_x.1 = (f32[2352,128]{1,0:T(8,128)S(1)}, f32[416,128]{1,0:T(8,128)S(1)}, f32[416,128]{1,0:T(8,128)S(1)}, f32[128,128]{1,0:T(8,128)S(1)}, f32[32,128]{1,0:T(8,128)S(1)}, /*index=5*/f32[32,128]{1,0:T(8,128)S(1)}) custom-call(f32[5]{0:T(128)S(1)} %convert_element_type.3.flags, f32[2352,128]{1,0:T(8,128)S(1)} %get-tuple-element.59.sol, ...), custom_call_target="tpu_custom_call" | custom-call | flops 1000000000 | bytes 2000000 | tf_op jit(solution)/shard_map/fold_x/pallas_call | solution.py:110
  66.4 5.5 %collective-permute-start.7 = (f32[416,128]{1,0:T(8,128)S(1)}, f32[416,128]{1,0:T(8,128)S(1)}, u32[]{:S(2)}, u32[]{:S(2)}) collective-permute-start(f32[416,128]{1,0:T(8,128)S(1)} %get-tuple-element.65), channel_id=1, source_target_pairs={{0,2},{2,4},{4,6},{1,3},{3,5},{5,7},{8,10},{10,12},{12,14},{9,11},... | collective-permute-start | bytes 638984 | tf_op jit(solution)/shard_map/ppermute | solution.py:766
  71.9 1.3 %collective-permute-start.8 = (f32[416,128]{1,0:T(8,128)S(1)}, f32[416,128]{1,0:T(8,128)S(1)}, u32[]{:S(2)}, u32[]{:S(2)}) collective-permute-start(f32[416,128]{1,0:T(8,128)S(1)} %get-tuple-element.66), channel_id=1, source_target_pairs={{2,0},{4,2},{6,4},{3,1},{5,3},{7,5},{10,8},{12,10},{14,12},{11,9},... | collective-permute-start | bytes 638984 | tf_op jit(solution)/shard_map/ppermute | solution.py:766
  73.2 4.6 %collective-permute-start.10 = (f32[32,128]{1,0:T(8,128)S(1)}, f32[32,128]{1,0:T(8,128)S(1)}, u32[]{:S(2)}, u32[]{:S(2)}) collective-permute-start(f32[32,128]{1,0:T(8,128)S(1)} %get-tuple-element.68), channel_id=1, source_target_pairs={{0,3},{1,2},{2,5},{3,4},{4,7},{5,6},{8,11},{9,10},{10,13},{11,12},... | collective-permute-start | bytes 49160 | tf_op jit(solution)/shard_map/ppermute | solution.py:837
  77.8 1.3 %collective-permute-start.11 = (f32[32,128]{1,0:T(8,128)S(1)}, f32[32,128]{1,0:T(8,128)S(1)}, u32[]{:S(2)}, u32[]{:S(2)}) collective-permute-start(f32[32,128]{1,0:T(8,128)S(1)} %get-tuple-element.69), channel_id=1, source_target_pairs={{3,0},{2,1},{5,2},{4,3},{7,4},{6,5},{11,8},{10,9},{13,10},{12,11},... | collective-permute-start | bytes 49160 | tf_op jit(solution)/shard_map/ppermute | solution.py:838
  79.1 2.5 %collective-permute-start.9 = (f32[128,128]{1,0:T(8,128)S(1)}, f32[128,128]{1,0:T(8,128)S(1)}, u32[]{:S(2)}, u32[]{:S(2)}) collective-permute-start(f32[128,128]{1,0:T(8,128)S(1)} %get-tuple-element.67.own_z), channel_id=1, source_target_pairs={{0,1},{1,0},{2,3},{3,2},{4,5},{5,4},{6,7},{7,6},{8,9},{9,8},{10,11... | collective-permute-start | bytes 196616 | tf_op jit(solution)/shard_map/ppermute | solution.py:773
  81.6 4.7 %collective-permute-done.8.high = f32[416,128]{1,0:T(8,128)S(1)} collective-permute-done((f32[416,128]{1,0:T(8,128)S(1)}, f32[416,128]{1,0:T(8,128)S(1)}, u32[]{:S(2)}, u32[]{:S(2)}) %collective-permute-start.8) | collective-permute-done | bytes 213024 | tf_op jit(solution)/shard_map/ppermute | solution.py:766
  87.0 0.9 collective-permute-done.9.far_z
  87.9 2.2 %apply.1 = (f32[1600,128]{1,0:T(8,128)S(1)}, f32[1600,128]{1,0:T(8,128)S(1)}, f32[16,128]{1,0:T(8,128)S(1)}) custom-call(f32[2352,128]{1,0:T(8,128)S(1)} %fold_y.1.sol, f32[416,128]{1,0:T(8,128)S(1)} %collective-permute-done.7.low, f32[416,128]{1,0:T(8,128)S(1)} %collective-permute-done.8.high, f32[128,128]{1,0:T(8,128)S(1)} %get-tuple-element.67.own_z, ...), custom_call_target="tpu_custom_call" | custom-call | flops 3000000000 | bytes 6000000 | tf_op jit(solution)/shard_map/apply/pallas_call | solution.py:110
  90.1 13.4 %all_to_all.22 = f32[16,1,128]{2,1,0:T(1,128)S(1)} all-to-all(f32[16,1,128]{2,1,0:T(1,128)S(1)} %bitcast.21), channel_id=1, replica_groups=mesh['gx_x'=4,'gx_y'=8,'gx_c'=2,'gy'=4,'gz'=2] {'gx_c','gy','gz'}, dimensions={0} | all-to-all | bytes 16384 | tf_op jit(solution)/shard_map/all_to_all | solution.py:848
  103.4 18.7 %all_to_all.23 = f32[32,1,128]{2,1,0:T(1,128)S(1)} all-to-all(f32[32,1,128]{2,1,0:T(1,128)S(1)} %bitcast.18), channel_id=1, replica_groups=mesh['gx_x'=4,'gx_y'=8,'gx_c'=2,'gy'=4,'gz'=2] {'gx_x','gx_y'}, dimensions={0} | all-to-all | bytes 32768 | tf_op jit(solution)/shard_map/all_to_all | solution.py:850
  122.1 1.4 %update.1 = (f32[1600,128]{1,0:T(8,128)}, f32[1600,128]{1,0:T(8,128)}) custom-call(f32[32,128]{1,0:T(8,128)S(1)} %bitcast.20, f32[1600,128]{1,0:T(8,128)S(1)} %bitcast.29, f32[1600,128]{1,0:T(8,128)S(1)} %get-tuple-element.63._.resid, f32[1600,128]{1,0:T(8,128)S(1)} %get-tuple-element.76.field, f32[1600,128]{1,0:T(8,128)S(1)} %get-tuple-element.77.applied), custom_call_target="tpu_custom_call" | custom-call | flops 2000000000 | bytes 4000000 | tf_op jit(solution)/shard_map/update/pallas_call | solution.py:110
  (33 shorter events, 1.8 us)
Async XLA Ops:
  0.6 15.4 %copy-start.1 = (f32[40,40,128]{2,1,0:T(8,128)S(1)}, f32[40,40,128]{2,1,0:T(8,128)}, u32[]{:S(2)}) copy-start(f32[40,40,128]{2,1,0:T(8,128)} %h_in.1) | copy-start | bytes 2457604
  0.6 15.4 %copy-start.2 = (f32[40,40,128]{2,1,0:T(8,128)S(1)}, f32[40,40,128]{2,1,0:T(8,128)}, u32[]{:S(2)}) copy-start(f32[40,40,128]{2,1,0:T(8,128)} %v_in.1) | copy-start | bytes 2457604
  0.6 15.4 %copy-start = (f32[40,40,128]{2,1,0:T(8,128)S(1)}, f32[40,40,128]{2,1,0:T(8,128)}, u32[]{:S(2)}) copy-start(f32[40,40,128]{2,1,0:T(8,128)} %b_in.1) | copy-start | bytes 2457604
  7.9 12.2 %collective-permute-start = (f32[440,128]{1,0:T(8,128)}, f32[440,128]{1,0:T(8,128)S(1)}, u32[]{:S(2)}, u32[]{:S(2)}) collective-permute-start(f32[440,128]{1,0:T(8,128)} %get-tuple-element.42.up), channel_id=1, source_target_pairs={{0,2},{2,4},{4,6},{1,3},{3,5},{5,7},{8,10},{10,12},{12,14},{9,11},... | collective-permute-start | bytes 675848 | tf_op jit(solution)/shard_map/ppermute | solution.py:766
  14.6 17.1 %collective-permute-start.1 = (f32[440,128]{1,0:T(8,128)}, f32[440,128]{1,0:T(8,128)S(1)}, u32[]{:S(2)}, u32[]{:S(2)}) collective-permute-start(f32[440,128]{1,0:T(8,128)} %get-tuple-element.43.down), channel_id=1, source_target_pairs={{2,0},{4,2},{6,4},{3,1},{5,3},{7,5},{10,8},{12,10},{14,12},{11,9},... | collective-permute-start | bytes 675848 | tf_op jit(solution)/shard_map/ppermute | solution.py:766
  16.0 1.9 %copy-start.7 = (f32[56,256]{1,0:T(8,128)S(1)}, f32[56,256]{1,0:T(8,128)}, u32[]{:S(2)}) copy-start(f32[56,256]{1,0:T(8,128)} %constant.49.clone.denom) | copy-start | bytes 172036
  16.0 1.9 %copy-start.9 = (f32[56]{0:T(128)S(1)}, f32[56]{0:T(128)}, u32[]{:S(2)}) copy-start(f32[56]{0:T(128)} %constant.48.clone.eigen) | copy-start | bytes 676
  19.8 11.9 %copy-start.3 = (f32[440,128]{1,0:T(8,128)S(1)}, f32[440,128]{1,0:T(8,128)}, u32[]{:S(2)}) copy-start(f32[440,128]{1,0:T(8,128)} %get-tuple-element.42.up) | copy-start | bytes 675844
  19.8 11.8 %copy-start.4 = (f32[440,128]{1,0:T(8,128)S(1)}, f32[440,128]{1,0:T(8,128)}, u32[]{:S(2)}) copy-start(f32[440,128]{1,0:T(8,128)} %get-tuple-element.43.down) | copy-start | bytes 675844
  31.7 7.3 %copy-start.8 = (bf16[56,192]{1,0:T(8,128)(2,1)S(1)}, bf16[56,192]{1,0:T(8,128)(2,1)}, u32[]{:S(2)}) copy-start(bf16[56,192]{1,0:T(8,128)(2,1)} %constant.50.clone.plane) | copy-start | bytes 64516
  32.5 9.1 %collective-permute-start.2 = (f32[616,128]{1,0:T(8,128)S(1)}, f32[616,128]{1,0:T(8,128)S(1)}, u32[]{:S(2)}, u32[]{:S(2)}) collective-permute-start(f32[616,128]{1,0:T(8,128)S(1)} %get-tuple-element.48), channel_id=1, source_target_pairs={{8,16},{16,8},{24,32},{32,24},{40,48},{48,40},{56,64},{64,56},{72,... | collective-permute-start | bytes 946184 | tf_op jit(solution)/shard_map/ppermute | solution.py:770
  37.1 4.6 %collective-permute-start.3 = (f32[616,128]{1,0:T(8,128)S(1)}, f32[616,128]{1,0:T(8,128)S(1)}, u32[]{:S(2)}, u32[]{:S(2)}) collective-permute-start(f32[616,128]{1,0:T(8,128)S(1)} %get-tuple-element.49), channel_id=1, source_target_pairs={{0,8},{8,0},{16,24},{24,16},{32,40},{40,32},{48,56},{56,48},{64,72... | collective-permute-start | bytes 946184 | tf_op jit(solution)/shard_map/ppermute | solution.py:770
  42.4 7.7 %collective-permute-start.4 = (f32[280,128]{1,0:T(8,128)S(1)}, f32[280,128]{1,0:T(8,128)S(1)}, u32[]{:S(2)}, u32[]{:S(2)}) collective-permute-start(f32[280,128]{1,0:T(8,128)S(1)} %get-tuple-element.51.own_z), channel_id=1, source_target_pairs={{0,1},{1,0},{2,3},{3,2},{4,5},{5,4},{6,7},{7,6},{8,9},{9,8},{10,11... | collective-permute-start | bytes 430088 | tf_op jit(solution)/shard_map/ppermute | solution.py:773
  44.3 5.7 %copy-start.5 = (bf16[2,768,256]{2,1,0:T(8,128)(2,1)S(1)}, bf16[2,768,256]{2,1,0:T(8,128)(2,1)}, u32[]{:S(2)}) copy-start(bf16[2,768,256]{2,1,0:T(8,128)(2,1)} %constant.52.clone.inverse) | copy-start | bytes 2359300
  44.3 5.7 %copy-start.6 = (bf16[2,768,256]{2,1,0:T(8,128)(2,1)S(1)}, bf16[2,768,256]{2,1,0:T(8,128)(2,1)}, u32[]{:S(2)}) copy-start(bf16[2,768,256]{2,1,0:T(8,128)(2,1)} %constant.51.clone.forward) | copy-start | bytes 2359300
  56.3 8.8 %collective-permute-start.5 = (f32[544,128]{1,0:T(8,128)S(1)}, f32[544,128]{1,0:T(8,128)S(1)}, u32[]{:S(2)}, u32[]{:S(2)}) collective-permute-start(f32[544,128]{1,0:T(8,128)S(1)} %get-tuple-element.61), channel_id=1, source_target_pairs={{8,16},{16,8},{24,32},{32,24},{40,48},{48,40},{56,64},{64,56},{72,... | collective-permute-start | bytes 835592 | tf_op jit(solution)/shard_map/ppermute | solution.py:770
  60.0 5.1 %collective-permute-start.6 = (f32[544,128]{1,0:T(8,128)S(1)}, f32[544,128]{1,0:T(8,128)S(1)}, u32[]{:S(2)}, u32[]{:S(2)}) collective-permute-start(f32[544,128]{1,0:T(8,128)S(1)} %get-tuple-element.62), channel_id=1, source_target_pairs={{0,8},{8,0},{16,24},{24,16},{32,40},{40,32},{48,56},{56,48},{64,72... | collective-permute-start | bytes 835592 | tf_op jit(solution)/shard_map/ppermute | solution.py:770
  66.4 15.2 %collective-permute-start.7 = (f32[416,128]{1,0:T(8,128)S(1)}, f32[416,128]{1,0:T(8,128)S(1)}, u32[]{:S(2)}, u32[]{:S(2)}) collective-permute-start(f32[416,128]{1,0:T(8,128)S(1)} %get-tuple-element.65), channel_id=1, source_target_pairs={{0,2},{2,4},{4,6},{1,3},{3,5},{5,7},{8,10},{10,12},{12,14},{9,11},... | collective-permute-start | bytes 638984 | tf_op jit(solution)/shard_map/ppermute | solution.py:766
  71.9 14.4 %collective-permute-start.8 = (f32[416,128]{1,0:T(8,128)S(1)}, f32[416,128]{1,0:T(8,128)S(1)}, u32[]{:S(2)}, u32[]{:S(2)}) collective-permute-start(f32[416,128]{1,0:T(8,128)S(1)} %get-tuple-element.66), channel_id=1, source_target_pairs={{2,0},{4,2},{6,4},{3,1},{5,3},{7,5},{10,8},{12,10},{14,12},{11,9},... | collective-permute-start | bytes 638984 | tf_op jit(solution)/shard_map/ppermute | solution.py:766
  73.2 13.8 %collective-permute-start.10 = (f32[32,128]{1,0:T(8,128)S(1)}, f32[32,128]{1,0:T(8,128)S(1)}, u32[]{:S(2)}, u32[]{:S(2)}) collective-permute-start(f32[32,128]{1,0:T(8,128)S(1)} %get-tuple-element.68), channel_id=1, source_target_pairs={{0,3},{1,2},{2,5},{3,4},{4,7},{5,6},{8,11},{9,10},{10,13},{11,12},... | collective-permute-start | bytes 49160 | tf_op jit(solution)/shard_map/ppermute | solution.py:837
  77.8 9.2 %collective-permute-start.11 = (f32[32,128]{1,0:T(8,128)S(1)}, f32[32,128]{1,0:T(8,128)S(1)}, u32[]{:S(2)}, u32[]{:S(2)}) collective-permute-start(f32[32,128]{1,0:T(8,128)S(1)} %get-tuple-element.69), channel_id=1, source_target_pairs={{3,0},{2,1},{5,2},{4,3},{7,4},{6,5},{11,8},{10,9},{13,10},{12,11},... | collective-permute-start | bytes 49160 | tf_op jit(solution)/shard_map/ppermute | solution.py:838
  79.1 8.8 %collective-permute-start.9 = (f32[128,128]{1,0:T(8,128)S(1)}, f32[128,128]{1,0:T(8,128)S(1)}, u32[]{:S(2)}, u32[]{:S(2)}) collective-permute-start(f32[128,128]{1,0:T(8,128)S(1)} %get-tuple-element.67.own_z), channel_id=1, source_target_pairs={{0,1},{1,0},{2,3},{3,2},{4,5},{5,4},{6,7},{7,6},{8,9},{9,8},{10,11... | collective-permute-start | bytes 196616 | tf_op jit(solution)/shard_map/ppermute | solution.py:773
